TPU v7x, 512 devices: a whole 4x8x8 slice. The times are simulated.
512 devices in a mesh: dp: 32 (over z_hi, x, core), tensor: 16 (over y, z_lo).
Axes of the slice: x: 4, y: 8, z: 8 (z_hi: 4, z_lo: 2; z = z_hi * 2 + z_lo), core: 2. Of those that a mesh axis runs over, the one named last changes fastest.
Arguments:
- tokens: bfloat16 [512, 8192], P('tensor', 'dp'), may hold values from -6 to 6
- weight_in: bfloat16 [8192, 16384], P('dp', 'tensor'), may hold values from -0.0625 to 0.0625
- tangent_in: bfloat16 [8192, 16384], P('dp', 'tensor'), may hold values from -0.0625 to 0.0625
- weight_out: bfloat16 [16384, 8192], P('tensor', 'dp'), may hold values from -0.046875 to 0.046875
- tangent_out: bfloat16 [16384, 8192], P('tensor', 'dp'), may hold values from -0.046875 to 0.046875
- curvature: float32 [512, 8192], P('tensor', 'dp'), may hold values from 0.02 to 0.2
Outputs:
- product_in: bfloat16 [8192, 16384], P('dp', 'tensor')
- product_out: bfloat16 [16384, 8192], P('tensor', 'dp')
All inputs are finite; a program needn't handle non-finite values.
Results may differ from a plain program's by a relative error of at most 0.035.
Values may be sent and summed in bfloat16 or wider, within the bound.
No kernel may reach another device: no remote copies, remote signals or barrier semaphores. Data moves between devices by JAX's collectives and lax.ppermute only.
A program may use at most 64 MiB of HBM per device.

v0:
```python
import math

import jax
import jax.numpy as jnp
from jax import lax
from jax.sharding import PartitionSpec as P

gelu_scale = math.sqrt(2.0 / math.pi)


def gelu_pair(hidden):
    argument = gelu_scale * (hidden + 0.044715 * hidden * hidden * hidden)
    hyper = jnp.tanh(argument)
    values = 0.5 * hidden * (1.0 + hyper)
    derivative = 0.5 * (1.0 + hyper) + 0.5 * hidden * (1.0 - hyper * hyper) * gelu_scale * (
        1.0 + 3.0 * 0.044715 * hidden * hidden
    )
    return (values, derivative)


def contract_rows(left_side, right_side):
    return lax.dot_general(
        left_side, right_side, (((0,), (0,)), ((), ())), preferred_element_type=jnp.float32
    )


def times_transposed(left_side, right_side):
    return lax.dot_general(
        left_side, right_side, (((1,), (1,)), ((), ())), preferred_element_type=jnp.float32
    )


def on_device(tokens, weight_in, tangent_in, weight_out, tangent_out, curvature):
    gathered = lax.all_gather(tokens, "tensor", axis=0, tiled=True)
    columns = weight_in.shape[1]
    picked = gathered
    joined = lax.psum_scatter(
        jnp.concatenate(
            [
                jnp.dot(picked, weight_in, preferred_element_type=jnp.float32),
                jnp.dot(picked, tangent_in, preferred_element_type=jnp.float32),
            ],
            axis=1,
        ).astype(jnp.bfloat16),
        "dp",
        scatter_dimension=0,
        tiled=True,
    ).astype(jnp.float32)
    values, derivative = gelu_pair(joined[:, :columns])
    active = values.astype(jnp.bfloat16)
    moved = (derivative * joined[:, columns:]).astype(jnp.bfloat16)
    active_all, moved_all = (
        lax.all_gather(active, "dp", axis=0, tiled=True),
        lax.all_gather(moved, "dp", axis=0, tiled=True),
    )
    output_tangent = lax.psum_scatter(
        (
            jnp.dot(moved_all, weight_out, preferred_element_type=jnp.float32)
            + jnp.dot(active_all, tangent_out, preferred_element_type=jnp.float32)
        ).astype(jnp.bfloat16),
        "tensor",
        scatter_dimension=0,
        tiled=True,
    ).astype(jnp.float32)
    cotangent = (curvature * output_tangent).astype(jnp.bfloat16)
    cotangent_all = lax.all_gather(cotangent, "tensor", axis=0, tiled=True)
    product_out = contract_rows(active_all, cotangent_all).astype(jnp.bfloat16)
    picked = cotangent_all
    backward = lax.psum_scatter(
        times_transposed(picked, weight_out).astype(jnp.bfloat16),
        "dp",
        scatter_dimension=0,
        tiled=True,
    ).astype(jnp.float32)
    hidden_grad = (backward * derivative).astype(jnp.bfloat16)
    picked = gathered
    product_in = contract_rows(
        picked, lax.all_gather(hidden_grad, "dp", axis=0, tiled=True)
    ).astype(jnp.bfloat16)
    return (product_in, product_out)


def solution(mesh):
    return jax.shard_map(
        on_device,
        mesh=mesh,
        in_specs=(
            P("tensor", "dp"),
            P("dp", "tensor"),
            P("dp", "tensor"),
            P("tensor", "dp"),
            P("tensor", "dp"),
            P("tensor", "dp"),
        ),
        out_specs=(P("dp", "tensor"), P("tensor", "dp")),
        check_vma=False,
    )
```

profile of v0, /device:TPU:1, one launch (start us, length us, event | category | flops | bytes accessed | tf_op | source)
XLA Modules:
  0.0 542.5 jit_solution(16510207266633188824)
XLA Ops:
  7.2 0.0 copy-start
  7.2 0.0 copy-start.2
  7.2 0.0 reduce-scatter.4.cloned.1.call-start
  7.2 30.4 %all_gather.15 = bf16[512,256]{1,0:T(8,128)(2,1)S(1)} all-gather(bf16[32,256]{1,0:T(8,128)(2,1)} %param.6), channel_id=1, replica_groups=mesh['dp'=32,'tensor'=16] {'tensor'}, dimensions={0}, use_global_device_ids=true | all-gather | bytes 278528 | tf_op jit(solution)/shard_map/all_gather | solution.py:34
  37.6 1.5 convolution_convert_fusion.1
  39.1 0.0 copy-done.2
  39.1 0.4 convolution_convert_fusion.2
  39.6 1.5 pad_maximum_fusion
  41.1 0.0 copy-start.3
  41.1 0.0 reduce-scatter.4.cloned.1.call-update
  41.1 0.0 all-gather.4.cloned.1.call-start
  41.2 106.8 %reduce-scatter.4.cloned.1.call-done = bf16[16,2048]{1,0:T(8,128)(2,1)} async-done(((bf16[512,2048]{1,0:T(8,128)(2,1)}), bf16[16,2048]{1,0:T(8,128)(2,1)}) %reduce-scatter.4.cloned.1.call-update) | async-done | bytes 65552 | tf_op jit(solution)/shard_map/reduce_scatter | solution.py:37
  148.0 0.8 convert_element_type.37
  148.8 0.7 multiply_convert_fusion.1
  149.5 0.0 all-gather.4.cloned.1.call-update
  149.5 0.0 all-gather.6.cloned.1.call-start
  149.6 0.7 all-gather.6.cloned.1.call-update
  150.3 0.0 copy-start.4
  150.3 0.0 reduce-scatter.6.cloned.1.call-start
  150.3 59.0 %all-gather.4.cloned.1.call-done = bf16[512,1024]{1,0:T(8,128)(2,1)} async-done(((bf16[16,1024]{1,0:T(8,128)(2,1)}), bf16[512,1024]{1,0:T(8,128)(2,1)}) %all-gather.4.cloned.1.call-update) | async-done | bytes 1048592 | tf_op jit(solution)/shard_map/all_gather | solution.py:54
  209.3 0.0 copy-done
  209.3 1.7 fusion.8
  211.0 57.4 %all-gather.6.cloned.1.call-done = bf16[512,1024]{1,0:T(8,128)(2,1)} async-done(((bf16[16,1024]{1,0:T(8,128)(2,1)}), bf16[512,1024]{1,0:T(8,128)(2,1)}) %all-gather.6.cloned.1.call-update) | async-done | bytes 1048592 | tf_op jit(solution)/shard_map/all_gather | solution.py:53
  268.3 0.0 copy-done.3
  268.3 2.4 fusion.1
  270.7 0.0 copy-start.1
  270.7 0.0 reduce-scatter.6.cloned.1.call-update
  270.7 0.0 reduce-scatter.8.cloned.1.call-start
  270.8 58.7 %reduce-scatter.6.cloned.1.call-done = bf16[32,256]{1,0:T(8,128)(2,1)} async-done(((bf16[512,256]{1,0:T(8,128)(2,1)}), bf16[32,256]{1,0:T(8,128)(2,1)}) %reduce-scatter.6.cloned.1.call-update) | async-done | bytes 16400 | tf_op jit(solution)/shard_map/reduce_scatter | solution.py:56
  329.5 0.0 copy-done.4
  329.5 0.7 multiply_convert_fusion.2
  330.2 24.2 %all_gather.18 = bf16[512,256]{1,0:T(8,128)(2,1)S(1)} all-gather(bf16[32,256]{1,0:T(8,128)(2,1)S(1)} %multiply_convert_fusion.2), channel_id=1, replica_groups=mesh['dp'=32,'tensor'=16] {'tensor'}, dimensions={0}, use_global_device_ids=true | all-gather | bytes 278528 | tf_op jit(solution)/shard_map/all_gather | solution.py:66
  354.4 1.5 convolution_convert_fusion
  355.9 0.0 reduce-scatter.8.cloned.1.call-update
  355.9 0.0 all-gather.8.cloned.1.call-start
  356.0 115.7 %reduce-scatter.8.cloned.1.call-done = bf16[16,1024]{1,0:T(8,128)(2,1)} async-done(((bf16[512,1024]{1,0:T(8,128)(2,1)}), bf16[16,1024]{1,0:T(8,128)(2,1)}) %reduce-scatter.8.cloned.1.call-update) | async-done | bytes 32784 | tf_op jit(solution)/shard_map/reduce_scatter | solution.py:69
  471.7 1.4 multiply_convert_fusion
  473.1 0.0 all-gather.8.cloned.1.call-update
  473.1 0.0 copy-done.1
  473.2 1.3 convolution_convert_fusion.3
  474.4 58.5 %all-gather.8.cloned.1.call-done = bf16[512,1024]{1,0:T(8,128)(2,1)} async-done(((bf16[16,1024]{1,0:T(8,128)(2,1)}), bf16[512,1024]{1,0:T(8,128)(2,1)}) %all-gather.8.cloned.1.call-update) | async-done | bytes 1048592 | tf_op jit(solution)/shard_map/all_gather | solution.py:78
  532.9 1.7 fusion
  534.6 1.0 copy.8
Async XLA Ops:
  7.2 202.1 %copy-start = (bf16[1024,256]{1,0:T(8,128)(2,1)S(1)}, bf16[1024,256]{1,0:T(8,128)(2,1)}, u32[]{:S(2)}) copy-start(bf16[1024,256]{1,0:T(8,128)(2,1)} %param.9) | copy-start | bytes 1572868
  7.2 32.0 %copy-start.2 = (bf16[256,1024]{1,0:T(8,128)(2,1)S(1)}, bf16[256,1024]{1,0:T(8,128)(2,1)}, u32[]{:S(2)}) copy-start(bf16[256,1024]{1,0:T(8,128)(2,1)} %param.7) | copy-start | bytes 1572868
  7.2 140.8 %reduce-scatter.4.cloned.1.call-start = ((), (), s32[]{:S(2)}) async-start(), calls=%async_computation.3 | async-start | bytes 2162688 | tf_op jit(solution)/shard_map/reduce_scatter | solution.py:37
  41.1 227.2 %copy-start.3 = (bf16[1024,256]{1,0:T(8,128)(2,1)S(1)}, bf16[1024,256]{1,0:T(8,128)(2,1)}, u32[]{:S(2)}) copy-start(bf16[1024,256]{1,0:T(8,128)(2,1)} %param.10) | copy-start | bytes 1572868
  41.1 168.2 %all-gather.4.cloned.1.call-start = ((), (), s32[]{:S(2)}) async-start(), calls=%async_computation.4 | async-start | bytes 1081344 | tf_op jit(solution)/shard_map/all_gather | solution.py:54
  149.5 118.8 %all-gather.6.cloned.1.call-start = ((), (), s32[]{:S(2)}) async-start(), calls=%async_computation.5 | async-start | bytes 1081344 | tf_op jit(solution)/shard_map/all_gather | solution.py:53
  150.3 179.2 %copy-start.4 = (f32[32,256]{1,0:T(8,128)S(1)}, f32[32,256]{1,0:T(8,128)}, u32[]{:S(2)}) copy-start(f32[32,256]{1,0:T(8,128)} %param.11) | copy-start | bytes 98308
  150.3 179.2 %reduce-scatter.6.cloned.1.call-start = ((), (), s32[]{:S(2)}) async-start(), calls=%async_computation.6 | async-start | bytes 278528 | tf_op jit(solution)/shard_map/reduce_scatter | solution.py:56
  270.7 202.4 %copy-start.1 = (bf16[512,1024]{1,0:T(8,128)(2,1)S(1)}, bf16[512,1024]{1,0:T(8,128)(2,1)}, u32[]{:S(2)}) copy-start(bf16[512,1024]{1,0:T(8,128)(2,1)} %all-gather.6.cloned.1.call-done) | copy-start | bytes 3145732
  270.7 201.0 %reduce-scatter.8.cloned.1.call-start = ((), (), s32[]{:S(2)}) async-start(), calls=%async_computation.7 | async-start | bytes 1081344 | tf_op jit(solution)/shard_map/reduce_scatter | solution.py:69
  355.9 177.0 %all-gather.8.cloned.1.call-start = ((), (), s32[]{:S(2)}) async-start(), calls=%async_computation.8 | async-start | bytes 1081344 | tf_op jit(solution)/shard_map/all_gather | solution.py:78
Sparse Core Ops, SparseCore 0:
  41.3 106.6 reduce-scatter.3
  151.7 57.5 all-gather.3
  213.0 55.2 all-gather.5
  271.5 57.9 reduce-scatter.5
  356.0 115.6 reduce-scatter.7
  475.3 57.6 all-gather.7
where the time goes:
time: 543 us; the launch traced here: 542 us
  waiting for transfers between devices  457 us (84%)
  blocking collectives  54.6 us (10%)
  between operations  14.2 us (3%)
  matrix products  10.4 us (2%)
    reduce_scatter x1, waiting for transfers between devices, on_device(): lax.psum_scatter(times_transposed(picked, weight_out).astype(jnp.bfloat16...  116 us
    reduce_scatter x1, waiting for transfers between devices, on_device(): lax.psum_scatter(jnp.concatenate([jnp.dot(picked, weight_in, preferred_el...  107 us
    all_gather x1, waiting for transfers between devices, on_device(): lax.all_gather(moved, 'dp', axis=0, tiled=True)  59 us
    reduce_scatter x1, waiting for transfers between devices, on_device(): lax.psum_scatter((jnp.dot(moved_all, weight_out, preferred_element_type=j...  58.7 us
    all_gather x1, waiting for transfers between devices, on_device(): lax.all_gather(hidden_grad, 'dp', axis=0, tiled=True)  58.5 us
    all_gather x1, waiting for transfers between devices, on_device(): lax.all_gather(active, 'dp', axis=0, tiled=True)  57.4 us
    all_gather x1, blocking collectives, on_device(): gathered = lax.all_gather(tokens, 'tensor', axis=0, tiled=True)  30.4 us
    all_gather x1, blocking collectives, on_device(): cotangent_all = lax.all_gather(cotangent, 'tensor', axis=0, tiled=True)  24.2 us
  transfers between devices with their start and end apart: 6, of which 6 were waited for; matrix products, arithmetic and copies ran while one was open for 1% of the time, Pallas kernels for 0%

commit v1 on v0

v1 whole, which is shorter than its diff:
```python
import math

import jax
import jax.numpy as jnp
from jax import lax
from jax.sharding import Mesh
from jax.sharding import PartitionSpec as P

gelu_scale = math.sqrt(2.0 / math.pi)
ROWS = ("zh", "x")
TENSOR = ("y", "zl")
SWAP = [(0, 1), (1, 0)]


def gelu_pair(hidden):
    argument = gelu_scale * (hidden + 0.044715 * hidden * hidden * hidden)
    hyper = jnp.tanh(argument)
    values = 0.5 * hidden * (1.0 + hyper)
    derivative = 0.5 * (1.0 + hyper) + 0.5 * hidden * (1.0 - hyper * hyper) * gelu_scale * (
        1.0 + 3.0 * 0.044715 * hidden * hidden
    )
    return (values, derivative)


def dot(left_side, right_side, left_dim=1, right_dim=0):
    return lax.dot_general(
        left_side,
        right_side,
        (((left_dim,), (right_dim,)), ((), ())),
        preferred_element_type=jnp.float32,
    )


def gather_rows(block, axes):
    count = lax.axis_size(axes)
    copies = jnp.broadcast_to(block[None], (count,) + block.shape)
    copies = copies.reshape(count * block.shape[0], block.shape[1])
    return lax.all_to_all(copies, axes, split_axis=0, concat_axis=0, tiled=True)


def sum_rows(partial, axes):
    count = lax.axis_size(axes)
    pieces = lax.all_to_all(partial, axes, split_axis=0, concat_axis=0, tiled=True)
    pieces = pieces.reshape(count, partial.shape[0] // count, partial.shape[1])
    return jnp.sum(pieces.astype(jnp.float32), axis=0)


def swap_cores(block):
    return lax.ppermute(block, "c", SWAP)


def other_core(block, other):
    both = lax.all_gather(block, "c", axis=0, tiled=False)
    return lax.dynamic_index_in_dim(both, other, 0, keepdims=False)


def on_device(tokens, weight_in, tangent_in, weight_out, tangent_out, curvature):
    core = lax.axis_index("c")
    other = 1 - core
    half = weight_in.shape[1] // 2

    def columns(array, which):
        return lax.dynamic_slice_in_dim(array, which * half, half, 1)

    def rows(array, which):
        return lax.dynamic_slice_in_dim(array, which * half, half, 0)

    pair_own = jnp.concatenate([columns(weight_in, core), columns(tangent_in, core)], axis=1)
    pair_far = swap_cores(
        jnp.concatenate([columns(weight_in, other), columns(tangent_in, other)], axis=1)
    )
    out_own = rows(weight_out, core)
    out_far = swap_cores(rows(weight_out, other))

    tokens_own = gather_rows(tokens, TENSOR)
    tokens_far = other_core(tokens_own, other)
    joined = (dot(tokens_own, pair_own) + dot(tokens_far, pair_far)).astype(jnp.bfloat16)
    joined = sum_rows(joined, ROWS)
    values, derivative = gelu_pair(joined[:, :half])
    moved = derivative * joined[:, half:]
    both = jnp.concatenate([values, moved], axis=1).astype(jnp.bfloat16)
    both_own = gather_rows(both, ROWS)
    both_far = swap_cores(both_own)

    output_tangent = (
        dot(both_own[:, half:], out_own)
        + dot(both_own[:, :half], rows(tangent_out, core))
        + dot(both_far[:, half:], rows(weight_out, other))
        + dot(both_far[:, :half], rows(tangent_out, other))
    ).astype(jnp.bfloat16)
    output_tangent = sum_rows(output_tangent, TENSOR)
    cotangent = (curvature * output_tangent).astype(jnp.bfloat16)
    cotangent_own = gather_rows(cotangent, TENSOR)
    cotangent_far = other_core(cotangent_own, other)

    backward = (
        dot(cotangent_own, out_own, 1, 1) + dot(cotangent_far, out_far, 1, 1)
    ).astype(jnp.bfloat16)
    backward = sum_rows(backward, ROWS)
    first = jnp.where(core == 0, both_own[:, :half], both_far[:, :half])
    second = jnp.where(core == 0, both_far[:, :half], both_own[:, :half])
    product_out = jnp.concatenate(
        [dot(first, cotangent_own, 0, 0), dot(second, cotangent_own, 0, 0)], axis=0
    ).astype(jnp.bfloat16)

    hidden_grad = (backward * derivative).astype(jnp.bfloat16)
    grad_own = gather_rows(hidden_grad, ROWS)
    grad_far = swap_cores(grad_own)
    first = jnp.where(core == 0, grad_own, grad_far)
    second = jnp.where(core == 0, grad_far, grad_own)
    product_in = jnp.concatenate(
        [dot(tokens_own, first, 0, 0), dot(tokens_own, second, 0, 0)], axis=1
    ).astype(jnp.bfloat16)
    return (product_in, product_out)


def solution(mesh):
    fine = Mesh(mesh.devices.reshape(4, 4, 2, 8, 2), ("zh", "x", "c", "y", "zl"))
    by_dp = ("zh", "x", "c")
    return jax.shard_map(
        on_device,
        mesh=fine,
        in_specs=(
            P(TENSOR, by_dp),
            P(by_dp, TENSOR),
            P(by_dp, TENSOR),
            P(TENSOR, by_dp),
            P(TENSOR, by_dp),
            P(TENSOR, by_dp),
        ),
        out_specs=(P(by_dp, TENSOR), P(TENSOR, by_dp)),
        check_vma=False,
    )
```

time: 543 us -> 192 us (0.35)
  waiting for transfers between devices: 457 us -> 28.6 us
  blocking collectives: 54.6 us -> 113 us
  starting transfers between devices: 0.24 us -> 34.8 us
  between operations: 14.2 us -> 0.9 us
    reduce_scatter x3 -> x0, waiting for transfers between devices: 281 us -> none  [the longest x1 116 us: on_device(): lax.psum_scatter(times_transposed(picked, weight_out).astype(jnp.bfloat16...]
    all_gather x3 -> x0, waiting for transfers between devices: 175 us -> none  [the longest x1 59 us: on_device(): lax.all_gather(moved, 'dp', axis=0, tiled=True)]
    all_to_all x0 -> x4, blocking collectives: none -> 104 us  [the longest x3 74.7 us: sum_rows(): lax.all_to_all(partial, axes, split_axis=0, concat_axis=0, tiled=True)]
    all_gather x2, blocking collectives: 54.6 us -> 9.5 us  [other_core(): both = lax.all_gather(block, 'c', axis=0, tiled=False)]
    all_to_all x0 -> x3, waiting for transfers between devices: none -> 27 us  [gather_rows(): return lax.all_to_all(copies, axes, split_axis=0, concat_axis=0, tiled=True)]
    all_to_all x0 -> x3, starting transfers between devices: none -> 18.7 us  [gather_rows(): return lax.all_to_all(copies, axes, split_axis=0, concat_axis=0, tiled=True)]
    ppermute x0 -> x4, starting transfers between devices: none -> 16.1 us  [swap_cores(): return lax.ppermute(block, 'c', SWAP)]
  transfers between devices with their start and end apart: 6 -> 7, of which waited for: 6 -> 4; matrix products, arithmetic and copies ran while one was open for 1% -> 2% of each run, Pallas kernels for 0% -> 0%
where the time goes in v1:
time: 192 us; the launch traced here: 191 us
  blocking collectives  113 us (59%)
  starting transfers between devices  34.8 us (18%)
  waiting for transfers between devices  28.6 us (15%)
  matrix products  6.43 us (3%)
  local copies, waits for them, and re-layouts  5.51 us (3%)
    all_to_all x3, blocking collectives, sum_rows(): lax.all_to_all(partial, axes, split_axis=0, concat_axis=0, tiled=True)  74.7 us
    all_to_all x1, blocking collectives, gather_rows(): return lax.all_to_all(copies, axes, split_axis=0, concat_axis=0, tiled=True)  28.9 us
    all_to_all x3, waiting for transfers between devices, gather_rows(): return lax.all_to_all(copies, axes, split_axis=0, concat_axis=0, tiled=True)  27 us
    all_to_all x3, starting transfers between devices, gather_rows(): return lax.all_to_all(copies, axes, split_axis=0, concat_axis=0, tiled=True)  18.7 us
    ppermute x4, starting transfers between devices, swap_cores(): return lax.ppermute(block, 'c', SWAP)  16.1 us
    all_gather x2, blocking collectives, other_core(): both = lax.all_gather(block, 'c', axis=0, tiled=False)  9.5 us
    dot_general x12, matrix products, dot(): lax.dot_general(left_side, right_side, (((left_dim,), (right_dim,)), ((),...  6.43 us
  transfers between devices with their start and end apart: 7, of which 4 were waited for; matrix products, arithmetic and copies ran while one was open for 2% of the time, Pallas kernels for 0%

profile of v1, /device:TPU:1, one launch (start us, length us, event | category | flops | bytes accessed | tf_op | source)
XLA Modules:
  0.0 190.7 jit_solution(12721194326358352649)
XLA Ops:
  0.6 0.0 copy-start
  0.6 1.5 broadcast_in_dim.8
  2.1 9.6 %all-to-all-start = ((bf16[16,32,256]{2,1,0:T(8,128)(2,1)}), bf16[16,32,256]{2,1,0:T(8,128)(2,1)S(1)}, u32[]{:S(2)}, u32[]{:S(2)}) async-start(bf16[16,32,256]{2,1,0:T(8,128)(2,1)} %broadcast_in_dim.8), calls=%async_computation | async-start | bytes 524288 | tf_op jit(solution)/shard_map/all_to_all | solution.py:38
  11.7 1.3 constant_dynamic-slice_fusion.1
  13.0 0.1 pad_maximum_fusion
  13.1 2.9 %collective-permute-start = (bf16[256,1024]{1,0:T(8,128)(2,1)S(1)}, bf16[256,1024]{1,0:T(8,128)(2,1)S(1)}, u32[]{:S(2)}, u32[]{:S(2)}) collective-permute-start(bf16[256,1024]{1,0:T(8,128)(2,1)S(1)} %pad_maximum_fusion), channel_id=1, source_target_pairs={{0,16},{16,0},{1,17},{17,1},{2,18},{18,2},{3,19},{19,3},{4,20},{20... | collective-permute-start | bytes 1572872 | tf_op jit(solution)/shard_map/ppermute | solution.py:49
  15.9 6.3 %all-to-all-done = bf16[16,32,256]{2,1,0:T(8,128)(2,1)S(1)} async-done(((bf16[16,32,256]{2,1,0:T(8,128)(2,1)}), bf16[16,32,256]{2,1,0:T(8,128)(2,1)S(1)}, u32[]{:S(2)}, u32[]{:S(2)}) %all-to-all-start) | async-done | bytes 262176 | tf_op jit(solution)/shard_map/all_to_all | solution.py:38
  22.2 4.3 %all_gather.13 = bf16[2,512,256]{2,1,0:T(8,128)(2,1)S(1)} all-gather(bf16[1,512,256]{2,1,0:T(8,128)(2,1)S(1)} %bitcast.42), channel_id=1, replica_groups=mesh['zh'=4,'x'=4,'c'=2,'y'=8,'zl'=2] {'c'}, dimensions={0}, use_global_device_ids=true | all-gather | bytes 786432 | tf_op jit(solution)/shard_map/all_gather | solution.py:53
  26.5 0.4 fusion.9
  26.9 0.0 collective-permute-done
  27.0 0.5 fusion
  27.4 39.6 %all_to_all.63 = bf16[16,32,1024]{2,1,0:T(8,128)(2,1)S(1)} all-to-all(bf16[16,32,1024]{2,1,0:T(8,128)(2,1)S(1)} %bitcast.37), channel_id=1, replica_groups=mesh['zh'=4,'x'=4,'c'=2,'y'=8,'zl'=2] {'zh','x'}, dimensions={0} | all-to-all | bytes 2097152 | tf_op jit(solution)/shard_map/all_to_all | solution.py:43
  67.0 0.2 convert_reduce_fusion
  67.2 0.1 multiply_convert_fusion.1
  67.3 0.1 broadcast_in_dim.9
  67.4 0.0 copy-start.1
  67.4 28.9 %all_to_all.64 = bf16[16,32,1024]{2,1,0:T(8,128)(2,1)S(1)} all-to-all(bf16[16,32,1024]{2,1,0:T(8,128)(2,1)S(1)} %broadcast_in_dim.9), channel_id=1, replica_groups=mesh['zh'=4,'x'=4,'c'=2,'y'=8,'zl'=2] {'zh','x'}, dimensions={0} | all-to-all | bytes 2097152 | tf_op jit(solution)/shard_map/all_to_all | solution.py:38
  96.3 5.1 %collective-permute-start.1 = (bf16[512,1024]{1,0:T(8,128)(2,1)S(1)}, bf16[512,1024]{1,0:T(8,128)(2,1)S(1)}, u32[]{:S(2)}, u32[]{:S(2)}) collective-permute-start(bf16[512,1024]{1,0:T(8,128)(2,1)S(1)} %bitcast.32), channel_id=1, source_target_pairs={{0,16},{16,0},{1,17},{17,1},{2,18},{18,2},{3,19},{19,3},{4,20},{20... | collective-permute-start | bytes 3145736 | tf_op jit(solution)/shard_map/ppermute | solution.py:49
  101.5 0.3 fusion.7
  101.8 0.0 copy-done.1
  101.8 0.3 convolution_add_fusion.2
  102.1 0.0 copy-start.2
  102.1 1.6 collective-permute-done.1
  103.7 0.3 fusion.23
  104.0 0.3 fusion.3
  104.3 14.6 %all_to_all.65 = bf16[16,32,256]{2,1,0:T(8,128)(2,1)S(1)} all-to-all(bf16[16,32,256]{2,1,0:T(8,128)(2,1)S(1)} %bitcast.47), channel_id=1, replica_groups=mesh['zh'=4,'x'=4,'c'=2,'y'=8,'zl'=2] {'y','zl'}, dimensions={0} | all-to-all | bytes 524288 | tf_op jit(solution)/shard_map/all_to_all | solution.py:43
  119.0 0.7 broadcast_in_dim.10
  119.7 3.5 %all-to-all-start.4 = ((bf16[16,32,256]{2,1,0:T(8,128)(2,1)}), bf16[16,32,256]{2,1,0:T(8,128)(2,1)S(1)}, u32[]{:S(2)}, u32[]{:S(2)}) async-start(bf16[16,32,256]{2,1,0:T(8,128)(2,1)} %broadcast_in_dim.10), calls=%async_computation.4 | async-start | bytes 524288 | tf_op jit(solution)/shard_map/all_to_all | solution.py:38
  123.3 3.9 %collective-permute-start.2 = (bf16[512,256]{1,0:T(8,128)(2,1)S(1)}, bf16[512,256]{1,0:T(8,128)(2,1)}, u32[]{:S(2)}, u32[]{:S(2)}) collective-permute-start(bf16[512,256]{1,0:T(8,128)(2,1)S(1)} %constant_dynamic-slice_fusion), channel_id=1, source_target_pairs={{0,16},{16,0},{1,17},{17,1},{2,18},{18,2},{3,19},{19,3},{4,20},{20... | collective-permute-start | bytes 786440 | tf_op jit(solution)/shard_map/ppermute | solution.py:49
  127.1 5.8 %all-to-all-done.4 = bf16[16,32,256]{2,1,0:T(8,128)(2,1)S(1)} async-done(((bf16[16,32,256]{2,1,0:T(8,128)(2,1)}), bf16[16,32,256]{2,1,0:T(8,128)(2,1)S(1)}, u32[]{:S(2)}, u32[]{:S(2)}) %all-to-all-start.4) | async-done | bytes 262176 | tf_op jit(solution)/shard_map/all_to_all | solution.py:38
  132.9 5.2 %all_gather.15 = bf16[2,512,256]{2,1,0:T(8,128)(2,1)S(1)} all-gather(bf16[1,512,256]{2,1,0:T(8,128)(2,1)S(1)} %bitcast.38), channel_id=1, replica_groups=mesh['zh'=4,'x'=4,'c'=2,'y'=8,'zl'=2] {'c'}, dimensions={0}, use_global_device_ids=true | all-gather | bytes 786432 | tf_op jit(solution)/shard_map/all_gather | solution.py:53
  138.1 0.3 fusion.34
  138.5 0.0 collective-permute-done.2
  138.5 1.3 fusion.1
  139.8 20.5 %all_to_all.66 = bf16[16,32,512]{2,1,0:T(8,128)(2,1)S(1)} all-to-all(bf16[16,32,512]{2,1,0:T(8,128)(2,1)S(1)} %bitcast.46), channel_id=1, replica_groups=mesh['zh'=4,'x'=4,'c'=2,'y'=8,'zl'=2] {'zh','x'}, dimensions={0} | all-to-all | bytes 1048576 | tf_op jit(solution)/shard_map/all_to_all | solution.py:43
  160.3 0.1 convert_reduce_fusion.1
  160.4 0.1 multiply_convert_fusion
  160.4 0.8 broadcast_in_dim.11
  161.3 5.6 %all-to-all-start.6 = ((bf16[16,32,512]{2,1,0:T(8,128)(2,1)}), bf16[16,32,512]{2,1,0:T(8,128)(2,1)}, u32[]{:S(2)}, u32[]{:S(2)}) async-start(bf16[16,32,512]{2,1,0:T(8,128)(2,1)} %broadcast_in_dim.11), calls=%async_computation.6 | async-start | bytes 1048576 | tf_op jit(solution)/shard_map/all_to_all | solution.py:38
  166.9 15.0 %all-to-all-done.6 = bf16[16,32,512]{2,1,0:T(8,128)(2,1)} async-done(((bf16[16,32,512]{2,1,0:T(8,128)(2,1)}), bf16[16,32,512]{2,1,0:T(8,128)(2,1)}, u32[]{:S(2)}, u32[]{:S(2)}) %all-to-all-start.6) | async-done | bytes 524320 | tf_op jit(solution)/shard_map/all_to_all | solution.py:38
  181.9 4.2 %collective-permute-start.3 = (bf16[512,512]{1,0:T(8,128)(2,1)}, bf16[512,512]{1,0:T(8,128)(2,1)S(1)}, u32[]{:S(2)}, u32[]{:S(2)}) collective-permute-start(bf16[512,512]{1,0:T(8,128)(2,1)} %bitcast.11), channel_id=1, source_target_pairs={{0,16},{16,0},{1,17},{17,1},{2,18},{18,2},{3,19},{19,3},{4,20},{20... | collective-permute-start | bytes 1572872 | tf_op jit(solution)/shard_map/ppermute | solution.py:49
  186.1 0.4 convolution_convert_fusion.1
  186.5 0.4 convolution_convert_fusion
  187.0 0.8 pad_maximum_fusion.2
  187.8 0.0 collective-permute-done.3
  187.8 0.4 fusion.4
  188.2 1.5 fusion.5
  189.7 1.0 copy.9
  (7 shorter events, 0.1 us)
Async XLA Ops:
  0.6 100.8 %copy-start = (bf16[1024,256]{1,0:T(8,128)(2,1)S(1)}, bf16[1024,256]{1,0:T(8,128)(2,1)}, u32[]{:S(2)}) copy-start(bf16[1024,256]{1,0:T(8,128)(2,1)} %param.9) | copy-start | bytes 1572868
  2.1 20.1 %all-to-all-start = ((bf16[16,32,256]{2,1,0:T(8,128)(2,1)}), bf16[16,32,256]{2,1,0:T(8,128)(2,1)S(1)}, u32[]{:S(2)}, u32[]{:S(2)}) async-start(bf16[16,32,256]{2,1,0:T(8,128)(2,1)} %broadcast_in_dim.8), calls=%async_computation | async-start | bytes 524288 | tf_op jit(solution)/shard_map/all_to_all | solution.py:38
  13.1 13.9 %collective-permute-start = (bf16[256,1024]{1,0:T(8,128)(2,1)S(1)}, bf16[256,1024]{1,0:T(8,128)(2,1)S(1)}, u32[]{:S(2)}, u32[]{:S(2)}) collective-permute-start(bf16[256,1024]{1,0:T(8,128)(2,1)S(1)} %pad_maximum_fusion), channel_id=1, source_target_pairs={{0,16},{16,0},{1,17},{17,1},{2,18},{18,2},{3,19},{19,3},{4,20},{20... | collective-permute-start | bytes 1572872 | tf_op jit(solution)/shard_map/ppermute | solution.py:49
  67.4 34.4 %copy-start.1 = (bf16[1024,256]{1,0:T(8,128)(2,1)S(1)}, bf16[1024,256]{1,0:T(8,128)(2,1)}, u32[]{:S(2)}) copy-start(bf16[1024,256]{1,0:T(8,128)(2,1)} %param.10) | copy-start | bytes 1572868
  96.3 7.4 %collective-permute-start.1 = (bf16[512,1024]{1,0:T(8,128)(2,1)S(1)}, bf16[512,1024]{1,0:T(8,128)(2,1)S(1)}, u32[]{:S(2)}, u32[]{:S(2)}) collective-permute-start(bf16[512,1024]{1,0:T(8,128)(2,1)S(1)} %bitcast.32), channel_id=1, source_target_pairs={{0,16},{16,0},{1,17},{17,1},{2,18},{18,2},{3,19},{19,3},{4,20},{20... | collective-permute-start | bytes 3145736 | tf_op jit(solution)/shard_map/ppermute | solution.py:49
  102.1 16.9 %copy-start.2 = (f32[32,256]{1,0:T(8,128)S(1)}, f32[32,256]{1,0:T(8,128)}, u32[]{:S(2)}) copy-start(f32[32,256]{1,0:T(8,128)} %param.11) | copy-start | bytes 98308
  119.7 13.2 %all-to-all-start.4 = ((bf16[16,32,256]{2,1,0:T(8,128)(2,1)}), bf16[16,32,256]{2,1,0:T(8,128)(2,1)S(1)}, u32[]{:S(2)}, u32[]{:S(2)}) async-start(bf16[16,32,256]{2,1,0:T(8,128)(2,1)} %broadcast_in_dim.10), calls=%async_computation.4 | async-start | bytes 524288 | tf_op jit(solution)/shard_map/all_to_all | solution.py:38
  123.3 15.2 %collective-permute-start.2 = (bf16[512,256]{1,0:T(8,128)(2,1)S(1)}, bf16[512,256]{1,0:T(8,128)(2,1)}, u32[]{:S(2)}, u32[]{:S(2)}) collective-permute-start(bf16[512,256]{1,0:T(8,128)(2,1)S(1)} %constant_dynamic-slice_fusion), channel_id=1, source_target_pairs={{0,16},{16,0},{1,17},{17,1},{2,18},{18,2},{3,19},{19,3},{4,20},{20... | collective-permute-start | bytes 786440 | tf_op jit(solution)/shard_map/ppermute | solution.py:49
  161.3 20.6 %all-to-all-start.6 = ((bf16[16,32,512]{2,1,0:T(8,128)(2,1)}), bf16[16,32,512]{2,1,0:T(8,128)(2,1)}, u32[]{:S(2)}, u32[]{:S(2)}) async-start(bf16[16,32,512]{2,1,0:T(8,128)(2,1)} %broadcast_in_dim.11), calls=%async_computation.6 | async-start | bytes 1048576 | tf_op jit(solution)/shard_map/all_to_all | solution.py:38
  181.9 6.0 %collective-permute-start.3 = (bf16[512,512]{1,0:T(8,128)(2,1)}, bf16[512,512]{1,0:T(8,128)(2,1)S(1)}, u32[]{:S(2)}, u32[]{:S(2)}) collective-permute-start(bf16[512,512]{1,0:T(8,128)(2,1)} %bitcast.11), channel_id=1, source_target_pairs={{0,16},{16,0},{1,17},{17,1},{2,18},{18,2},{3,19},{19,3},{4,20},{20... | collective-permute-start | bytes 1572872 | tf_op jit(solution)/shard_map/ppermute | solution.py:49

commit v2 on v1

v2 whole, which is shorter than its diff:
```python
import math

import jax
import jax.numpy as jnp
from jax import lax
from jax.sharding import Mesh
from jax.sharding import PartitionSpec as P

gelu_scale = math.sqrt(2.0 / math.pi)
ROWS = ("zh", "x")
TENSOR = ("y", "zl")
SWAP = [(0, 1), (1, 0)]


def gelu_pair(hidden):
    argument = gelu_scale * (hidden + 0.044715 * hidden * hidden * hidden)
    hyper = jnp.tanh(argument)
    values = 0.5 * hidden * (1.0 + hyper)
    derivative = 0.5 * (1.0 + hyper) + 0.5 * hidden * (1.0 - hyper * hyper) * gelu_scale * (
        1.0 + 3.0 * 0.044715 * hidden * hidden
    )
    return (values, derivative)


def dot(left_side, right_side, left_dim=1, right_dim=0):
    return lax.dot_general(
        left_side,
        right_side,
        (((left_dim,), (right_dim,)), ((), ())),
        preferred_element_type=jnp.float32,
    )


def gather_rows(block, axes):
    count = lax.axis_size(axes)
    copies = jnp.broadcast_to(block[None], (count,) + block.shape)
    copies = copies.reshape(count * block.shape[0], block.shape[1])
    return lax.all_to_all(copies, axes, split_axis=0, concat_axis=0, tiled=True)


def sum_rows(partial, axes):
    count = lax.axis_size(axes)
    pieces = lax.all_to_all(partial, axes, split_axis=0, concat_axis=0, tiled=True)
    pieces = pieces.reshape(count, partial.shape[0] // count, partial.shape[1])
    return jnp.sum(pieces.astype(jnp.float32), axis=0)


def swap_cores(block):
    return lax.ppermute(block, "c", SWAP)


def on_device(tokens, weight_in, tangent_in, weight_out, tangent_out, curvature):
    core = lax.axis_index("c")
    hidden = weight_in.shape[1]
    features = tokens.shape[1]
    share = tokens.shape[0] // 2

    def rows(array, which):
        return lax.dynamic_slice_in_dim(array, which * share, share, 0)

    def both_cores(array, axis):
        return jnp.concatenate([array, swap_cores(array)], axis=axis)

    def my_rows(array):
        mine = rows(array, core)
        return jnp.concatenate([mine, swap_cores(rows(array, 1 - core))], axis=1)

    tokens_all = gather_rows(my_rows(tokens), TENSOR)
    scale = my_rows(curvature)
    pair = both_cores(jnp.concatenate([weight_in, tangent_in], axis=1), 0)
    out_both = both_cores(weight_out, 1)
    tangent_both = both_cores(tangent_out, 1)

    joined = sum_rows(dot(tokens_all, pair).astype(jnp.bfloat16), ROWS)
    values, derivative = gelu_pair(joined[:, :hidden])
    moved = derivative * joined[:, hidden:]
    both = gather_rows(jnp.concatenate([values, moved], axis=1).astype(jnp.bfloat16), ROWS)
    active = both[:, :hidden]

    output_tangent = dot(both[:, hidden:], out_both) + dot(active, tangent_both)
    output_tangent = sum_rows(output_tangent.astype(jnp.bfloat16), TENSOR)
    cotangent = gather_rows((scale * output_tangent).astype(jnp.bfloat16), TENSOR)

    backward = sum_rows(dot(cotangent, out_both, 1, 1).astype(jnp.bfloat16), ROWS)
    far_out = swap_cores(dot(active, cotangent[:, features:], 0, 0).astype(jnp.bfloat16))
    product_out = dot(active, cotangent[:, :features], 0, 0) + far_out.astype(jnp.float32)

    hidden_grad = gather_rows((backward * derivative).astype(jnp.bfloat16), ROWS)
    far_in = swap_cores(dot(tokens_all[:, features:], hidden_grad, 0, 0).astype(jnp.bfloat16))
    product_in = dot(tokens_all[:, :features], hidden_grad, 0, 0) + far_in.astype(jnp.float32)
    return (product_in.astype(jnp.bfloat16), product_out.astype(jnp.bfloat16))


def solution(mesh):
    fine = Mesh(mesh.devices.reshape(4, 4, 2, 8, 2), ("zh", "x", "c", "y", "zl"))
    by_dp = ("zh", "x", "c")
    return jax.shard_map(
        on_device,
        mesh=fine,
        in_specs=(
            P(TENSOR, by_dp),
            P(by_dp, TENSOR),
            P(by_dp, TENSOR),
            P(TENSOR, by_dp),
            P(TENSOR, by_dp),
            P(TENSOR, by_dp),
        ),
        out_specs=(P(by_dp, TENSOR), P(TENSOR, by_dp)),
        check_vma=False,
    )
```

time: 192 us -> 180 us (0.938)
  blocking collectives: 113 us -> 86.1 us
  starting transfers between devices: 34.8 us -> 46.7 us
  waiting for transfers between devices: 28.6 us -> 33.8 us
  local copies, waits for them, and re-layouts: 5.51 us -> 3.3 us
    all_to_all x3 -> x2, blocking collectives: 74.7 us -> 58 us  [sum_rows(): lax.all_to_all(partial, axes, split_axis=0, concat_axis=0, tiled=True)]
    ppermute x4 -> x7, starting transfers between devices: 16.1 us -> 28.4 us  [swap_cores(): return lax.ppermute(block, 'c', SWAP)]
    all_gather x2 -> x0, blocking collectives: 9.5 us -> none  [other_core(): both = lax.all_gather(block, 'c', axis=0, tiled=False)]
    all_to_all x3 -> x2, starting transfers between devices: 18.7 us -> 13.8 us  [gather_rows(): return lax.all_to_all(copies, axes, split_axis=0, concat_axis=0, tiled=True)]
    all_to_all x0 -> x1, starting transfers between devices: none -> 4.54 us  [sum_rows(): lax.all_to_all(partial, axes, split_axis=0, concat_axis=0, tiled=True)]
    all_to_all x0 -> x1, waiting for transfers between devices: none -> 4.39 us  [sum_rows(): lax.all_to_all(partial, axes, split_axis=0, concat_axis=0, tiled=True)]
    ppermute x4 -> x7, waiting for transfers between devices: 1.59 us -> 3.62 us  [swap_cores(): return lax.ppermute(block, 'c', SWAP)]
    all_to_all x3 -> x2, waiting for transfers between devices: 27 us -> 25.8 us  [gather_rows(): return lax.all_to_all(copies, axes, split_axis=0, concat_axis=0, tiled=True)]
  transfers between devices with their start and end apart: 7 -> 10, of which waited for: 4 -> 6; matrix products, arithmetic and copies ran while one was open for 2% -> 2% of each run, Pallas kernels for 0% -> 0%
where the time goes in v2:
time: 180 us; the launch traced here: 179 us
  blocking collectives  86.1 us (48%)
  starting transfers between devices  46.7 us (26%)
  waiting for transfers between devices  33.8 us (19%)
  matrix products  7.69 us (4%)
  local copies, waits for them, and re-layouts  3.3 us (2%)
    all_to_all x2, blocking collectives, sum_rows(): lax.all_to_all(partial, axes, split_axis=0, concat_axis=0, tiled=True)  58 us
    ppermute x7, starting transfers between devices, swap_cores(): return lax.ppermute(block, 'c', SWAP)  28.4 us
    all_to_all x2, blocking collectives, gather_rows(): return lax.all_to_all(copies, axes, split_axis=0, concat_axis=0, tiled=True)  28.1 us
    all_to_all x2, waiting for transfers between devices, gather_rows(): return lax.all_to_all(copies, axes, split_axis=0, concat_axis=0, tiled=True)  25.8 us
    all_to_all x2, starting transfers between devices, gather_rows(): return lax.all_to_all(copies, axes, split_axis=0, concat_axis=0, tiled=True)  13.8 us
    dot_general x8, matrix products, dot(): lax.dot_general(left_side, right_side, (((left_dim,), (right_dim,)), ((),...  7.69 us
    all_to_all x1, starting transfers between devices, sum_rows(): lax.all_to_all(partial, axes, split_axis=0, concat_axis=0, tiled=True)  4.54 us
    all_to_all x1, waiting for transfers between devices, sum_rows(): lax.all_to_all(partial, axes, split_axis=0, concat_axis=0, tiled=True)  4.39 us
  transfers between devices with their start and end apart: 10, of which 6 were waited for; matrix products, arithmetic and copies ran while one was open for 2% of the time, Pallas kernels for 0%

profile of v2, /device:TPU:1, one launch (start us, length us, event | category | flops | bytes accessed | tf_op | source)
XLA Modules:
  0.0 178.9 jit_solution(8069939272542871906)
XLA Ops:
  0.6 0.0 copy-start
  0.6 0.0 copy-start.3
  0.6 1.1 constant_dynamic-update-slice_fusion.1
  1.8 0.0 copy-done
  1.9 8.8 %collective-permute-start.2 = (bf16[256,2048]{1,0:T(8,128)(2,1)S(1)}, bf16[256,2048]{1,0:T(8,128)(2,1)S(1)}, u32[]{:S(2)}, u32[]{:S(2)}) collective-permute-start(bf16[256,2048]{1,0:T(8,128)(2,1)S(1)} %constant_dynamic-update-slice_fusion), channel_id=1, source_target_pairs={{0,16},{16,0},{1,17},{17,1},{2,18},{18,2},{3,19},{19,3},{4,20},{20... | collective-permute-start | bytes 3145736 | tf_op jit(solution)/shard_map/ppermute | solution.py:49
  10.7 0.0 copy-done.3
  10.7 1.9 %collective-permute-start = (bf16[16,256]{1,0:T(8,128)(2,1)S(1)}, bf16[16,256]{1,0:T(8,128)(2,1)S(1)}, u32[]{:S(2)}, u32[]{:S(2)}) collective-permute-start(bf16[16,256]{1,0:T(8,128)(2,1)S(1)} %get-tuple-element.7), channel_id=1, source_target_pairs={{0,16},{16,0},{1,17},{17,1},{2,18},{18,2},{3,19},{19,3},{4,20},{20... | collective-permute-start | bytes 24584 | tf_op jit(solution)/shard_map/ppermute | solution.py:49
  12.6 1.1 collective-permute-done
  13.8 14.5 %all_to_all.63 = bf16[16,16,512]{2,1,0:T(8,128)(2,1)S(1)} all-to-all(bf16[16,16,512]{2,1,0:T(8,128)(2,1)S(1)} %broadcast_in_dim.8), channel_id=1, replica_groups=mesh['zh'=4,'x'=4,'c'=2,'y'=8,'zl'=2] {'y','zl'}, dimensions={0} | all-to-all | bytes 524288 | tf_op jit(solution)/shard_map/all_to_all | solution.py:38
  28.3 0.0 collective-permute-done.2
  28.3 0.7 convolution_convert_fusion
  29.0 39.2 %all_to_all.64 = bf16[16,16,2048]{2,1,0:T(8,128)(2,1)S(1)} all-to-all(bf16[16,16,2048]{2,1,0:T(8,128)(2,1)S(1)} %bitcast.23), channel_id=1, replica_groups=mesh['zh'=4,'x'=4,'c'=2,'y'=8,'zl'=2] {'zh','x'}, dimensions={0} | all-to-all | bytes 2097152 | tf_op jit(solution)/shard_map/all_to_all | solution.py:43
  68.2 0.1 convert_reduce_fusion
  68.4 0.1 multiply_convert_fusion.1
  68.4 1.1 broadcast_in_dim.9
  69.5 0.0 copy-start.1
  69.5 6.1 %all-to-all-start.2 = ((bf16[16,16,2048]{2,1,0:T(8,128)(2,1)}), bf16[16,16,2048]{2,1,0:T(8,128)(2,1)S(1)}, u32[]{:S(2)}, u32[]{:S(2)}) async-start(bf16[16,16,2048]{2,1,0:T(8,128)(2,1)} %broadcast_in_dim.9), calls=%async_computation.2 | async-start | bytes 2097152 | tf_op jit(solution)/shard_map/all_to_all | solution.py:38
  75.6 0.0 copy-done.1
  75.6 2.7 %collective-permute-start.3 = (bf16[1024,256]{1,0:T(8,128)(2,1)S(1)}, bf16[1024,256]{1,0:T(8,128)(2,1)S(1)}, u32[]{:S(2)}, u32[]{:S(2)}) collective-permute-start(bf16[1024,256]{1,0:T(8,128)(2,1)S(1)} %copy-done.1), channel_id=1, source_target_pairs={{0,16},{16,0},{1,17},{17,1},{2,18},{18,2},{3,19},{19,3},{4,20},{20... | collective-permute-start | bytes 1572872 | tf_op jit(solution)/shard_map/ppermute | solution.py:49
  78.4 1.9 %collective-permute-start.4 = (bf16[1024,256]{1,0:T(8,128)(2,1)}, bf16[1024,256]{1,0:T(8,128)(2,1)}, u32[]{:S(2)}, u32[]{:S(2)}) collective-permute-start(bf16[1024,256]{1,0:T(8,128)(2,1)} %param.10), channel_id=1, source_target_pairs={{0,16},{16,0},{1,17},{17,1},{2,18},{18,2},{3,19},{19,3},{4,20},{20... | collective-permute-start | bytes 1572872 | tf_op jit(solution)/shard_map/ppermute | solution.py:49
  80.4 0.0 collective-permute-done.3
  80.4 2.1 %collective-permute-done.4 = bf16[1024,256]{1,0:T(8,128)(2,1)} collective-permute-done((bf16[1024,256]{1,0:T(8,128)(2,1)}, bf16[1024,256]{1,0:T(8,128)(2,1)}, u32[]{:S(2)}, u32[]{:S(2)}) %collective-permute-start.4) | collective-permute-done | bytes 524320 | tf_op jit(solution)/shard_map/ppermute | solution.py:49
  82.5 16.6 %all-to-all-done.2 = bf16[16,16,2048]{2,1,0:T(8,128)(2,1)S(1)} async-done(((bf16[16,16,2048]{2,1,0:T(8,128)(2,1)}), bf16[16,16,2048]{2,1,0:T(8,128)(2,1)S(1)}, u32[]{:S(2)}, u32[]{:S(2)}) %all-to-all-start.2) | async-done | bytes 1048608 | tf_op jit(solution)/shard_map/all_to_all | solution.py:38
  99.1 1.6 fusion.4
  100.8 0.0 copy-start.2
  100.8 1.1 fusion.3
  101.9 4.5 %all-to-all-start.3 = ((bf16[16,16,512]{2,1,0:T(8,128)(2,1)}), bf16[16,16,512]{2,1,0:T(8,128)(2,1)S(1)}, u32[]{:S(2)}, u32[]{:S(2)}) async-start(bf16[16,16,512]{2,1,0:T(8,128)(2,1)} %bitcast.3), calls=%async_computation.3 | async-start | bytes 524288 | tf_op jit(solution)/shard_map/all_to_all | solution.py:43
  106.5 0.0 copy-done.2
  106.5 5.2 %collective-permute-start.1 = (f32[16,256]{1,0:T(8,128)S(1)}, f32[16,256]{1,0:T(8,128)S(1)}, u32[]{:S(2)}, u32[]{:S(2)}) collective-permute-start(f32[16,256]{1,0:T(8,128)S(1)} %get-tuple-element.5), channel_id=1, source_target_pairs={{0,16},{16,0},{1,17},{17,1},{2,18},{18,2},{3,19},{19,3},{4,20},{20... | collective-permute-start | bytes 49160 | tf_op jit(solution)/shard_map/ppermute | solution.py:49
  111.7 4.4 %all-to-all-done.3 = bf16[16,16,512]{2,1,0:T(8,128)(2,1)S(1)} async-done(((bf16[16,16,512]{2,1,0:T(8,128)(2,1)}), bf16[16,16,512]{2,1,0:T(8,128)(2,1)S(1)}, u32[]{:S(2)}, u32[]{:S(2)}) %all-to-all-start.3) | async-done | bytes 262176 | tf_op jit(solution)/shard_map/all_to_all | solution.py:43
  116.2 0.0 collective-permute-done.1
  116.2 13.6 %all_to_all.65 = bf16[16,16,512]{2,1,0:T(8,128)(2,1)S(1)} all-to-all(bf16[16,16,512]{2,1,0:T(8,128)(2,1)S(1)} %broadcast_in_dim.10), channel_id=1, replica_groups=mesh['zh'=4,'x'=4,'c'=2,'y'=8,'zl'=2] {'y','zl'}, dimensions={0} | all-to-all | bytes 524288 | tf_op jit(solution)/shard_map/all_to_all | solution.py:38
  129.8 0.5 convolution_convert_fusion.3
  130.3 18.8 %all_to_all.66 = bf16[16,16,1024]{2,1,0:T(8,128)(2,1)S(1)} all-to-all(bf16[16,16,1024]{2,1,0:T(8,128)(2,1)S(1)} %bitcast.19), channel_id=1, replica_groups=mesh['zh'=4,'x'=4,'c'=2,'y'=8,'zl'=2] {'zh','x'}, dimensions={0} | all-to-all | bytes 1048576 | tf_op jit(solution)/shard_map/all_to_all | solution.py:43
  149.1 0.1 convert_reduce_fusion.1
  149.2 0.1 multiply_convert_fusion
  149.2 0.9 broadcast_in_dim.11
  150.1 7.7 %all-to-all-start.6 = ((bf16[16,16,1024]{2,1,0:T(8,128)(2,1)}), bf16[16,16,1024]{2,1,0:T(8,128)(2,1)S(1)}, u32[]{:S(2)}, u32[]{:S(2)}) async-start(bf16[16,16,1024]{2,1,0:T(8,128)(2,1)} %broadcast_in_dim.11), calls=%async_computation.6 | async-start | bytes 1048576 | tf_op jit(solution)/shard_map/all_to_all | solution.py:38
  157.8 1.1 convolution_convert_fusion.1
  158.9 2.7 %collective-permute-start.6 = (bf16[1024,256]{1,0:T(8,128)(2,1)}, bf16[1024,256]{1,0:T(8,128)(2,1)S(1)}, u32[]{:S(2)}, u32[]{:S(2)}) collective-permute-start(bf16[1024,256]{1,0:T(8,128)(2,1)} %convolution_convert_fusion.1), channel_id=1, source_target_pairs={{0,16},{16,0},{1,17},{17,1},{2,18},{18,2},{3,19},{19,3},{4,20},{20... | collective-permute-start | bytes 1572872 | tf_op jit(solution)/shard_map/ppermute | solution.py:49
  161.6 9.1 %all-to-all-done.6 = bf16[16,16,1024]{2,1,0:T(8,128)(2,1)S(1)} async-done(((bf16[16,16,1024]{2,1,0:T(8,128)(2,1)}), bf16[16,16,1024]{2,1,0:T(8,128)(2,1)S(1)}, u32[]{:S(2)}, u32[]{:S(2)}) %all-to-all-start.6) | async-done | bytes 524320 | tf_op jit(solution)/shard_map/all_to_all | solution.py:38
  170.8 0.3 convolution_convert_fusion.2
  171.1 5.1 %collective-permute-start.5 = (bf16[256,1024]{1,0:T(8,128)(2,1)S(1)}, bf16[256,1024]{1,0:T(8,128)(2,1)S(1)}, u32[]{:S(2)}, u32[]{:S(2)}) collective-permute-start(bf16[256,1024]{1,0:T(8,128)(2,1)S(1)} %convolution_convert_fusion.2), channel_id=1, source_target_pairs={{0,16},{16,0},{1,17},{17,1},{2,18},{18,2},{3,19},{19,3},{4,20},{20... | collective-permute-start | bytes 1572872 | tf_op jit(solution)/shard_map/ppermute | solution.py:49
  176.2 0.0 collective-permute-done.6
  176.2 1.2 add_convert_fusion
  177.4 0.4 collective-permute-done.5
  177.7 1.1 add_convert_fusion.1
  (11 shorter events, 0.2 us)
Async XLA Ops:
  0.6 1.2 copy-start
  0.6 10.0 %copy-start.3 = (bf16[32,256]{1,0:T(8,128)(2,1)S(1)}, bf16[32,256]{1,0:T(8,128)(2,1)}, u32[]{:S(2)}) copy-start(bf16[32,256]{1,0:T(8,128)(2,1)} %param.6) | copy-start | bytes 49156
  1.9 26.4 %collective-permute-start.2 = (bf16[256,2048]{1,0:T(8,128)(2,1)S(1)}, bf16[256,2048]{1,0:T(8,128)(2,1)S(1)}, u32[]{:S(2)}, u32[]{:S(2)}) collective-permute-start(bf16[256,2048]{1,0:T(8,128)(2,1)S(1)} %constant_dynamic-update-slice_fusion), channel_id=1, source_target_pairs={{0,16},{16,0},{1,17},{17,1},{2,18},{18,2},{3,19},{19,3},{4,20},{20... | collective-permute-start | bytes 3145736 | tf_op jit(solution)/shard_map/ppermute | solution.py:49
  10.7 3.1 %collective-permute-start = (bf16[16,256]{1,0:T(8,128)(2,1)S(1)}, bf16[16,256]{1,0:T(8,128)(2,1)S(1)}, u32[]{:S(2)}, u32[]{:S(2)}) collective-permute-start(bf16[16,256]{1,0:T(8,128)(2,1)S(1)} %get-tuple-element.7), channel_id=1, source_target_pairs={{0,16},{16,0},{1,17},{17,1},{2,18},{18,2},{3,19},{19,3},{4,20},{20... | collective-permute-start | bytes 24584 | tf_op jit(solution)/shard_map/ppermute | solution.py:49
  69.5 6.1 %copy-start.1 = (bf16[1024,256]{1,0:T(8,128)(2,1)S(1)}, bf16[1024,256]{1,0:T(8,128)(2,1)}, u32[]{:S(2)}) copy-start(bf16[1024,256]{1,0:T(8,128)(2,1)} %param.9) | copy-start | bytes 1572868
  69.5 29.6 %all-to-all-start.2 = ((bf16[16,16,2048]{2,1,0:T(8,128)(2,1)}), bf16[16,16,2048]{2,1,0:T(8,128)(2,1)S(1)}, u32[]{:S(2)}, u32[]{:S(2)}) async-start(bf16[16,16,2048]{2,1,0:T(8,128)(2,1)} %broadcast_in_dim.9), calls=%async_computation.2 | async-start | bytes 2097152 | tf_op jit(solution)/shard_map/all_to_all | solution.py:38
  75.6 4.7 %collective-permute-start.3 = (bf16[1024,256]{1,0:T(8,128)(2,1)S(1)}, bf16[1024,256]{1,0:T(8,128)(2,1)S(1)}, u32[]{:S(2)}, u32[]{:S(2)}) collective-permute-start(bf16[1024,256]{1,0:T(8,128)(2,1)S(1)} %copy-done.1), channel_id=1, source_target_pairs={{0,16},{16,0},{1,17},{17,1},{2,18},{18,2},{3,19},{19,3},{4,20},{20... | collective-permute-start | bytes 1572872 | tf_op jit(solution)/shard_map/ppermute | solution.py:49
  78.4 4.1 %collective-permute-start.4 = (bf16[1024,256]{1,0:T(8,128)(2,1)}, bf16[1024,256]{1,0:T(8,128)(2,1)}, u32[]{:S(2)}, u32[]{:S(2)}) collective-permute-start(bf16[1024,256]{1,0:T(8,128)(2,1)} %param.10), channel_id=1, source_target_pairs={{0,16},{16,0},{1,17},{17,1},{2,18},{18,2},{3,19},{19,3},{4,20},{20... | collective-permute-start | bytes 1572872 | tf_op jit(solution)/shard_map/ppermute | solution.py:49
  100.8 5.7 %copy-start.2 = (f32[32,256]{1,0:T(8,128)S(1)}, f32[32,256]{1,0:T(8,128)}, u32[]{:S(2)}) copy-start(f32[32,256]{1,0:T(8,128)} %param.11) | copy-start | bytes 98308
  101.9 14.2 %all-to-all-start.3 = ((bf16[16,16,512]{2,1,0:T(8,128)(2,1)}), bf16[16,16,512]{2,1,0:T(8,128)(2,1)S(1)}, u32[]{:S(2)}, u32[]{:S(2)}) async-start(bf16[16,16,512]{2,1,0:T(8,128)(2,1)} %bitcast.3), calls=%async_computation.3 | async-start | bytes 524288 | tf_op jit(solution)/shard_map/all_to_all | solution.py:43
  106.5 9.7 %collective-permute-start.1 = (f32[16,256]{1,0:T(8,128)S(1)}, f32[16,256]{1,0:T(8,128)S(1)}, u32[]{:S(2)}, u32[]{:S(2)}) collective-permute-start(f32[16,256]{1,0:T(8,128)S(1)} %get-tuple-element.5), channel_id=1, source_target_pairs={{0,16},{16,0},{1,17},{17,1},{2,18},{18,2},{3,19},{19,3},{4,20},{20... | collective-permute-start | bytes 49160 | tf_op jit(solution)/shard_map/ppermute | solution.py:49
  150.1 20.7 %all-to-all-start.6 = ((bf16[16,16,1024]{2,1,0:T(8,128)(2,1)}), bf16[16,16,1024]{2,1,0:T(8,128)(2,1)S(1)}, u32[]{:S(2)}, u32[]{:S(2)}) async-start(bf16[16,16,1024]{2,1,0:T(8,128)(2,1)} %broadcast_in_dim.11), calls=%async_computation.6 | async-start | bytes 1048576 | tf_op jit(solution)/shard_map/all_to_all | solution.py:38
  158.9 17.3 %collective-permute-start.6 = (bf16[1024,256]{1,0:T(8,128)(2,1)}, bf16[1024,256]{1,0:T(8,128)(2,1)S(1)}, u32[]{:S(2)}, u32[]{:S(2)}) collective-permute-start(bf16[1024,256]{1,0:T(8,128)(2,1)} %convolution_convert_fusion.1), channel_id=1, source_target_pairs={{0,16},{16,0},{1,17},{17,1},{2,18},{18,2},{3,19},{19,3},{4,20},{20... | collective-permute-start | bytes 1572872 | tf_op jit(solution)/shard_map/ppermute | solution.py:49
  171.1 6.6 %collective-permute-start.5 = (bf16[256,1024]{1,0:T(8,128)(2,1)S(1)}, bf16[256,1024]{1,0:T(8,128)(2,1)S(1)}, u32[]{:S(2)}, u32[]{:S(2)}) collective-permute-start(bf16[256,1024]{1,0:T(8,128)(2,1)S(1)} %convolution_convert_fusion.2), channel_id=1, source_target_pairs={{0,16},{16,0},{1,17},{17,1},{2,18},{18,2},{3,19},{19,3},{4,20},{20... | collective-permute-start | bytes 1572872 | tf_op jit(solution)/shard_map/ppermute | solution.py:49

commit v3 on v2

v3 whole, which is shorter than its diff:
```python
import math

import jax
import jax.numpy as jnp
from jax import lax
from jax.sharding import Mesh
from jax.sharding import PartitionSpec as P

gelu_scale = math.sqrt(2.0 / math.pi)
ROWS = ("x", "zh")
TENSOR = ("y", "zl")
SWAP = [(0, 1), (1, 0)]


def gelu_pair(hidden):
    argument = gelu_scale * (hidden + 0.044715 * hidden * hidden * hidden)
    hyper = jnp.tanh(argument)
    values = 0.5 * hidden * (1.0 + hyper)
    derivative = 0.5 * (1.0 + hyper) + 0.5 * hidden * (1.0 - hyper * hyper) * gelu_scale * (
        1.0 + 3.0 * 0.044715 * hidden * hidden
    )
    return (values, derivative)


def dot(left_side, right_side, left_dim=1, right_dim=0):
    return lax.dot_general(
        left_side,
        right_side,
        (((left_dim,), (right_dim,)), ((), ())),
        preferred_element_type=jnp.float32,
    )


def exchange(pieces, axes):
    return lax.all_to_all(pieces, axes, split_axis=0, concat_axis=0, tiled=True)


def gather_rows(block, axes):
    count = lax.axis_size(axes)
    copies = jnp.broadcast_to(block[None], (count,) + block.shape)
    return exchange(copies.reshape(count * block.shape[0], block.shape[1]), axes)


def sum_rows(partial, axes):
    count = lax.axis_size(axes)
    pieces = exchange(partial, axes)
    pieces = pieces.reshape(count, partial.shape[0] // count, partial.shape[1])
    return jnp.sum(pieces.astype(jnp.float32), axis=0)


def sum_rows_staged(partial):
    return sum_rows(sum_rows(partial, ("x",)).astype(jnp.bfloat16), ("zh",))


def gather_rows_staged(block):
    return gather_rows(gather_rows(block, ("zh",)), ("x",))


def swap_cores(block):
    return lax.ppermute(block, "c", SWAP)


def on_device(tokens, weight_in, tangent_in, weight_out, tangent_out, curvature):
    core = lax.axis_index("c")
    first_core = core == 0
    hidden = weight_in.shape[1]
    features = tokens.shape[1]
    share = tokens.shape[0] // 2

    halves = tokens.reshape(2, 1, share, features)
    copies = jnp.broadcast_to(halves, (2, lax.axis_size(TENSOR), share, features))
    arrived = exchange(copies.reshape(-1, features), ("c",) + TENSOR).reshape(2, -1, features)
    tokens_own = lax.dynamic_index_in_dim(arrived, core, 0, keepdims=False)
    tokens_far = lax.dynamic_index_in_dim(arrived, 1 - core, 0, keepdims=False)

    in_own = jnp.concatenate([weight_in, tangent_in], axis=1)
    in_far = swap_cores(in_own)
    out_own = jnp.concatenate([weight_out, tangent_out], axis=0)
    out_far = swap_cores(out_own)
    scale_own = lax.dynamic_slice_in_dim(curvature, core * share, share, 0)
    scale_far = swap_cores(lax.dynamic_slice_in_dim(curvature, (1 - core) * share, share, 0))

    joined = (dot(tokens_own, in_own) + dot(tokens_far, in_far)).astype(jnp.bfloat16)
    joined, out_far, scale_far = lax.optimization_barrier((joined, out_far, scale_far))
    joined = lax.cond(first_core, sum_rows_staged, lambda p: sum_rows(p, ROWS), joined)
    values, derivative = gelu_pair(joined[:, :hidden])
    moved = derivative * joined[:, hidden:]
    both = jnp.concatenate([moved, values], axis=1).astype(jnp.bfloat16)
    both = lax.cond(first_core, lambda b: gather_rows(b, ROWS), gather_rows_staged, both)
    active = both[:, hidden:]

    output_tangent = jnp.concatenate([dot(both, out_own), dot(both, out_far)], axis=1)
    output_tangent = sum_rows(output_tangent.astype(jnp.bfloat16), TENSOR)
    scale = jnp.concatenate([scale_own, scale_far], axis=1)
    cotangent = gather_rows((scale * output_tangent).astype(jnp.bfloat16), TENSOR)
    cotangent_own, cotangent_far = cotangent[:, :features], cotangent[:, features:]

    backward = dot(cotangent_own, weight_out, 1, 1) + dot(cotangent_far, out_far[:hidden], 1, 1)
    backward = sum_rows(backward.astype(jnp.bfloat16), ROWS)
    far_out = swap_cores(dot(active, cotangent_far, 0, 0).astype(jnp.bfloat16))
    product_out = dot(active, cotangent_own, 0, 0) + far_out.astype(jnp.float32)

    hidden_grad = gather_rows((backward * derivative).astype(jnp.bfloat16), ROWS)
    far_in = swap_cores(dot(tokens_far, hidden_grad, 0, 0).astype(jnp.bfloat16))
    product_in = dot(tokens_own, hidden_grad, 0, 0) + far_in.astype(jnp.float32)
    return (product_in.astype(jnp.bfloat16), product_out.astype(jnp.bfloat16))


def solution(mesh):
    fine = Mesh(mesh.devices.reshape(4, 4, 2, 8, 2), ("zh", "x", "c", "y", "zl"))
    by_dp = ("zh", "x", "c")
    return jax.shard_map(
        on_device,
        mesh=fine,
        in_specs=(
            P(TENSOR, by_dp),
            P(by_dp, TENSOR),
            P(by_dp, TENSOR),
            P(TENSOR, by_dp),
            P(TENSOR, by_dp),
            P(TENSOR, by_dp),
        ),
        out_specs=(P(by_dp, TENSOR), P(TENSOR, by_dp)),
        check_vma=False,
    )
```

time: 180 us -> 166 us (0.922)
  waiting for transfers between devices: 33.8 us -> 10.2 us
  blocking collectives: 86.1 us -> 99.6 us
  starting transfers between devices: 46.7 us -> 40.6 us
  local copies, waits for them, and re-layouts: 3.3 us -> 5.64 us
    all_to_all x3 -> x2, waiting for transfers between devices: 30.1 us -> 9.81 us  [exchange(): return lax.all_to_all(pieces, axes, split_axis=0, concat_axis=0, tiled=True)]
    all_to_all x4 -> x6, blocking collectives: 86.1 us -> 99.6 us  [exchange(): return lax.all_to_all(pieces, axes, split_axis=0, concat_axis=0, tiled=True)]
    all_to_all x3 -> x2, starting transfers between devices: 18.3 us -> 7.38 us  [exchange(): return lax.all_to_all(pieces, axes, split_axis=0, concat_axis=0, tiled=True)]
    ppermute x7 -> x5, starting transfers between devices: 28.4 us -> 33.2 us  [swap_cores(): return lax.ppermute(block, 'c', SWAP)]
    ppermute x7 -> x5, waiting for transfers between devices: 3.62 us -> 0.36 us  [swap_cores(): return lax.ppermute(block, 'c', SWAP)]
    dot_general x8 -> x10, matrix products: 7.69 us -> 7.41 us  [dot(): lax.dot_general(left_side, right_side, (((left_dim,), (right_dim,)), ((),...]
  transfers between devices with their start and end apart: 10 -> 7, of which waited for: 6 -> 3; matrix products, arithmetic and copies ran while one was open for 2% -> 3% of each run, Pallas kernels for 0% -> 0%
where the time goes in v3:
time: 166 us; the launch traced here: 165 us
  blocking collectives  99.6 us (60%)
  starting transfers between devices  40.6 us (24%)
  waiting for transfers between devices  10.2 us (6%)
  matrix products  7.41 us (4%)
  local copies, waits for them, and re-layouts  5.64 us (3%)
    all_to_all x6, blocking collectives, exchange(): return lax.all_to_all(pieces, axes, split_axis=0, concat_axis=0, tiled=True)  99.6 us
    ppermute x5, starting transfers between devices, swap_cores(): return lax.ppermute(block, 'c', SWAP)  33.2 us
    all_to_all x2, waiting for transfers between devices, exchange(): return lax.all_to_all(pieces, axes, split_axis=0, concat_axis=0, tiled=True)  9.81 us
    dot_general x10, matrix products, dot(): lax.dot_general(left_side, right_side, (((left_dim,), (right_dim,)), ((),...  7.41 us
    all_to_all x2, starting transfers between devices, exchange(): return lax.all_to_all(pieces, axes, split_axis=0, concat_axis=0, tiled=True)  7.38 us
  transfers between devices with their start and end apart: 7, of which 3 were waited for; matrix products, arithmetic and copies ran while one was open for 3% of the time, Pallas kernels for 0%

profile of v3, /device:TPU:1, one launch (start us, length us, event | category | flops | bytes accessed | tf_op | source)
XLA Modules:
  0.0 165.5 jit_solution(9425633783665219337)
XLA Ops:
  0.6 0.0 copy-start.2
  0.7 1.2 constant_dynamic-update-slice_fusion.1
  1.8 0.0 copy-start.7
  1.8 1.1 constant_dynamic-update-slice_fusion
  2.9 8.8 %collective-permute-start = (bf16[256,2048]{1,0:T(8,128)(2,1)S(1)}, bf16[256,2048]{1,0:T(8,128)(2,1)}, u32[]{:S(2)}, u32[]{:S(2)}) collective-permute-start(bf16[256,2048]{1,0:T(8,128)(2,1)S(1)} %constant_dynamic-update-slice_fusion), channel_id=1, source_target_pairs={{0,16},{16,0},{1,17},{17,1},{2,18},{18,2},{3,19},{19,3},{4,20},{20... | collective-permute-start | bytes 3145736 | tf_op jit(solution)/shard_map/ppermute | solution.py:60
  11.7 0.7 broadcast_in_dim.29
  12.5 3.8 %all-to-all-start.6 = ((bf16[32,16,256]{2,1,0:T(8,128)(2,1)}), bf16[32,16,256]{2,1,0:T(8,128)(2,1)S(1)}, u32[]{:S(2)}, u32[]{:S(2)}) async-start(bf16[32,16,256]{2,1,0:T(8,128)(2,1)} %bitcast.7), calls=%async_computation.6 | async-start | bytes 524288 | tf_op jit(solution)/shard_map/all_to_all | solution.py:35
  16.4 2.1 %collective-permute-start.1 = (bf16[2048,256]{1,0:T(8,128)(2,1)S(1)}, bf16[2048,256]{1,0:T(8,128)(2,1)S(1)}, u32[]{:S(2)}, u32[]{:S(2)}) collective-permute-start(bf16[2048,256]{1,0:T(8,128)(2,1)S(1)} %constant_dynamic-update-slice_fusion.2), channel_id=1, source_target_pairs={{0,16},{16,0},{1,17},{17,1},{2,18},{18,2},{3,19},{19,3},{4,20},{20... | collective-permute-start | bytes 3145736 | tf_op jit(solution)/shard_map/ppermute | solution.py:60
  18.6 2.2 %collective-permute-start.2 = (f32[16,256]{1,0:T(8,128)S(1)}, f32[16,256]{1,0:T(8,128)S(1)}, u32[]{:S(2)}, u32[]{:S(2)}) collective-permute-start(f32[16,256]{1,0:T(8,128)S(1)} %get-tuple-element.31), channel_id=1, source_target_pairs={{0,16},{16,0},{1,17},{17,1},{2,18},{18,2},{3,19},{19,3},{4,20},{20... | collective-permute-start | bytes 49160 | tf_op jit(solution)/shard_map/ppermute | solution.py:60
  20.8 7.3 %all-to-all-done.6 = bf16[32,16,256]{2,1,0:T(8,128)(2,1)S(1)} async-done(((bf16[32,16,256]{2,1,0:T(8,128)(2,1)}), bf16[32,16,256]{2,1,0:T(8,128)(2,1)S(1)}, u32[]{:S(2)}, u32[]{:S(2)}) %all-to-all-start.6) | async-done | bytes 262176 | tf_op jit(solution)/shard_map/all_to_all | solution.py:35
  28.1 0.4 fusion.12
  28.5 0.0 collective-permute-done
  28.5 1.7 %fusion = bf16[256,2048]{1,0:T(8,128)(2,1)S(1)} fusion(f32[256,2048]{1,0:T(8,128)S(1)} %fusion.12, bf16[256,2048]{1,0:T(8,128)(2,1)} %collective-permute-done, bf16[2,256,256]{2,1,0:T(8,128)(2,1)S(1)} %bitcast.42, s32[]{:T(128)S(6)} %select_n.15), kind=kOutput, calls=%fused_computation.3 | convolution fusion | flops 269484032 | bytes 4325380 | tf_op jit(solution)/shard_map/dot_general | solution.py:26
  30.2 0.0 copy-start.9
  30.3 0.0 collective-permute-done.1
  30.3 0.6 copy-done.9
  30.9 28.9 %conditional.2 = (f32[16,2048]{1,0:T(8,128)S(1)}) conditional(s32[]{:T(128)} %convert_element_type.60, bf16[256,2048]{1,0:T(8,128)(2,1)S(1)} %fusion, bf16[256,2048]{1,0:T(8,128)(2,1)S(1)} %fusion), branch_computations={%region_0.2_spmd, %region_2.5_spmd} | conditional | flops 1015808 | bytes 4325386 | solution.py:85
  30.9 28.8 %all_to_all.82 = bf16[16,16,2048]{2,1,0:T(8,128)(2,1)S(1)} all-to-all(bf16[16,16,2048]{2,1,0:T(8,128)(2,1)S(1)} %bitcast.35), channel_id=1, replica_groups=mesh['zh'=4,'x'=4,'c'=2,'y'=8,'zl'=2] {'x','zh'}, dimensions={0} | all-to-all | bytes 2097152 | tf_op jit(solution)/shard_map/cond/branch_0_fun/all_to_all | solution.py:35
  59.6 0.1 convert_reduce_fusion
  59.8 0.1 fusion.30
  59.9 0.6 pad_maximum_fusion.1
  60.5 26.1 %conditional.3 = (bf16[256,2048]{1,0:T(8,128)(2,1)S(1)}) conditional(s32[]{:T(128)} %convert_element_type.60, bf16[16,2048]{1,0:T(8,128)(2,1)} %pad_maximum_fusion.1, bf16[16,2048]{1,0:T(8,128)(2,1)} %pad_maximum_fusion.1), branch_computations={%region_5.6_spmd, %region_6.7_spmd} | conditional | bytes 4259848 | solution.py:89
  60.5 0.9 broadcast_in_dim.4
  61.5 10.9 %all_to_all.85 = bf16[4,16,2048]{2,1,0:T(8,128)(2,1)S(1)} all-to-all(bf16[4,16,2048]{2,1,0:T(8,128)(2,1)S(1)} %broadcast_in_dim.4), channel_id=1, replica_groups=mesh['zh'=4,'x'=4,'c'=2,'y'=8,'zl'=2] {'zh'}, dimensions={0} | all-to-all | bytes 524288 | tf_op jit(solution)/shard_map/cond/branch_0_fun/all_to_all | solution.py:35
  72.4 0.1 broadcast_in_dim.10
  72.5 14.1 %all_to_all.86 = bf16[4,64,2048]{2,1,0:T(8,128)(2,1)S(1)} all-to-all(bf16[4,64,2048]{2,1,0:T(8,128)(2,1)S(1)} %broadcast_in_dim.10), channel_id=1, replica_groups=mesh['zh'=4,'x'=4,'c'=2,'y'=8,'zl'=2] {'x'}, dimensions={0} | all-to-all | bytes 2097152 | tf_op jit(solution)/shard_map/cond/branch_0_fun/all_to_all | solution.py:35
  86.6 0.4 convolution_convert_fusion.3
  87.0 0.0 copy-start.10
  87.0 0.0 copy-start.3
  87.0 0.4 convolution_convert_fusion.2
  87.5 16.1 %all_to_all.88 = bf16[16,16,512]{2,1,0:T(8,128)(2,1)S(1)} all-to-all(bf16[16,16,512]{2,1,0:T(8,128)(2,1)S(1)} %pad_maximum_fusion), channel_id=1, replica_groups=mesh['zh'=4,'x'=4,'c'=2,'y'=8,'zl'=2] {'y','zl'}, dimensions={0} | all-to-all | bytes 524288 | tf_op jit(solution)/shard_map/all_to_all | solution.py:35
  103.8 12.2 %all_to_all.89 = bf16[16,16,512]{2,1,0:T(8,128)(2,1)S(1)} all-to-all(bf16[16,16,512]{2,1,0:T(8,128)(2,1)S(1)} %broadcast_in_dim.30), channel_id=1, replica_groups=mesh['zh'=4,'x'=4,'c'=2,'y'=8,'zl'=2] {'y','zl'}, dimensions={0} | all-to-all | bytes 524288 | tf_op jit(solution)/shard_map/all_to_all | solution.py:35
  116.0 0.3 fusion.19
  116.3 0.3 fusion.1
  116.6 0.0 copy-done.4
  116.7 17.5 %all_to_all.90 = bf16[16,16,1024]{2,1,0:T(8,128)(2,1)S(1)} all-to-all(bf16[16,16,1024]{2,1,0:T(8,128)(2,1)S(1)} %bitcast.45), channel_id=1, replica_groups=mesh['zh'=4,'x'=4,'c'=2,'y'=8,'zl'=2] {'x','zh'}, dimensions={0} | all-to-all | bytes 1048576 | tf_op jit(solution)/shard_map/all_to_all | solution.py:35
  134.1 0.1 convert_reduce_fusion.2
  134.2 0.1 multiply_convert_fusion
  134.3 0.9 broadcast_in_dim.31
  135.1 3.6 %all-to-all-start.10 = ((bf16[16,16,1024]{2,1,0:T(8,128)(2,1)}), bf16[16,16,1024]{2,1,0:T(8,128)(2,1)S(1)}, u32[]{:S(2)}, u32[]{:S(2)}) async-start(bf16[16,16,1024]{2,1,0:T(8,128)(2,1)} %broadcast_in_dim.31), calls=%async_computation.10 | async-start | bytes 1048576 | tf_op jit(solution)/shard_map/all_to_all | solution.py:35
  138.7 1.1 convolution_convert_fusion
  139.8 9.6 %collective-permute-start.4 = (bf16[1024,256]{1,0:T(8,128)(2,1)}, bf16[1024,256]{1,0:T(8,128)(2,1)S(1)}, u32[]{:S(2)}, u32[]{:S(2)}) collective-permute-start(bf16[1024,256]{1,0:T(8,128)(2,1)} %convolution_convert_fusion), channel_id=1, source_target_pairs={{0,16},{16,0},{1,17},{17,1},{2,18},{18,2},{3,19},{19,3},{4,20},{20... | collective-permute-start | bytes 1572872 | tf_op jit(solution)/shard_map/ppermute | solution.py:60
  149.4 2.5 %all-to-all-done.10 = bf16[16,16,1024]{2,1,0:T(8,128)(2,1)S(1)} async-done(((bf16[16,16,1024]{2,1,0:T(8,128)(2,1)}), bf16[16,16,1024]{2,1,0:T(8,128)(2,1)S(1)}, u32[]{:S(2)}, u32[]{:S(2)}) %all-to-all-start.10) | async-done | bytes 524320 | tf_op jit(solution)/shard_map/all_to_all | solution.py:35
  152.0 0.3 convolution_convert_fusion.1
  152.3 10.5 %collective-permute-start.3 = (bf16[256,1024]{1,0:T(8,128)(2,1)S(1)}, bf16[256,1024]{1,0:T(8,128)(2,1)S(1)}, u32[]{:S(2)}, u32[]{:S(2)}) collective-permute-start(bf16[256,1024]{1,0:T(8,128)(2,1)S(1)} %convolution_convert_fusion.1), channel_id=1, source_target_pairs={{0,16},{16,0},{1,17},{17,1},{2,18},{18,2},{3,19},{19,3},{4,20},{20... | collective-permute-start | bytes 1572872 | tf_op jit(solution)/shard_map/ppermute | solution.py:60
  162.9 1.2 add_convert_fusion
  164.0 0.4 collective-permute-done.3
  164.4 1.1 add_convert_fusion.1
  (24 shorter events, 0.2 us)
Async XLA Ops:
  0.6 11.1 %copy-start.8 = (bf16[32,256]{1,0:T(8,128)(2,1)S(1)}, bf16[32,256]{1,0:T(8,128)(2,1)}, u32[]{:S(2)}) copy-start(bf16[32,256]{1,0:T(8,128)(2,1)} %param.10) | copy-start | bytes 49156
  0.6 15.6 %copy-start.2 = (bf16[1024,256]{1,0:T(8,128)(2,1)S(1)}, bf16[1024,256]{1,0:T(8,128)(2,1)}, u32[]{:S(2)}) copy-start(bf16[1024,256]{1,0:T(8,128)(2,1)} %param.13) | copy-start | bytes 1572868
  0.7 15.7 %copy-start.6 = (bf16[1024,256]{1,0:T(8,128)(2,1)S(1)}, bf16[1024,256]{1,0:T(8,128)(2,1)}, u32[]{:S(2)}) copy-start(bf16[1024,256]{1,0:T(8,128)(2,1)} %param.14) | copy-start | bytes 1572868
  1.8 16.7 %copy-start.7 = (f32[32,256]{1,0:T(8,128)S(1)}, f32[32,256]{1,0:T(8,128)}, u32[]{:S(2)}) copy-start(f32[32,256]{1,0:T(8,128)} %param.15) | copy-start | bytes 98308
  2.9 25.6 %collective-permute-start = (bf16[256,2048]{1,0:T(8,128)(2,1)S(1)}, bf16[256,2048]{1,0:T(8,128)(2,1)}, u32[]{:S(2)}, u32[]{:S(2)}) collective-permute-start(bf16[256,2048]{1,0:T(8,128)(2,1)S(1)} %constant_dynamic-update-slice_fusion), channel_id=1, source_target_pairs={{0,16},{16,0},{1,17},{17,1},{2,18},{18,2},{3,19},{19,3},{4,20},{20... | collective-permute-start | bytes 3145736 | tf_op jit(solution)/shard_map/ppermute | solution.py:60
  12.5 15.6 %all-to-all-start.6 = ((bf16[32,16,256]{2,1,0:T(8,128)(2,1)}), bf16[32,16,256]{2,1,0:T(8,128)(2,1)S(1)}, u32[]{:S(2)}, u32[]{:S(2)}) async-start(bf16[32,16,256]{2,1,0:T(8,128)(2,1)} %bitcast.7), calls=%async_computation.6 | async-start | bytes 524288 | tf_op jit(solution)/shard_map/all_to_all | solution.py:35
  16.4 13.8 %copy-start = (bf16[2048,256]{1,0:T(8,128)(2,1)}, bf16[2048,256]{1,0:T(8,128)(2,1)S(1)}, u32[]{:S(2)}) copy-start(bf16[2048,256]{1,0:T(8,128)(2,1)S(1)} %constant_dynamic-update-slice_fusion.2) | copy-start | bytes 3145732
  16.4 13.9 %collective-permute-start.1 = (bf16[2048,256]{1,0:T(8,128)(2,1)S(1)}, bf16[2048,256]{1,0:T(8,128)(2,1)S(1)}, u32[]{:S(2)}, u32[]{:S(2)}) collective-permute-start(bf16[2048,256]{1,0:T(8,128)(2,1)S(1)} %constant_dynamic-update-slice_fusion.2), channel_id=1, source_target_pairs={{0,16},{16,0},{1,17},{17,1},{2,18},{18,2},{3,19},{19,3},{4,20},{20... | collective-permute-start | bytes 3145736 | tf_op jit(solution)/shard_map/ppermute | solution.py:60
  18.6 11.7 %collective-permute-start.2 = (f32[16,256]{1,0:T(8,128)S(1)}, f32[16,256]{1,0:T(8,128)S(1)}, u32[]{:S(2)}, u32[]{:S(2)}) collective-permute-start(f32[16,256]{1,0:T(8,128)S(1)} %get-tuple-element.31), channel_id=1, source_target_pairs={{0,16},{16,0},{1,17},{17,1},{2,18},{18,2},{3,19},{19,3},{4,20},{20... | collective-permute-start | bytes 49160 | tf_op jit(solution)/shard_map/ppermute | solution.py:60
  30.2 0.6 copy-start.9
  60.5 26.1 %copy-start.1 = (bf16[2048,256]{1,0:T(8,128)(2,1)S(1)}, bf16[2048,256]{1,0:T(8,128)(2,1)}, u32[]{:S(2)}) copy-start(bf16[2048,256]{1,0:T(8,128)(2,1)} %copy-done) | copy-start | bytes 3145732
  87.0 16.7 %copy-start.10 = (f32[16,256]{1,0:T(8,128)S(1)}, f32[16,256]{1,0:T(8,128)}, u32[]{:S(2)}) copy-start(f32[16,256]{1,0:T(8,128)} %copy-done.9) | copy-start | bytes 49156
  87.0 28.9 %copy-start.3 = (bf16[1024,256]{1,0:T(8,128)(2,1)S(1)}, bf16[1024,256]{1,0:T(8,128)(2,1)}, u32[]{:S(2)}) copy-start(bf16[1024,256]{1,0:T(8,128)(2,1)} %param.13) | copy-start | bytes 1572868
  116.0 0.7 copy-start.4
  116.7 22.0 %copy-start.5 = (bf16[16,16,512]{2,1,0:T(8,128)(2,1)S(1)}, bf16[16,16,512]{2,1,0:T(8,128)(2,1)}, u32[]{:S(2)}) copy-start(bf16[16,16,512]{2,1,0:T(8,128)(2,1)} %copy-done.4) | copy-start | bytes 786436
  135.1 16.9 %all-to-all-start.10 = ((bf16[16,16,1024]{2,1,0:T(8,128)(2,1)}), bf16[16,16,1024]{2,1,0:T(8,128)(2,1)S(1)}, u32[]{:S(2)}, u32[]{:S(2)}) async-start(bf16[16,16,1024]{2,1,0:T(8,128)(2,1)} %broadcast_in_dim.31), calls=%async_computation.10 | async-start | bytes 1048576 | tf_op jit(solution)/shard_map/all_to_all | solution.py:35
  139.8 23.0 %collective-permute-start.4 = (bf16[1024,256]{1,0:T(8,128)(2,1)}, bf16[1024,256]{1,0:T(8,128)(2,1)S(1)}, u32[]{:S(2)}, u32[]{:S(2)}) collective-permute-start(bf16[1024,256]{1,0:T(8,128)(2,1)} %convolution_convert_fusion), channel_id=1, source_target_pairs={{0,16},{16,0},{1,17},{17,1},{2,18},{18,2},{3,19},{19,3},{4,20},{20... | collective-permute-start | bytes 1572872 | tf_op jit(solution)/shard_map/ppermute | solution.py:60
  152.3 12.1 %collective-permute-start.3 = (bf16[256,1024]{1,0:T(8,128)(2,1)S(1)}, bf16[256,1024]{1,0:T(8,128)(2,1)S(1)}, u32[]{:S(2)}, u32[]{:S(2)}) collective-permute-start(bf16[256,1024]{1,0:T(8,128)(2,1)S(1)} %convolution_convert_fusion.1), channel_id=1, source_target_pairs={{0,16},{16,0},{1,17},{17,1},{2,18},{18,2},{3,19},{19,3},{4,20},{20... | collective-permute-start | bytes 1572872 | tf_op jit(solution)/shard_map/ppermute | solution.py:60

commit v4 on v3

v4 whole, which is shorter than its diff:
```python
import math

import jax
import jax.numpy as jnp
from jax import lax
from jax.experimental import pallas as pl
from jax.experimental.pallas import tpu as pltpu
from jax.sharding import Mesh
from jax.sharding import PartitionSpec as P

gelu_scale = math.sqrt(2.0 / math.pi)
ROWS = ("x", "zh")
TENSOR = ("y", "zl")
SWAP = [(0, 1), (1, 0)]


def gelu_pair(hidden):
    argument = gelu_scale * (hidden + 0.044715 * hidden * hidden * hidden)
    hyper = jnp.tanh(argument)
    values = 0.5 * hidden * (1.0 + hyper)
    derivative = 0.5 * (1.0 + hyper) + 0.5 * hidden * (1.0 - hyper * hyper) * gelu_scale * (
        1.0 + 3.0 * 0.044715 * hidden * hidden
    )
    return (values, derivative)


def dot(left_side, right_side, left_dim=1, right_dim=0):
    return lax.dot_general(
        left_side,
        right_side,
        (((left_dim,), (right_dim,)), ((), ())),
        preferred_element_type=jnp.float32,
    )


def exchange(pieces, axes):
    return lax.all_to_all(pieces, axes, split_axis=0, concat_axis=0, tiled=True)


IN_VMEM = pl.BlockSpec(memory_space=pltpu.VMEM)


def kernel_call(kernel, results, operands, flops):
    moved_bytes = sum(x.size * x.dtype.itemsize for x in (*results, *operands))
    return pl.pallas_call(
        kernel,
        out_shape=results,
        in_specs=[IN_VMEM] * len(operands),
        out_specs=[IN_VMEM] * len(results),
        compiler_params=pltpu.CompilerParams(vmem_limit_bytes=16 * 2**20),
        cost_estimate=pl.CostEstimate(flops=flops, bytes_accessed=moved_bytes, transcendentals=0),
    )(*operands)


def far_products_kernel(far_ref, in_far_ref, slope_far_ref, preact_ref, tangent_ref, result_ref):
    hidden = in_far_ref.shape[1]
    far = far_ref[...]
    preact = preact_ref[...] + dot(far, in_far_ref[...])
    result_ref[:, :hidden] = preact.astype(result_ref.dtype)
    tangent = tangent_ref[...] + dot(far, slope_far_ref[...])
    result_ref[:, hidden:] = tangent.astype(result_ref.dtype)


def both_products_kernel(both_ref, out_ref, turn_ref, out_far_ref, turn_far_ref, result_ref):
    hidden, width = out_ref.shape
    moved, active = both_ref[:, :hidden], both_ref[:, hidden:]
    own = dot(moved, out_ref[...]) + dot(active, turn_ref[...])
    result_ref[:, :width] = own.astype(result_ref.dtype)
    far = dot(moved, out_far_ref[...]) + dot(active, turn_far_ref[...])
    result_ref[:, width:] = far.astype(result_ref.dtype)


def sum_pieces(pieces_ref):
    return jnp.sum(pieces_ref[...].astype(jnp.float32), axis=0)


def partial_sum_kernel(pieces_ref, result_ref):
    result_ref[...] = sum_pieces(pieces_ref).astype(result_ref.dtype)


def gelu_kernel(pieces_ref, copies_ref, derivative_ref):
    total = sum_pieces(pieces_ref)
    hidden = derivative_ref.shape[1]
    values, derivative = gelu_pair(total[:, :hidden])
    derivative_ref[...] = derivative
    moved = (derivative * total[:, hidden:]).astype(copies_ref.dtype)
    active = values.astype(copies_ref.dtype)
    for n in range(copies_ref.shape[0]):
        copies_ref[n, :, :hidden] = moved
        copies_ref[n, :, hidden:] = active


def cotangent_kernel(pieces_ref, curvature_ref, curvature_far_ref, copies_ref):
    count, share, _ = pieces_ref.shape
    width = curvature_ref.shape[1]
    rows = pl.ds(pl.multiple_of(lax.axis_index("c") * share, share), share)
    total = sum_pieces(pieces_ref)
    own = (curvature_ref[rows, :] * total[:, :width]).astype(copies_ref.dtype)
    far = (curvature_far_ref[rows, :] * total[:, width:]).astype(copies_ref.dtype)
    for n in range(count):
        copies_ref[n, :, :width] = own
        copies_ref[n, :, width:] = far


def hidden_grad_kernel(pieces_ref, derivative_ref, copies_ref):
    grad = (sum_pieces(pieces_ref) * derivative_ref[...]).astype(copies_ref.dtype)
    for n in range(copies_ref.shape[0]):
        copies_ref[n] = grad


def apply_gelu(pieces, count, share):
    hidden = pieces.shape[1] // 2
    pieces = pieces.reshape(-1, share, 2 * hidden)
    results = [
        jax.ShapeDtypeStruct((count, share, 2 * hidden), jnp.bfloat16),
        jax.ShapeDtypeStruct((share, hidden), jnp.float32),
    ]
    copies, derivative = kernel_call(gelu_kernel, results, (pieces,), pieces.size)
    return copies.reshape(-1, 2 * hidden), derivative


def staged_then_direct(joined, share):
    pieces = exchange(joined, ("x",)).reshape(4, -1, joined.shape[1])
    results = [jax.ShapeDtypeStruct(pieces.shape[1:], jnp.bfloat16)]
    (partial,) = kernel_call(partial_sum_kernel, results, (pieces,), pieces.size)
    copies, derivative = apply_gelu(exchange(partial, ("zh",)), 16, share)
    return exchange(copies, ROWS), derivative


def direct_then_staged(joined, share):
    copies, derivative = apply_gelu(exchange(joined, ROWS), 4, share)
    block = exchange(copies, ("zh",))
    copies = jnp.broadcast_to(block[None], (4,) + block.shape).reshape(-1, block.shape[1])
    return exchange(copies, ("x",)), derivative


def swap_cores(block):
    return lax.ppermute(block, "c", SWAP)


def on_device(tokens, weight_in, tangent_in, weight_out, tangent_out, curvature):
    core = lax.axis_index("c")
    hidden = weight_in.shape[1]
    features = tokens.shape[1]
    share = tokens.shape[0] // 2

    halves = tokens.reshape(2, 1, share, features)
    copies = jnp.broadcast_to(halves, (2, lax.axis_size(TENSOR), share, features))
    arrived = exchange(copies.reshape(-1, features), ("c",) + TENSOR).reshape(2, -1, features)
    tokens_own = lax.dynamic_index_in_dim(arrived, core, 0, keepdims=False)
    tokens_far = lax.dynamic_index_in_dim(arrived, 1 - core, 0, keepdims=False)
    in_far, slope_far = swap_cores(weight_in), swap_cores(tangent_in)
    out_far, turn_far = swap_cores(weight_out), swap_cores(tangent_out)
    curvature_far = swap_cores(curvature)

    rows = arrived.shape[1]
    flops = 4 * rows * features * hidden
    preact, tangent = dot(tokens_own, weight_in), dot(tokens_own, tangent_in)
    (joined,) = kernel_call(
        far_products_kernel,
        [jax.ShapeDtypeStruct((rows, 2 * hidden), jnp.bfloat16)],
        (tokens_far, in_far, slope_far, preact, tangent),
        flops,
    )
    joined, out_far, turn_far, curvature_far = lax.optimization_barrier(
        (joined, out_far, turn_far, curvature_far)
    )
    both, derivative = lax.cond(
        core == 1,
        lambda j: staged_then_direct(j, share),
        lambda j: direct_then_staged(j, share),
        joined,
    )
    active = both[:, hidden:]

    (output_tangent,) = kernel_call(
        both_products_kernel,
        [jax.ShapeDtypeStruct((rows, 2 * features), jnp.bfloat16)],
        (both, weight_out, tangent_out, out_far, turn_far),
        2 * flops,
    )
    pieces = exchange(output_tangent, TENSOR).reshape(-1, share, 2 * features)
    (copies,) = kernel_call(
        cotangent_kernel,
        [jax.ShapeDtypeStruct(pieces.shape, jnp.bfloat16)],
        (pieces, curvature, curvature_far),
        pieces.size,
    )
    cotangent = exchange(copies.reshape(rows, 2 * features), TENSOR)
    cotangent_own, cotangent_far = cotangent[:, :features], cotangent[:, features:]

    backward = dot(cotangent_own, weight_out, 1, 1) + dot(cotangent_far, out_far, 1, 1)
    pieces = exchange(backward.astype(jnp.bfloat16), ROWS).reshape(-1, share, hidden)
    far_out = swap_cores(dot(active, cotangent_far, 0, 0).astype(jnp.bfloat16))
    product_out = dot(active, cotangent_own, 0, 0) + far_out.astype(jnp.float32)

    (copies,) = kernel_call(
        hidden_grad_kernel,
        [jax.ShapeDtypeStruct(pieces.shape, jnp.bfloat16)],
        (pieces, derivative),
        pieces.size,
    )
    hidden_grad = exchange(copies.reshape(rows, hidden), ROWS)
    product_out = product_out.astype(jnp.bfloat16)
    hidden_grad, product_out = lax.optimization_barrier((hidden_grad, product_out))
    far_in = swap_cores(dot(tokens_far, hidden_grad, 0, 0).astype(jnp.bfloat16))
    own_in = lax.optimization_barrier(dot(tokens_own, hidden_grad, 0, 0))
    product_in = (own_in + far_in.astype(jnp.float32)).astype(jnp.bfloat16)
    return (product_in, product_out)


def solution(mesh):
    fine = Mesh(mesh.devices.reshape(4, 4, 2, 8, 2), ("zh", "x", "c", "y", "zl"))
    by_dp = ("zh", "x", "c")
    return jax.shard_map(
        on_device,
        mesh=fine,
        in_specs=(
            P(TENSOR, by_dp),
            P(by_dp, TENSOR),
            P(by_dp, TENSOR),
            P(TENSOR, by_dp),
            P(TENSOR, by_dp),
            P(TENSOR, by_dp),
        ),
        out_specs=(P(by_dp, TENSOR), P(TENSOR, by_dp)),
        check_vma=False,
    )
```

time: 166 us -> 163 us (0.982)
  waiting for transfers between devices: 10.2 us -> 5.29 us
  local copies, waits for them, and re-layouts: 5.64 us -> 1.8 us
  starting transfers between devices: 40.6 us -> 44.4 us
  matrix products: 7.41 us -> 4.51 us
  blocking collectives: 99.6 us -> 102 us
  Pallas kernels: 0 us -> 2.35 us
    all_to_all x2, waiting for transfers between devices: 9.81 us -> 2.58 us  [exchange(): return lax.all_to_all(pieces, axes, split_axis=0, concat_axis=0, tiled=True)]
    all_to_all x2, starting transfers between devices: 7.38 us -> 14.3 us  [exchange(): return lax.all_to_all(pieces, axes, split_axis=0, concat_axis=0, tiled=True)]
    ppermute x5 -> x7, starting transfers between devices: 33.2 us -> 30.1 us  [swap_cores(): return lax.ppermute(block, 'c', SWAP)]
    dot_general x10 -> x8, matrix products: 7.41 us -> 4.51 us  [dot(): lax.dot_general(left_side, right_side, (((left_dim,), (right_dim,)), ((),...]
    pallas_call x0 -> x6, Pallas kernels: none -> 2.35 us  [kernel_call(): pl.pallas_call(kernel, out_shape=results, in_specs=[IN_VMEM] * len(operan...]
    ppermute x5 -> x7, waiting for transfers between devices: 0.36 us -> 2.71 us  [swap_cores(): return lax.ppermute(block, 'c', SWAP)]
    all_to_all x6, blocking collectives: 99.6 us -> 102 us  [exchange(): return lax.all_to_all(pieces, axes, split_axis=0, concat_axis=0, tiled=True)]
    broadcast_in_dim x4 -> x0, local copies, waits for them, and re-layouts: 1.93 us -> none  [gather_rows(): copies = jnp.broadcast_to(block[None], (count,) + block.shape)]
  transfers between devices with their start and end apart: 7 -> 9, of which waited for: 3 -> 4; matrix products, arithmetic and copies ran while one was open for 3% -> 2% of each run, Pallas kernels for 0% -> 0%
where the time goes in v4:
time: 163 us; the launch traced here: 162 us
  blocking collectives  102 us (63%)
  starting transfers between devices  44.4 us (27%)
  waiting for transfers between devices  5.29 us (3%)
  matrix products  4.51 us (3%)
  Pallas kernels  2.35 us (1%)
  local copies, waits for them, and re-layouts  1.8 us (1%)
    all_to_all x6, blocking collectives, exchange(): return lax.all_to_all(pieces, axes, split_axis=0, concat_axis=0, tiled=True)  102 us
    ppermute x7, starting transfers between devices, swap_cores(): return lax.ppermute(block, 'c', SWAP)  30.1 us
    all_to_all x2, starting transfers between devices, exchange(): return lax.all_to_all(pieces, axes, split_axis=0, concat_axis=0, tiled=True)  14.3 us
    dot_general x8, matrix products, dot(): lax.dot_general(left_side, right_side, (((left_dim,), (right_dim,)), ((),...  4.51 us
  transfers between devices with their start and end apart: 9, of which 4 were waited for; matrix products, arithmetic and copies ran while one was open for 2% of the time, Pallas kernels for 0%

profile of v4, /device:TPU:1, one launch (start us, length us, event | category | flops | bytes accessed | tf_op | source)
XLA Modules:
  0.0 162.0 jit_solution(667268762711652590)
XLA Ops:
  0.6 0.0 copy-start
  0.6 1.5 broadcast_in_dim.16
  2.1 10.7 %all-to-all-start.6 = ((bf16[32,16,256]{2,1,0:T(8,128)(2,1)}), bf16[32,16,256]{2,1,0:T(8,128)(2,1)S(1)}, u32[]{:S(2)}, u32[]{:S(2)}) async-start(bf16[32,16,256]{2,1,0:T(8,128)(2,1)} %bitcast.7), calls=%async_computation.6 | async-start | bytes 524288 | tf_op jit(solution)/shard_map/all_to_all | solution.py:37
  12.8 2.1 %collective-permute-start = (bf16[256,1024]{1,0:T(8,128)(2,1)}, bf16[256,1024]{1,0:T(8,128)(2,1)S(1)}, u32[]{:S(2)}, u32[]{:S(2)}) collective-permute-start(bf16[256,1024]{1,0:T(8,128)(2,1)} %param.9), channel_id=1, source_target_pairs={{0,16},{16,0},{1,17},{17,1},{2,18},{18,2},{3,19},{19,3},{4,20},{20... | collective-permute-start | bytes 1572872 | tf_op jit(solution)/shard_map/ppermute | solution.py:138
  15.0 2.2 %collective-permute-start.1 = (bf16[256,1024]{1,0:T(8,128)(2,1)}, bf16[256,1024]{1,0:T(8,128)(2,1)S(1)}, u32[]{:S(2)}, u32[]{:S(2)}) collective-permute-start(bf16[256,1024]{1,0:T(8,128)(2,1)} %param.10), channel_id=1, source_target_pairs={{0,16},{16,0},{1,17},{17,1},{2,18},{18,2},{3,19},{19,3},{4,20},{20... | collective-permute-start | bytes 1572872 | tf_op jit(solution)/shard_map/ppermute | solution.py:138
  17.2 0.0 copy-done
  17.2 2.1 %collective-permute-start.2 = (bf16[1024,256]{1,0:T(8,128)(2,1)S(1)}, bf16[1024,256]{1,0:T(8,128)(2,1)S(1)}, u32[]{:S(2)}, u32[]{:S(2)}) collective-permute-start(bf16[1024,256]{1,0:T(8,128)(2,1)S(1)} %copy-done), channel_id=1, source_target_pairs={{0,16},{16,0},{1,17},{17,1},{2,18},{18,2},{3,19},{19,3},{4,20},{20... | collective-permute-start | bytes 1572872 | tf_op jit(solution)/shard_map/ppermute | solution.py:138
  19.4 2.2 %collective-permute-start.3 = (bf16[1024,256]{1,0:T(8,128)(2,1)}, bf16[1024,256]{1,0:T(8,128)(2,1)S(1)}, u32[]{:S(2)}, u32[]{:S(2)}) collective-permute-start(bf16[1024,256]{1,0:T(8,128)(2,1)} %turn_ref.1), channel_id=1, source_target_pairs={{0,16},{16,0},{1,17},{17,1},{2,18},{18,2},{3,19},{19,3},{4,20},{20... | collective-permute-start | bytes 1572872 | tf_op jit(solution)/shard_map/ppermute | solution.py:138
  21.6 0.0 copy-done.2
  21.6 2.1 %collective-permute-start.4 = (f32[32,256]{1,0:T(8,128)S(1)}, f32[32,256]{1,0:T(8,128)S(1)}, u32[]{:S(2)}, u32[]{:S(2)}) collective-permute-start(f32[32,256]{1,0:T(8,128)S(1)} %copy-done.2), channel_id=1, source_target_pairs={{0,16},{16,0},{1,17},{17,1},{2,18},{18,2},{3,19},{19,3},{4,20},{20... | collective-permute-start | bytes 98312 | tf_op jit(solution)/shard_map/ppermute | solution.py:138
  23.7 0.9 all-to-all-done.6
  24.6 1.4 fusion.10.preact_ref
  26.0 0.0 copy-done.5
  26.0 0.3 fusion.8.tangent_ref
  26.4 0.0 collective-permute-done.in_far_ref
  26.4 0.0 collective-permute-done.1.slope_far_ref
  26.4 0.4 shard_map.77
  26.9 0.0 copy-start.1
  26.9 0.0 collective-permute-done.4.curvature_far_ref
  26.9 0.0 collective-permute-done.2.out_far_ref
  26.9 0.0 collective-permute-done.3.turn_far_ref
  26.9 55.7 %conditional.1 = (bf16[256,2048]{1,0:T(8,128)(2,1)S(1)}, f32[16,1024]{1,0:T(8,128)S(1)}) conditional(s32[]{:T(128)} %convert_element_type.24, bf16[256,2048]{1,0:T(8,128)(2,1)S(1)} %shard_map.77, bf16[256,2048]{1,0:T(8,128)(2,1)S(1)} %shard_map.77), branch_computations={%region_0.1_spmd, %region_1.2_spmd} | conditional | flops 655360 | bytes 7405584 | solution.py:168
  26.9 13.7 %all_to_all.88.pieces_ref = bf16[4,64,2048]{2,1,0:T(8,128)(2,1)S(1)} all-to-all(bf16[4,64,2048]{2,1,0:T(8,128)(2,1)S(1)} %bitcast.32), channel_id=1, replica_groups=mesh['zh'=4,'x'=4,'c'=2,'y'=8,'zl'=2] {'x'}, dimensions={0} | all-to-all | bytes 2097152 | tf_op jit(solution)/shard_map/cond/branch_1_fun/all_to_all | solution.py:37
  40.6 0.1 branch_1_fun.2
  40.7 21.0 %all_to_all.89.pieces_ref = bf16[4,16,2048]{2,1,0:T(8,128)(2,1)S(1)} all-to-all(bf16[4,16,2048]{2,1,0:T(8,128)(2,1)S(1)} %bitcast.29), channel_id=1, replica_groups=mesh['zh'=4,'x'=4,'c'=2,'y'=8,'zl'=2] {'zh'}, dimensions={0} | all-to-all | bytes 524288 | tf_op jit(solution)/shard_map/cond/branch_1_fun/all_to_all | solution.py:37
  61.7 0.1 branch_1_fun.3
  61.9 20.7 %all_to_all.90 = bf16[16,16,2048]{2,1,0:T(8,128)(2,1)S(1)} all-to-all(bf16[16,16,2048]{2,1,0:T(8,128)(2,1)S(1)} %get-tuple-element.10), channel_id=1, replica_groups=mesh['zh'=4,'x'=4,'c'=2,'y'=8,'zl'=2] {'x','zh'}, dimensions={0} | all-to-all | bytes 2097152 | tf_op jit(solution)/shard_map/cond/branch_1_fun/all_to_all | solution.py:37
  82.6 0.0 copy-done.1
  82.6 0.7 shard_map.78
  83.3 0.3 copy-done.3
  83.6 18.1 %all_to_all.91.pieces_ref = bf16[16,16,512]{2,1,0:T(8,128)(2,1)S(1)} all-to-all(bf16[16,16,512]{2,1,0:T(8,128)(2,1)S(1)} %bitcast.30), channel_id=1, replica_groups=mesh['zh'=4,'x'=4,'c'=2,'y'=8,'zl'=2] {'y','zl'}, dimensions={0} | all-to-all | bytes 524288 | tf_op jit(solution)/shard_map/all_to_all | solution.py:37
  101.7 12.2 %all_to_all.92 = bf16[16,16,512]{2,1,0:T(8,128)(2,1)S(1)} all-to-all(bf16[16,16,512]{2,1,0:T(8,128)(2,1)S(1)} %shard_map.79), channel_id=1, replica_groups=mesh['zh'=4,'x'=4,'c'=2,'y'=8,'zl'=2] {'y','zl'}, dimensions={0} | all-to-all | bytes 524288 | tf_op jit(solution)/shard_map/all_to_all | solution.py:37
  113.9 0.3 fusion.15
  114.2 0.3 fusion
  114.6 16.2 %all_to_all.93.pieces_ref = bf16[16,16,1024]{2,1,0:T(8,128)(2,1)S(1)} all-to-all(bf16[16,16,1024]{2,1,0:T(8,128)(2,1)S(1)} %bitcast.41), channel_id=1, replica_groups=mesh['zh'=4,'x'=4,'c'=2,'y'=8,'zl'=2] {'x','zh'}, dimensions={0} | all-to-all | bytes 1048576 | tf_op jit(solution)/shard_map/all_to_all | solution.py:37
  130.8 0.9 shard_map.80
  131.7 3.6 %all-to-all-start.10 = ((bf16[16,16,1024]{2,1,0:T(8,128)(2,1)}), bf16[16,16,1024]{2,1,0:T(8,128)(2,1)S(1)}, u32[]{:S(2)}, u32[]{:S(2)}) async-start(bf16[16,16,1024]{2,1,0:T(8,128)(2,1)} %shard_map.80), calls=%async_computation.10 | async-start | bytes 1048576 | tf_op jit(solution)/shard_map/all_to_all | solution.py:37
  135.2 0.0 copy-done.4
  135.2 0.4 convolution_convert_fusion.1
  135.6 8.8 %collective-permute-start.5 = (bf16[1024,256]{1,0:T(8,128)(2,1)S(1)}, bf16[1024,256]{1,0:T(8,128)(2,1)S(1)}, u32[]{:S(2)}, u32[]{:S(2)}) collective-permute-start(bf16[1024,256]{1,0:T(8,128)(2,1)S(1)} %convolution_convert_fusion.1), channel_id=1, source_target_pairs={{0,16},{16,0},{1,17},{17,1},{2,18},{18,2},{3,19},{19,3},{4,20},{20... | collective-permute-start | bytes 1572872 | tf_op jit(solution)/shard_map/ppermute | solution.py:138
  144.4 1.5 collective-permute-done.5
  145.9 1.1 add_convert_fusion.1
  147.1 1.7 %all-to-all-done.10 = bf16[16,16,1024]{2,1,0:T(8,128)(2,1)S(1)} async-done(((bf16[16,16,1024]{2,1,0:T(8,128)(2,1)}), bf16[16,16,1024]{2,1,0:T(8,128)(2,1)S(1)}, u32[]{:S(2)}, u32[]{:S(2)}) %all-to-all-start.10) | async-done | bytes 524320 | tf_op jit(solution)/shard_map/all_to_all | solution.py:37
  148.7 0.3 convolution_convert_fusion
  149.1 10.5 %collective-permute-start.6 = (bf16[256,1024]{1,0:T(8,128)(2,1)S(1)}, bf16[256,1024]{1,0:T(8,128)(2,1)S(1)}, u32[]{:S(2)}, u32[]{:S(2)}) collective-permute-start(bf16[256,1024]{1,0:T(8,128)(2,1)S(1)} %convolution_convert_fusion), channel_id=1, source_target_pairs={{0,16},{16,0},{1,17},{17,1},{2,18},{18,2},{3,19},{19,3},{4,20},{20... | collective-permute-start | bytes 1572872 | tf_op jit(solution)/shard_map/ppermute | solution.py:138
  159.6 0.3 fusion.6
  159.9 1.2 collective-permute-done.6
  161.1 0.9 add_convert_fusion
  (6 shorter events, 0.1 us)
Async XLA Ops:
  0.6 16.6 %copy-start = (bf16[1024,256]{1,0:T(8,128)(2,1)S(1)}, bf16[1024,256]{1,0:T(8,128)(2,1)}, u32[]{:S(2)}) copy-start(bf16[1024,256]{1,0:T(8,128)(2,1)} %out_ref.1) | copy-start | bytes 1572868
  2.1 19.4 %copy-start.2 = (f32[32,256]{1,0:T(8,128)S(1)}, f32[32,256]{1,0:T(8,128)}, u32[]{:S(2)}) copy-start(f32[32,256]{1,0:T(8,128)} %curvature_ref.1) | copy-start | bytes 98308
  2.1 22.5 %all-to-all-start.6 = ((bf16[32,16,256]{2,1,0:T(8,128)(2,1)}), bf16[32,16,256]{2,1,0:T(8,128)(2,1)S(1)}, u32[]{:S(2)}, u32[]{:S(2)}) async-start(bf16[32,16,256]{2,1,0:T(8,128)(2,1)} %bitcast.7), calls=%async_computation.6 | async-start | bytes 524288 | tf_op jit(solution)/shard_map/all_to_all | solution.py:37
  12.8 13.5 %collective-permute-start = (bf16[256,1024]{1,0:T(8,128)(2,1)}, bf16[256,1024]{1,0:T(8,128)(2,1)S(1)}, u32[]{:S(2)}, u32[]{:S(2)}) collective-permute-start(bf16[256,1024]{1,0:T(8,128)(2,1)} %param.9), channel_id=1, source_target_pairs={{0,16},{16,0},{1,17},{17,1},{2,18},{18,2},{3,19},{19,3},{4,20},{20... | collective-permute-start | bytes 1572872 | tf_op jit(solution)/shard_map/ppermute | solution.py:138
  15.0 11.4 %collective-permute-start.1 = (bf16[256,1024]{1,0:T(8,128)(2,1)}, bf16[256,1024]{1,0:T(8,128)(2,1)S(1)}, u32[]{:S(2)}, u32[]{:S(2)}) collective-permute-start(bf16[256,1024]{1,0:T(8,128)(2,1)} %param.10), channel_id=1, source_target_pairs={{0,16},{16,0},{1,17},{17,1},{2,18},{18,2},{3,19},{19,3},{4,20},{20... | collective-permute-start | bytes 1572872 | tf_op jit(solution)/shard_map/ppermute | solution.py:138
  17.2 9.7 %collective-permute-start.2 = (bf16[1024,256]{1,0:T(8,128)(2,1)S(1)}, bf16[1024,256]{1,0:T(8,128)(2,1)S(1)}, u32[]{:S(2)}, u32[]{:S(2)}) collective-permute-start(bf16[1024,256]{1,0:T(8,128)(2,1)S(1)} %copy-done), channel_id=1, source_target_pairs={{0,16},{16,0},{1,17},{17,1},{2,18},{18,2},{3,19},{19,3},{4,20},{20... | collective-permute-start | bytes 1572872 | tf_op jit(solution)/shard_map/ppermute | solution.py:138
  19.4 7.5 %collective-permute-start.3 = (bf16[1024,256]{1,0:T(8,128)(2,1)}, bf16[1024,256]{1,0:T(8,128)(2,1)S(1)}, u32[]{:S(2)}, u32[]{:S(2)}) collective-permute-start(bf16[1024,256]{1,0:T(8,128)(2,1)} %turn_ref.1), channel_id=1, source_target_pairs={{0,16},{16,0},{1,17},{17,1},{2,18},{18,2},{3,19},{19,3},{4,20},{20... | collective-permute-start | bytes 1572872 | tf_op jit(solution)/shard_map/ppermute | solution.py:138
  21.6 5.3 %collective-permute-start.4 = (f32[32,256]{1,0:T(8,128)S(1)}, f32[32,256]{1,0:T(8,128)S(1)}, u32[]{:S(2)}, u32[]{:S(2)}) collective-permute-start(f32[32,256]{1,0:T(8,128)S(1)} %copy-done.2), channel_id=1, source_target_pairs={{0,16},{16,0},{1,17},{17,1},{2,18},{18,2},{3,19},{19,3},{4,20},{20... | collective-permute-start | bytes 98312 | tf_op jit(solution)/shard_map/ppermute | solution.py:138
  24.6 1.4 copy-start.5
  26.9 55.7 %copy-start.1 = (bf16[1024,256]{1,0:T(8,128)(2,1)S(1)}, bf16[1024,256]{1,0:T(8,128)(2,1)}, u32[]{:S(2)}) copy-start(bf16[1024,256]{1,0:T(8,128)(2,1)} %turn_ref.1) | copy-start | bytes 1572868
  82.6 1.0 copy-start.3
  130.8 4.5 %copy-start.4 = (bf16[256,2048]{1,0:T(8,128)(2,1)S(1)}, bf16[256,2048]{1,0:T(8,128)(2,1)}, u32[]{:S(2)}) copy-start(bf16[256,2048]{1,0:T(8,128)(2,1)} %copy-done.3) | copy-start | bytes 3145732
  131.7 17.1 %all-to-all-start.10 = ((bf16[16,16,1024]{2,1,0:T(8,128)(2,1)}), bf16[16,16,1024]{2,1,0:T(8,128)(2,1)S(1)}, u32[]{:S(2)}, u32[]{:S(2)}) async-start(bf16[16,16,1024]{2,1,0:T(8,128)(2,1)} %shard_map.80), calls=%async_computation.10 | async-start | bytes 1048576 | tf_op jit(solution)/shard_map/all_to_all | solution.py:37
  135.6 10.3 %collective-permute-start.5 = (bf16[1024,256]{1,0:T(8,128)(2,1)S(1)}, bf16[1024,256]{1,0:T(8,128)(2,1)S(1)}, u32[]{:S(2)}, u32[]{:S(2)}) collective-permute-start(bf16[1024,256]{1,0:T(8,128)(2,1)S(1)} %convolution_convert_fusion.1), channel_id=1, source_target_pairs={{0,16},{16,0},{1,17},{17,1},{2,18},{18,2},{3,19},{19,3},{4,20},{20... | collective-permute-start | bytes 1572872 | tf_op jit(solution)/shard_map/ppermute | solution.py:138
  149.1 12.0 %collective-permute-start.6 = (bf16[256,1024]{1,0:T(8,128)(2,1)S(1)}, bf16[256,1024]{1,0:T(8,128)(2,1)S(1)}, u32[]{:S(2)}, u32[]{:S(2)}) collective-permute-start(bf16[256,1024]{1,0:T(8,128)(2,1)S(1)} %convolution_convert_fusion), channel_id=1, source_target_pairs={{0,16},{16,0},{1,17},{17,1},{2,18},{18,2},{3,19},{19,3},{4,20},{20... | collective-permute-start | bytes 1572872 | tf_op jit(solution)/shard_map/ppermute | solution.py:138

commit v5 on v4

--- a/solution.py
+++ b/solution.py
@@ -166,7 +166,7 @@
         (joined, out_far, turn_far, curvature_far)
     )
     both, derivative = lax.cond(
-        core == 1,
+        core != lax.axis_index("zl"),
         lambda j: staged_then_direct(j, share),
         lambda j: direct_then_staged(j, share),
         joined,

time: 163 us -> 162 us (level)
  starting transfers between devices: 44.4 us -> 40.7 us
  blocking collectives: 102 us -> 104 us
    ppermute x7, starting transfers between devices: 30.1 us -> 26.2 us  [swap_cores(): return lax.ppermute(block, 'c', SWAP)]
    all_to_all x6, blocking collectives: 102 us -> 104 us  [exchange(): return lax.all_to_all(pieces, axes, split_axis=0, concat_axis=0, tiled=True)]
where the time goes in v5:
time: 162 us; the launch traced here: 161 us
  blocking collectives  104 us (64%)
  starting transfers between devices  40.7 us (25%)
  waiting for transfers between devices  6.51 us (4%)
  matrix products  4.51 us (3%)
  Pallas kernels  2.35 us (1%)
  local copies, waits for them, and re-layouts  1.8 us (1%)
    all_to_all x6, blocking collectives, exchange(): return lax.all_to_all(pieces, axes, split_axis=0, concat_axis=0, tiled=True)  104 us
    ppermute x7, starting transfers between devices, swap_cores(): return lax.ppermute(block, 'c', SWAP)  26.2 us
    all_to_all x2, starting transfers between devices, exchange(): return lax.all_to_all(pieces, axes, split_axis=0, concat_axis=0, tiled=True)  14.4 us
    dot_general x8, matrix products, dot(): lax.dot_general(left_side, right_side, (((left_dim,), (right_dim,)), ((),...  4.51 us
    all_to_all x2, waiting for transfers between devices, exchange(): return lax.all_to_all(pieces, axes, split_axis=0, concat_axis=0, tiled=True)  3.8 us
  transfers between devices with their start and end apart: 9, of which 4 were waited for; matrix products, arithmetic and copies ran while one was open for 2% of the time, Pallas kernels for 0%

profile of v5, /device:TPU:1, one launch (start us, length us, event | category | flops | bytes accessed | tf_op | source)
XLA Modules:
  0.0 161.2 jit_solution(14719146162292537765)
XLA Ops:
  0.6 0.0 copy-start
  0.6 1.5 broadcast_in_dim.16
  2.1 10.7 %all-to-all-start.6 = ((bf16[32,16,256]{2,1,0:T(8,128)(2,1)}), bf16[32,16,256]{2,1,0:T(8,128)(2,1)S(1)}, u32[]{:S(2)}, u32[]{:S(2)}) async-start(bf16[32,16,256]{2,1,0:T(8,128)(2,1)} %bitcast.7), calls=%async_computation.6 | async-start | bytes 524288 | tf_op jit(solution)/shard_map/all_to_all | solution.py:37
  12.8 2.1 %collective-permute-start = (bf16[256,1024]{1,0:T(8,128)(2,1)}, bf16[256,1024]{1,0:T(8,128)(2,1)S(1)}, u32[]{:S(2)}, u32[]{:S(2)}) collective-permute-start(bf16[256,1024]{1,0:T(8,128)(2,1)} %param.9), channel_id=1, source_target_pairs={{0,16},{16,0},{1,17},{17,1},{2,18},{18,2},{3,19},{19,3},{4,20},{20... | collective-permute-start | bytes 1572872 | tf_op jit(solution)/shard_map/ppermute | solution.py:138
  15.0 2.2 %collective-permute-start.1 = (bf16[256,1024]{1,0:T(8,128)(2,1)}, bf16[256,1024]{1,0:T(8,128)(2,1)S(1)}, u32[]{:S(2)}, u32[]{:S(2)}) collective-permute-start(bf16[256,1024]{1,0:T(8,128)(2,1)} %param.10), channel_id=1, source_target_pairs={{0,16},{16,0},{1,17},{17,1},{2,18},{18,2},{3,19},{19,3},{4,20},{20... | collective-permute-start | bytes 1572872 | tf_op jit(solution)/shard_map/ppermute | solution.py:138
  17.2 0.0 copy-done
  17.2 2.1 %collective-permute-start.2 = (bf16[1024,256]{1,0:T(8,128)(2,1)S(1)}, bf16[1024,256]{1,0:T(8,128)(2,1)S(1)}, u32[]{:S(2)}, u32[]{:S(2)}) collective-permute-start(bf16[1024,256]{1,0:T(8,128)(2,1)S(1)} %copy-done), channel_id=1, source_target_pairs={{0,16},{16,0},{1,17},{17,1},{2,18},{18,2},{3,19},{19,3},{4,20},{20... | collective-permute-start | bytes 1572872 | tf_op jit(solution)/shard_map/ppermute | solution.py:138
  19.4 2.2 %collective-permute-start.3 = (bf16[1024,256]{1,0:T(8,128)(2,1)}, bf16[1024,256]{1,0:T(8,128)(2,1)S(1)}, u32[]{:S(2)}, u32[]{:S(2)}) collective-permute-start(bf16[1024,256]{1,0:T(8,128)(2,1)} %turn_ref.1), channel_id=1, source_target_pairs={{0,16},{16,0},{1,17},{17,1},{2,18},{18,2},{3,19},{19,3},{4,20},{20... | collective-permute-start | bytes 1572872 | tf_op jit(solution)/shard_map/ppermute | solution.py:138
  21.6 0.0 copy-done.2
  21.6 2.1 %collective-permute-start.4 = (f32[32,256]{1,0:T(8,128)S(1)}, f32[32,256]{1,0:T(8,128)S(1)}, u32[]{:S(2)}, u32[]{:S(2)}) collective-permute-start(f32[32,256]{1,0:T(8,128)S(1)} %copy-done.2), channel_id=1, source_target_pairs={{0,16},{16,0},{1,17},{17,1},{2,18},{18,2},{3,19},{19,3},{4,20},{20... | collective-permute-start | bytes 98312 | tf_op jit(solution)/shard_map/ppermute | solution.py:138
  23.7 0.9 all-to-all-done.6
  24.6 1.4 fusion.10.preact_ref
  26.0 0.0 copy-done.5
  26.0 0.3 fusion.8.tangent_ref
  26.4 0.0 collective-permute-done.in_far_ref
  26.4 0.0 collective-permute-done.1.slope_far_ref
  26.4 0.4 shard_map.77
  26.9 0.0 copy-start.1
  26.9 0.0 collective-permute-done.4.curvature_far_ref
  26.9 0.0 collective-permute-done.2.out_far_ref
  26.9 0.0 collective-permute-done.3.turn_far_ref
  26.9 56.0 %conditional.1 = (bf16[256,2048]{1,0:T(8,128)(2,1)S(1)}, f32[16,1024]{1,0:T(8,128)S(1)}) conditional(s32[]{:T(128)} %convert_element_type.24, bf16[256,2048]{1,0:T(8,128)(2,1)S(1)} %shard_map.77, bf16[256,2048]{1,0:T(8,128)(2,1)S(1)} %shard_map.77), branch_computations={%region_0.1_spmd, %region_1.2_spmd} | conditional | flops 655360 | bytes 7405584 | solution.py:168
  26.9 13.7 %all_to_all.88.pieces_ref = bf16[4,64,2048]{2,1,0:T(8,128)(2,1)S(1)} all-to-all(bf16[4,64,2048]{2,1,0:T(8,128)(2,1)S(1)} %bitcast.32), channel_id=1, replica_groups=mesh['zh'=4,'x'=4,'c'=2,'y'=8,'zl'=2] {'x'}, dimensions={0} | all-to-all | bytes 2097152 | tf_op jit(solution)/shard_map/cond/branch_1_fun/all_to_all | solution.py:37
  40.6 0.1 branch_1_fun.2
  40.7 19.6 %all_to_all.89.pieces_ref = bf16[4,16,2048]{2,1,0:T(8,128)(2,1)S(1)} all-to-all(bf16[4,16,2048]{2,1,0:T(8,128)(2,1)S(1)} %bitcast.29), channel_id=1, replica_groups=mesh['zh'=4,'x'=4,'c'=2,'y'=8,'zl'=2] {'zh'}, dimensions={0} | all-to-all | bytes 524288 | tf_op jit(solution)/shard_map/cond/branch_1_fun/all_to_all | solution.py:37
  60.4 0.1 branch_1_fun.3
  60.5 22.4 %all_to_all.90 = bf16[16,16,2048]{2,1,0:T(8,128)(2,1)S(1)} all-to-all(bf16[16,16,2048]{2,1,0:T(8,128)(2,1)S(1)} %get-tuple-element.10), channel_id=1, replica_groups=mesh['zh'=4,'x'=4,'c'=2,'y'=8,'zl'=2] {'x','zh'}, dimensions={0} | all-to-all | bytes 2097152 | tf_op jit(solution)/shard_map/cond/branch_1_fun/all_to_all | solution.py:37
  82.9 0.0 copy-done.1
  82.9 0.7 shard_map.78
  83.6 0.3 copy-done.3
  83.9 18.9 %all_to_all.91.pieces_ref = bf16[16,16,512]{2,1,0:T(8,128)(2,1)S(1)} all-to-all(bf16[16,16,512]{2,1,0:T(8,128)(2,1)S(1)} %bitcast.30), channel_id=1, replica_groups=mesh['zh'=4,'x'=4,'c'=2,'y'=8,'zl'=2] {'y','zl'}, dimensions={0} | all-to-all | bytes 524288 | tf_op jit(solution)/shard_map/all_to_all | solution.py:37
  102.8 12.3 %all_to_all.92 = bf16[16,16,512]{2,1,0:T(8,128)(2,1)S(1)} all-to-all(bf16[16,16,512]{2,1,0:T(8,128)(2,1)S(1)} %shard_map.79), channel_id=1, replica_groups=mesh['zh'=4,'x'=4,'c'=2,'y'=8,'zl'=2] {'y','zl'}, dimensions={0} | all-to-all | bytes 524288 | tf_op jit(solution)/shard_map/all_to_all | solution.py:37
  115.1 0.3 fusion.15
  115.4 0.3 fusion
  115.8 16.7 %all_to_all.93.pieces_ref = bf16[16,16,1024]{2,1,0:T(8,128)(2,1)S(1)} all-to-all(bf16[16,16,1024]{2,1,0:T(8,128)(2,1)S(1)} %bitcast.41), channel_id=1, replica_groups=mesh['zh'=4,'x'=4,'c'=2,'y'=8,'zl'=2] {'x','zh'}, dimensions={0} | all-to-all | bytes 1048576 | tf_op jit(solution)/shard_map/all_to_all | solution.py:37
  132.5 0.9 shard_map.80
  133.4 3.7 %all-to-all-start.10 = ((bf16[16,16,1024]{2,1,0:T(8,128)(2,1)}), bf16[16,16,1024]{2,1,0:T(8,128)(2,1)S(1)}, u32[]{:S(2)}, u32[]{:S(2)}) async-start(bf16[16,16,1024]{2,1,0:T(8,128)(2,1)} %shard_map.80), calls=%async_computation.10 | async-start | bytes 1048576 | tf_op jit(solution)/shard_map/all_to_all | solution.py:37
  137.1 0.0 copy-done.4
  137.1 0.4 convolution_convert_fusion.1
  137.4 7.1 %collective-permute-start.5 = (bf16[1024,256]{1,0:T(8,128)(2,1)S(1)}, bf16[1024,256]{1,0:T(8,128)(2,1)S(1)}, u32[]{:S(2)}, u32[]{:S(2)}) collective-permute-start(bf16[1024,256]{1,0:T(8,128)(2,1)S(1)} %convolution_convert_fusion.1), channel_id=1, source_target_pairs={{0,16},{16,0},{1,17},{17,1},{2,18},{18,2},{3,19},{19,3},{4,20},{20... | collective-permute-start | bytes 1572872 | tf_op jit(solution)/shard_map/ppermute | solution.py:138
  144.6 1.5 collective-permute-done.5
  146.1 1.1 add_convert_fusion.1
  147.2 2.9 %all-to-all-done.10 = bf16[16,16,1024]{2,1,0:T(8,128)(2,1)S(1)} async-done(((bf16[16,16,1024]{2,1,0:T(8,128)(2,1)}), bf16[16,16,1024]{2,1,0:T(8,128)(2,1)S(1)}, u32[]{:S(2)}, u32[]{:S(2)}) %all-to-all-start.10) | async-done | bytes 524320 | tf_op jit(solution)/shard_map/all_to_all | solution.py:37
  150.1 0.3 convolution_convert_fusion
  150.4 8.3 %collective-permute-start.6 = (bf16[256,1024]{1,0:T(8,128)(2,1)S(1)}, bf16[256,1024]{1,0:T(8,128)(2,1)S(1)}, u32[]{:S(2)}, u32[]{:S(2)}) collective-permute-start(bf16[256,1024]{1,0:T(8,128)(2,1)S(1)} %convolution_convert_fusion), channel_id=1, source_target_pairs={{0,16},{16,0},{1,17},{17,1},{2,18},{18,2},{3,19},{19,3},{4,20},{20... | collective-permute-start | bytes 1572872 | tf_op jit(solution)/shard_map/ppermute | solution.py:138
  158.8 0.3 fusion.6
  159.1 1.2 collective-permute-done.6
  160.3 0.9 add_convert_fusion
  (6 shorter events, 0.1 us)
Async XLA Ops:
  0.6 16.6 %copy-start = (bf16[1024,256]{1,0:T(8,128)(2,1)S(1)}, bf16[1024,256]{1,0:T(8,128)(2,1)}, u32[]{:S(2)}) copy-start(bf16[1024,256]{1,0:T(8,128)(2,1)} %out_ref.1) | copy-start | bytes 1572868
  2.1 19.4 %copy-start.2 = (f32[32,256]{1,0:T(8,128)S(1)}, f32[32,256]{1,0:T(8,128)}, u32[]{:S(2)}) copy-start(f32[32,256]{1,0:T(8,128)} %curvature_ref.1) | copy-start | bytes 98308
  2.1 22.5 %all-to-all-start.6 = ((bf16[32,16,256]{2,1,0:T(8,128)(2,1)}), bf16[32,16,256]{2,1,0:T(8,128)(2,1)S(1)}, u32[]{:S(2)}, u32[]{:S(2)}) async-start(bf16[32,16,256]{2,1,0:T(8,128)(2,1)} %bitcast.7), calls=%async_computation.6 | async-start | bytes 524288 | tf_op jit(solution)/shard_map/all_to_all | solution.py:37
  12.8 13.5 %collective-permute-start = (bf16[256,1024]{1,0:T(8,128)(2,1)}, bf16[256,1024]{1,0:T(8,128)(2,1)S(1)}, u32[]{:S(2)}, u32[]{:S(2)}) collective-permute-start(bf16[256,1024]{1,0:T(8,128)(2,1)} %param.9), channel_id=1, source_target_pairs={{0,16},{16,0},{1,17},{17,1},{2,18},{18,2},{3,19},{19,3},{4,20},{20... | collective-permute-start | bytes 1572872 | tf_op jit(solution)/shard_map/ppermute | solution.py:138
  15.0 11.4 %collective-permute-start.1 = (bf16[256,1024]{1,0:T(8,128)(2,1)}, bf16[256,1024]{1,0:T(8,128)(2,1)S(1)}, u32[]{:S(2)}, u32[]{:S(2)}) collective-permute-start(bf16[256,1024]{1,0:T(8,128)(2,1)} %param.10), channel_id=1, source_target_pairs={{0,16},{16,0},{1,17},{17,1},{2,18},{18,2},{3,19},{19,3},{4,20},{20... | collective-permute-start | bytes 1572872 | tf_op jit(solution)/shard_map/ppermute | solution.py:138
  17.2 9.7 %collective-permute-start.2 = (bf16[1024,256]{1,0:T(8,128)(2,1)S(1)}, bf16[1024,256]{1,0:T(8,128)(2,1)S(1)}, u32[]{:S(2)}, u32[]{:S(2)}) collective-permute-start(bf16[1024,256]{1,0:T(8,128)(2,1)S(1)} %copy-done), channel_id=1, source_target_pairs={{0,16},{16,0},{1,17},{17,1},{2,18},{18,2},{3,19},{19,3},{4,20},{20... | collective-permute-start | bytes 1572872 | tf_op jit(solution)/shard_map/ppermute | solution.py:138
  19.4 7.5 %collective-permute-start.3 = (bf16[1024,256]{1,0:T(8,128)(2,1)}, bf16[1024,256]{1,0:T(8,128)(2,1)S(1)}, u32[]{:S(2)}, u32[]{:S(2)}) collective-permute-start(bf16[1024,256]{1,0:T(8,128)(2,1)} %turn_ref.1), channel_id=1, source_target_pairs={{0,16},{16,0},{1,17},{17,1},{2,18},{18,2},{3,19},{19,3},{4,20},{20... | collective-permute-start | bytes 1572872 | tf_op jit(solution)/shard_map/ppermute | solution.py:138
  21.6 5.3 %collective-permute-start.4 = (f32[32,256]{1,0:T(8,128)S(1)}, f32[32,256]{1,0:T(8,128)S(1)}, u32[]{:S(2)}, u32[]{:S(2)}) collective-permute-start(f32[32,256]{1,0:T(8,128)S(1)} %copy-done.2), channel_id=1, source_target_pairs={{0,16},{16,0},{1,17},{17,1},{2,18},{18,2},{3,19},{19,3},{4,20},{20... | collective-permute-start | bytes 98312 | tf_op jit(solution)/shard_map/ppermute | solution.py:138
  24.6 1.4 copy-start.5
  26.9 56.0 %copy-start.1 = (bf16[1024,256]{1,0:T(8,128)(2,1)S(1)}, bf16[1024,256]{1,0:T(8,128)(2,1)}, u32[]{:S(2)}) copy-start(bf16[1024,256]{1,0:T(8,128)(2,1)} %turn_ref.1) | copy-start | bytes 1572868
  82.9 1.0 copy-start.3
  132.5 4.6 %copy-start.4 = (bf16[256,2048]{1,0:T(8,128)(2,1)S(1)}, bf16[256,2048]{1,0:T(8,128)(2,1)}, u32[]{:S(2)}) copy-start(bf16[256,2048]{1,0:T(8,128)(2,1)} %copy-done.3) | copy-start | bytes 3145732
  133.4 16.7 %all-to-all-start.10 = ((bf16[16,16,1024]{2,1,0:T(8,128)(2,1)}), bf16[16,16,1024]{2,1,0:T(8,128)(2,1)S(1)}, u32[]{:S(2)}, u32[]{:S(2)}) async-start(bf16[16,16,1024]{2,1,0:T(8,128)(2,1)} %shard_map.80), calls=%async_computation.10 | async-start | bytes 1048576 | tf_op jit(solution)/shard_map/all_to_all | solution.py:37
  137.4 8.6 %collective-permute-start.5 = (bf16[1024,256]{1,0:T(8,128)(2,1)S(1)}, bf16[1024,256]{1,0:T(8,128)(2,1)S(1)}, u32[]{:S(2)}, u32[]{:S(2)}) collective-permute-start(bf16[1024,256]{1,0:T(8,128)(2,1)S(1)} %convolution_convert_fusion.1), channel_id=1, source_target_pairs={{0,16},{16,0},{1,17},{17,1},{2,18},{18,2},{3,19},{19,3},{4,20},{20... | collective-permute-start | bytes 1572872 | tf_op jit(solution)/shard_map/ppermute | solution.py:138
  150.4 9.9 %collective-permute-start.6 = (bf16[256,1024]{1,0:T(8,128)(2,1)S(1)}, bf16[256,1024]{1,0:T(8,128)(2,1)S(1)}, u32[]{:S(2)}, u32[]{:S(2)}) collective-permute-start(bf16[256,1024]{1,0:T(8,128)(2,1)S(1)} %convolution_convert_fusion), channel_id=1, source_target_pairs={{0,16},{16,0},{1,17},{17,1},{2,18},{18,2},{3,19},{19,3},{4,20},{20... | collective-permute-start | bytes 1572872 | tf_op jit(solution)/shard_map/ppermute | solution.py:138

commit v6 on v5

--- a/solution.py
+++ b/solution.py
@@ -47,7 +47,7 @@
         out_shape=results,
         in_specs=[IN_VMEM] * len(operands),
         out_specs=[IN_VMEM] * len(results),
-        compiler_params=pltpu.CompilerParams(vmem_limit_bytes=16 * 2**20),
+        compiler_params=pltpu.CompilerParams(vmem_limit_bytes=8 * 2**20),
         cost_estimate=pl.CostEstimate(flops=flops, bytes_accessed=moved_bytes, transcendentals=0),
     )(*operands)
 
@@ -68,6 +68,13 @@
     result_ref[:, :width] = own.astype(result_ref.dtype)
     far = dot(moved, out_far_ref[...]) + dot(active, turn_far_ref[...])
     result_ref[:, width:] = far.astype(result_ref.dtype)
+
+
+def backward_kernel(cotangent_ref, out_ref, out_far_ref, result_ref):
+    width = out_ref.shape[1]
+    total = dot(cotangent_ref[:, :width], out_ref[...], 1, 1)
+    total += dot(cotangent_ref[:, width:], out_far_ref[...], 1, 1)
+    result_ref[...] = total.astype(result_ref.dtype)
 
 
 def sum_pieces(pieces_ref):
@@ -189,8 +196,13 @@
     cotangent = exchange(copies.reshape(rows, 2 * features), TENSOR)
     cotangent_own, cotangent_far = cotangent[:, :features], cotangent[:, features:]
 
-    backward = dot(cotangent_own, weight_out, 1, 1) + dot(cotangent_far, out_far, 1, 1)
-    pieces = exchange(backward.astype(jnp.bfloat16), ROWS).reshape(-1, share, hidden)
+    (backward,) = kernel_call(
+        backward_kernel,
+        [jax.ShapeDtypeStruct((rows, hidden), jnp.bfloat16)],
+        (cotangent, weight_out, out_far),
+        flops,
+    )
+    pieces = exchange(backward, ROWS).reshape(-1, share, hidden)
     far_out = swap_cores(dot(active, cotangent_far, 0, 0).astype(jnp.bfloat16))
     product_out = dot(active, cotangent_own, 0, 0) + far_out.astype(jnp.float32)
 

time: 162 us -> 162 us (level)
    dot_general x8 -> x6, matrix products: 4.51 us -> 3.85 us  [dot(): lax.dot_general(left_side, right_side, (((left_dim,), (right_dim,)), ((),...]
where the time goes in v6:
time: 162 us; the launch traced here: 161 us
  blocking collectives  104 us (64%)
  starting transfers between devices  40.7 us (25%)
  waiting for transfers between devices  6.51 us (4%)
  matrix products  3.85 us (2%)
  Pallas kernels  2.83 us (2%)
  local copies, waits for them, and re-layouts  1.8 us (1%)
    all_to_all x6, blocking collectives, exchange(): return lax.all_to_all(pieces, axes, split_axis=0, concat_axis=0, tiled=True)  104 us
    ppermute x7, starting transfers between devices, swap_cores(): return lax.ppermute(block, 'c', SWAP)  26.2 us
    all_to_all x2, starting transfers between devices, exchange(): return lax.all_to_all(pieces, axes, split_axis=0, concat_axis=0, tiled=True)  14.4 us
    dot_general x6, matrix products, dot(): lax.dot_general(left_side, right_side, (((left_dim,), (right_dim,)), ((),...  3.85 us
    all_to_all x2, waiting for transfers between devices, exchange(): return lax.all_to_all(pieces, axes, split_axis=0, concat_axis=0, tiled=True)  3.8 us
  transfers between devices with their start and end apart: 9, of which 4 were waited for; matrix products, arithmetic and copies ran while one was open for 2% of the time, Pallas kernels for 0%

profile of v6, /device:TPU:1, one launch (start us, length us, event | category | flops | bytes accessed | tf_op | source)
XLA Modules:
  0.0 161.0 jit_solution(12539152387447113362)
XLA Ops:
  0.6 0.0 copy-start
  0.6 1.5 broadcast_in_dim.16
  2.1 0.0 copy-start.2
  2.1 10.7 %all-to-all-start.6 = ((bf16[32,16,256]{2,1,0:T(8,128)(2,1)}), bf16[32,16,256]{2,1,0:T(8,128)(2,1)S(1)}, u32[]{:S(2)}, u32[]{:S(2)}) async-start(bf16[32,16,256]{2,1,0:T(8,128)(2,1)} %bitcast.7), calls=%async_computation.6 | async-start | bytes 524288 | tf_op jit(solution)/shard_map/all_to_all | solution.py:37
  12.8 2.1 %collective-permute-start = (bf16[256,1024]{1,0:T(8,128)(2,1)}, bf16[256,1024]{1,0:T(8,128)(2,1)S(1)}, u32[]{:S(2)}, u32[]{:S(2)}) collective-permute-start(bf16[256,1024]{1,0:T(8,128)(2,1)} %param.9), channel_id=1, source_target_pairs={{0,16},{16,0},{1,17},{17,1},{2,18},{18,2},{3,19},{19,3},{4,20},{20... | collective-permute-start | bytes 1572872 | tf_op jit(solution)/shard_map/ppermute | solution.py:145
  15.0 2.2 %collective-permute-start.1 = (bf16[256,1024]{1,0:T(8,128)(2,1)}, bf16[256,1024]{1,0:T(8,128)(2,1)S(1)}, u32[]{:S(2)}, u32[]{:S(2)}) collective-permute-start(bf16[256,1024]{1,0:T(8,128)(2,1)} %param.10), channel_id=1, source_target_pairs={{0,16},{16,0},{1,17},{17,1},{2,18},{18,2},{3,19},{19,3},{4,20},{20... | collective-permute-start | bytes 1572872 | tf_op jit(solution)/shard_map/ppermute | solution.py:145
  17.2 0.0 copy-done
  17.2 2.1 %collective-permute-start.2 = (bf16[1024,256]{1,0:T(8,128)(2,1)S(1)}, bf16[1024,256]{1,0:T(8,128)(2,1)S(1)}, u32[]{:S(2)}, u32[]{:S(2)}) collective-permute-start(bf16[1024,256]{1,0:T(8,128)(2,1)S(1)} %copy-done), channel_id=1, source_target_pairs={{0,16},{16,0},{1,17},{17,1},{2,18},{18,2},{3,19},{19,3},{4,20},{20... | collective-permute-start | bytes 1572872 | tf_op jit(solution)/shard_map/ppermute | solution.py:145
  19.4 2.2 %collective-permute-start.3 = (bf16[1024,256]{1,0:T(8,128)(2,1)}, bf16[1024,256]{1,0:T(8,128)(2,1)S(1)}, u32[]{:S(2)}, u32[]{:S(2)}) collective-permute-start(bf16[1024,256]{1,0:T(8,128)(2,1)} %turn_ref.1), channel_id=1, source_target_pairs={{0,16},{16,0},{1,17},{17,1},{2,18},{18,2},{3,19},{19,3},{4,20},{20... | collective-permute-start | bytes 1572872 | tf_op jit(solution)/shard_map/ppermute | solution.py:145
  21.6 0.0 copy-done.2
  21.6 2.1 %collective-permute-start.4 = (f32[32,256]{1,0:T(8,128)S(1)}, f32[32,256]{1,0:T(8,128)S(1)}, u32[]{:S(2)}, u32[]{:S(2)}) collective-permute-start(f32[32,256]{1,0:T(8,128)S(1)} %copy-done.2), channel_id=1, source_target_pairs={{0,16},{16,0},{1,17},{17,1},{2,18},{18,2},{3,19},{19,3},{4,20},{20... | collective-permute-start | bytes 98312 | tf_op jit(solution)/shard_map/ppermute | solution.py:145
  23.7 0.9 all-to-all-done.6
  24.6 1.4 fusion.11.preact_ref
  26.0 0.0 copy-done.5
  26.0 0.3 fusion.9.tangent_ref
  26.4 0.0 collective-permute-done.in_far_ref
  26.4 0.0 collective-permute-done.1.slope_far_ref
  26.4 0.4 shard_map.77
  26.9 0.0 copy-start.1
  26.9 0.0 collective-permute-done.4.curvature_far_ref
  26.9 0.0 collective-permute-done.2.out_far_ref
  26.9 0.0 collective-permute-done.3.turn_far_ref
  26.9 56.0 %conditional.1 = (bf16[256,2048]{1,0:T(8,128)(2,1)S(1)}, f32[16,1024]{1,0:T(8,128)S(1)}) conditional(s32[]{:T(128)} %convert_element_type.21, bf16[256,2048]{1,0:T(8,128)(2,1)S(1)} %shard_map.77, bf16[256,2048]{1,0:T(8,128)(2,1)S(1)} %shard_map.77), branch_computations={%region_0.1_spmd, %region_1.2_spmd} | conditional | flops 655360 | bytes 7405584 | solution.py:175
  26.9 13.7 %all_to_all.87.pieces_ref = bf16[4,64,2048]{2,1,0:T(8,128)(2,1)S(1)} all-to-all(bf16[4,64,2048]{2,1,0:T(8,128)(2,1)S(1)} %bitcast.34), channel_id=1, replica_groups=mesh['zh'=4,'x'=4,'c'=2,'y'=8,'zl'=2] {'x'}, dimensions={0} | all-to-all | bytes 2097152 | tf_op jit(solution)/shard_map/cond/branch_1_fun/all_to_all | solution.py:37
  40.6 0.1 branch_1_fun.2
  40.8 19.6 %all_to_all.88.pieces_ref = bf16[4,16,2048]{2,1,0:T(8,128)(2,1)S(1)} all-to-all(bf16[4,16,2048]{2,1,0:T(8,128)(2,1)S(1)} %bitcast.31), channel_id=1, replica_groups=mesh['zh'=4,'x'=4,'c'=2,'y'=8,'zl'=2] {'zh'}, dimensions={0} | all-to-all | bytes 524288 | tf_op jit(solution)/shard_map/cond/branch_1_fun/all_to_all | solution.py:37
  60.4 0.1 branch_1_fun.3
  60.5 22.4 %all_to_all.89 = bf16[16,16,2048]{2,1,0:T(8,128)(2,1)S(1)} all-to-all(bf16[16,16,2048]{2,1,0:T(8,128)(2,1)S(1)} %get-tuple-element.10), channel_id=1, replica_groups=mesh['zh'=4,'x'=4,'c'=2,'y'=8,'zl'=2] {'x','zh'}, dimensions={0} | all-to-all | bytes 2097152 | tf_op jit(solution)/shard_map/cond/branch_1_fun/all_to_all | solution.py:37
  82.9 0.0 copy-done.1
  82.9 0.7 shard_map.78
  83.6 0.3 copy-done.3
  83.9 18.9 %all_to_all.90.pieces_ref = bf16[16,16,512]{2,1,0:T(8,128)(2,1)S(1)} all-to-all(bf16[16,16,512]{2,1,0:T(8,128)(2,1)S(1)} %bitcast.32), channel_id=1, replica_groups=mesh['zh'=4,'x'=4,'c'=2,'y'=8,'zl'=2] {'y','zl'}, dimensions={0} | all-to-all | bytes 524288 | tf_op jit(solution)/shard_map/all_to_all | solution.py:37
  102.8 12.3 %all_to_all.91 = bf16[16,16,512]{2,1,0:T(8,128)(2,1)S(1)} all-to-all(bf16[16,16,512]{2,1,0:T(8,128)(2,1)S(1)} %shard_map.79), channel_id=1, replica_groups=mesh['zh'=4,'x'=4,'c'=2,'y'=8,'zl'=2] {'y','zl'}, dimensions={0} | all-to-all | bytes 524288 | tf_op jit(solution)/shard_map/all_to_all | solution.py:37
  115.1 0.5 shard_map.80
  115.6 16.7 %all_to_all.92.pieces_ref = bf16[16,16,1024]{2,1,0:T(8,128)(2,1)S(1)} all-to-all(bf16[16,16,1024]{2,1,0:T(8,128)(2,1)S(1)} %bitcast.27), channel_id=1, replica_groups=mesh['zh'=4,'x'=4,'c'=2,'y'=8,'zl'=2] {'x','zh'}, dimensions={0} | all-to-all | bytes 1048576 | tf_op jit(solution)/shard_map/all_to_all | solution.py:37
  132.3 0.9 shard_map.81
  133.2 3.7 %all-to-all-start.10 = ((bf16[16,16,1024]{2,1,0:T(8,128)(2,1)}), bf16[16,16,1024]{2,1,0:T(8,128)(2,1)S(1)}, u32[]{:S(2)}, u32[]{:S(2)}) async-start(bf16[16,16,1024]{2,1,0:T(8,128)(2,1)} %shard_map.81), calls=%async_computation.10 | async-start | bytes 1048576 | tf_op jit(solution)/shard_map/all_to_all | solution.py:37
  136.9 0.0 copy-done.4
  136.9 0.4 convolution_convert_fusion.1
  137.3 7.1 %collective-permute-start.5 = (bf16[1024,256]{1,0:T(8,128)(2,1)S(1)}, bf16[1024,256]{1,0:T(8,128)(2,1)S(1)}, u32[]{:S(2)}, u32[]{:S(2)}) collective-permute-start(bf16[1024,256]{1,0:T(8,128)(2,1)S(1)} %convolution_convert_fusion.1), channel_id=1, source_target_pairs={{0,16},{16,0},{1,17},{17,1},{2,18},{18,2},{3,19},{19,3},{4,20},{20... | collective-permute-start | bytes 1572872 | tf_op jit(solution)/shard_map/ppermute | solution.py:145
  144.4 1.5 collective-permute-done.5
  145.9 1.1 add_convert_fusion.1
  147.0 2.9 %all-to-all-done.10 = bf16[16,16,1024]{2,1,0:T(8,128)(2,1)S(1)} async-done(((bf16[16,16,1024]{2,1,0:T(8,128)(2,1)}), bf16[16,16,1024]{2,1,0:T(8,128)(2,1)S(1)}, u32[]{:S(2)}, u32[]{:S(2)}) %all-to-all-start.10) | async-done | bytes 524320 | tf_op jit(solution)/shard_map/all_to_all | solution.py:37
  149.9 0.3 convolution_convert_fusion
  150.2 8.3 %collective-permute-start.6 = (bf16[256,1024]{1,0:T(8,128)(2,1)S(1)}, bf16[256,1024]{1,0:T(8,128)(2,1)S(1)}, u32[]{:S(2)}, u32[]{:S(2)}) collective-permute-start(bf16[256,1024]{1,0:T(8,128)(2,1)S(1)} %convolution_convert_fusion), channel_id=1, source_target_pairs={{0,16},{16,0},{1,17},{17,1},{2,18},{18,2},{3,19},{19,3},{4,20},{20... | collective-permute-start | bytes 1572872 | tf_op jit(solution)/shard_map/ppermute | solution.py:145
  158.6 0.3 fusion.7
  158.9 1.2 collective-permute-done.6
  160.1 0.9 add_convert_fusion
  (5 shorter events, 0.1 us)
Async XLA Ops:
  0.6 16.6 %copy-start = (bf16[1024,256]{1,0:T(8,128)(2,1)S(1)}, bf16[1024,256]{1,0:T(8,128)(2,1)}, u32[]{:S(2)}) copy-start(bf16[1024,256]{1,0:T(8,128)(2,1)} %out_ref.3) | copy-start | bytes 1572868
  2.1 19.4 %copy-start.2 = (f32[32,256]{1,0:T(8,128)S(1)}, f32[32,256]{1,0:T(8,128)}, u32[]{:S(2)}) copy-start(f32[32,256]{1,0:T(8,128)} %curvature_ref.1) | copy-start | bytes 98308
  2.1 22.5 %all-to-all-start.6 = ((bf16[32,16,256]{2,1,0:T(8,128)(2,1)}), bf16[32,16,256]{2,1,0:T(8,128)(2,1)S(1)}, u32[]{:S(2)}, u32[]{:S(2)}) async-start(bf16[32,16,256]{2,1,0:T(8,128)(2,1)} %bitcast.7), calls=%async_computation.6 | async-start | bytes 524288 | tf_op jit(solution)/shard_map/all_to_all | solution.py:37
  12.8 13.5 %collective-permute-start = (bf16[256,1024]{1,0:T(8,128)(2,1)}, bf16[256,1024]{1,0:T(8,128)(2,1)S(1)}, u32[]{:S(2)}, u32[]{:S(2)}) collective-permute-start(bf16[256,1024]{1,0:T(8,128)(2,1)} %param.9), channel_id=1, source_target_pairs={{0,16},{16,0},{1,17},{17,1},{2,18},{18,2},{3,19},{19,3},{4,20},{20... | collective-permute-start | bytes 1572872 | tf_op jit(solution)/shard_map/ppermute | solution.py:145
  15.0 11.4 %collective-permute-start.1 = (bf16[256,1024]{1,0:T(8,128)(2,1)}, bf16[256,1024]{1,0:T(8,128)(2,1)S(1)}, u32[]{:S(2)}, u32[]{:S(2)}) collective-permute-start(bf16[256,1024]{1,0:T(8,128)(2,1)} %param.10), channel_id=1, source_target_pairs={{0,16},{16,0},{1,17},{17,1},{2,18},{18,2},{3,19},{19,3},{4,20},{20... | collective-permute-start | bytes 1572872 | tf_op jit(solution)/shard_map/ppermute | solution.py:145
  17.2 9.7 %collective-permute-start.2 = (bf16[1024,256]{1,0:T(8,128)(2,1)S(1)}, bf16[1024,256]{1,0:T(8,128)(2,1)S(1)}, u32[]{:S(2)}, u32[]{:S(2)}) collective-permute-start(bf16[1024,256]{1,0:T(8,128)(2,1)S(1)} %copy-done), channel_id=1, source_target_pairs={{0,16},{16,0},{1,17},{17,1},{2,18},{18,2},{3,19},{19,3},{4,20},{20... | collective-permute-start | bytes 1572872 | tf_op jit(solution)/shard_map/ppermute | solution.py:145
  19.4 7.5 %collective-permute-start.3 = (bf16[1024,256]{1,0:T(8,128)(2,1)}, bf16[1024,256]{1,0:T(8,128)(2,1)S(1)}, u32[]{:S(2)}, u32[]{:S(2)}) collective-permute-start(bf16[1024,256]{1,0:T(8,128)(2,1)} %turn_ref.1), channel_id=1, source_target_pairs={{0,16},{16,0},{1,17},{17,1},{2,18},{18,2},{3,19},{19,3},{4,20},{20... | collective-permute-start | bytes 1572872 | tf_op jit(solution)/shard_map/ppermute | solution.py:145
  21.6 5.3 %collective-permute-start.4 = (f32[32,256]{1,0:T(8,128)S(1)}, f32[32,256]{1,0:T(8,128)S(1)}, u32[]{:S(2)}, u32[]{:S(2)}) collective-permute-start(f32[32,256]{1,0:T(8,128)S(1)} %copy-done.2), channel_id=1, source_target_pairs={{0,16},{16,0},{1,17},{17,1},{2,18},{18,2},{3,19},{19,3},{4,20},{20... | collective-permute-start | bytes 98312 | tf_op jit(solution)/shard_map/ppermute | solution.py:145
  24.6 1.4 copy-start.5
  26.9 56.0 %copy-start.1 = (bf16[1024,256]{1,0:T(8,128)(2,1)S(1)}, bf16[1024,256]{1,0:T(8,128)(2,1)}, u32[]{:S(2)}) copy-start(bf16[1024,256]{1,0:T(8,128)(2,1)} %turn_ref.1) | copy-start | bytes 1572868
  82.9 1.0 copy-start.3
  132.3 4.6 %copy-start.4 = (bf16[256,2048]{1,0:T(8,128)(2,1)S(1)}, bf16[256,2048]{1,0:T(8,128)(2,1)}, u32[]{:S(2)}) copy-start(bf16[256,2048]{1,0:T(8,128)(2,1)} %copy-done.3) | copy-start | bytes 3145732
  133.2 16.7 %all-to-all-start.10 = ((bf16[16,16,1024]{2,1,0:T(8,128)(2,1)}), bf16[16,16,1024]{2,1,0:T(8,128)(2,1)S(1)}, u32[]{:S(2)}, u32[]{:S(2)}) async-start(bf16[16,16,1024]{2,1,0:T(8,128)(2,1)} %shard_map.81), calls=%async_computation.10 | async-start | bytes 1048576 | tf_op jit(solution)/shard_map/all_to_all | solution.py:37
  137.3 8.6 %collective-permute-start.5 = (bf16[1024,256]{1,0:T(8,128)(2,1)S(1)}, bf16[1024,256]{1,0:T(8,128)(2,1)S(1)}, u32[]{:S(2)}, u32[]{:S(2)}) collective-permute-start(bf16[1024,256]{1,0:T(8,128)(2,1)S(1)} %convolution_convert_fusion.1), channel_id=1, source_target_pairs={{0,16},{16,0},{1,17},{17,1},{2,18},{18,2},{3,19},{19,3},{4,20},{20... | collective-permute-start | bytes 1572872 | tf_op jit(solution)/shard_map/ppermute | solution.py:145
  150.2 9.9 %collective-permute-start.6 = (bf16[256,1024]{1,0:T(8,128)(2,1)S(1)}, bf16[256,1024]{1,0:T(8,128)(2,1)S(1)}, u32[]{:S(2)}, u32[]{:S(2)}) collective-permute-start(bf16[256,1024]{1,0:T(8,128)(2,1)S(1)} %convolution_convert_fusion), channel_id=1, source_target_pairs={{0,16},{16,0},{1,17},{17,1},{2,18},{18,2},{3,19},{19,3},{4,20},{20... | collective-permute-start | bytes 1572872 | tf_op jit(solution)/shard_map/ppermute | solution.py:145

commit v7 on v6

--- a/solution.py
+++ b/solution.py
@@ -85,6 +85,11 @@
     result_ref[...] = sum_pieces(pieces_ref).astype(result_ref.dtype)
 
 
+def copies_kernel(halves_ref, copies_ref):
+    for n in range(copies_ref.shape[1]):
+        copies_ref[:, n] = halves_ref[...]
+
+
 def gelu_kernel(pieces_ref, copies_ref, derivative_ref):
     total = sum_pieces(pieces_ref)
     hidden = derivative_ref.shape[1]
@@ -151,8 +156,11 @@
     features = tokens.shape[1]
     share = tokens.shape[0] // 2
 
-    halves = tokens.reshape(2, 1, share, features)
-    copies = jnp.broadcast_to(halves, (2, lax.axis_size(TENSOR), share, features))
+    halves = tokens.reshape(2, share, features)
+    shape = (2, lax.axis_size(TENSOR), share, features)
+    (copies,) = kernel_call(
+        copies_kernel, [jax.ShapeDtypeStruct(shape, tokens.dtype)], (halves,), 0
+    )
     arrived = exchange(copies.reshape(-1, features), ("c",) + TENSOR).reshape(2, -1, features)
     tokens_own = lax.dynamic_index_in_dim(arrived, core, 0, keepdims=False)
     tokens_far = lax.dynamic_index_in_dim(arrived, 1 - core, 0, keepdims=False)

time: 162 us -> 169 us (1.043)
  blocking collectives: 104 us -> 112 us
  starting transfers between devices: 40.7 us -> 33.8 us
  waiting for transfers between devices: 6.51 us -> 12.7 us
    all_to_all x6, blocking collectives: 104 us -> 112 us  [exchange(): return lax.all_to_all(pieces, axes, split_axis=0, concat_axis=0, tiled=True)]
    ppermute x7, starting transfers between devices: 26.2 us -> 18.3 us  [swap_cores(): return lax.ppermute(block, 'c', SWAP)]
    all_to_all x2, waiting for transfers between devices: 3.8 us -> 9.97 us  [exchange(): return lax.all_to_all(pieces, axes, split_axis=0, concat_axis=0, tiled=True)]
    pallas_call x7 -> x8, Pallas kernels: 2.83 us -> 3.54 us  [kernel_call(): pl.pallas_call(kernel, out_shape=results, in_specs=[IN_VMEM] * len(operan...]
where the time goes in v7:
time: 169 us; the launch traced here: 168 us
  blocking collectives  112 us (66%)
  starting transfers between devices  33.8 us (20%)
  waiting for transfers between devices  12.7 us (8%)
  matrix products  3.85 us (2%)
  Pallas kernels  3.54 us (2%)
    all_to_all x6, blocking collectives, exchange(): return lax.all_to_all(pieces, axes, split_axis=0, concat_axis=0, tiled=True)  112 us
    ppermute x7, starting transfers between devices, swap_cores(): return lax.ppermute(block, 'c', SWAP)  18.3 us
    all_to_all x2, starting transfers between devices, exchange(): return lax.all_to_all(pieces, axes, split_axis=0, concat_axis=0, tiled=True)  15.5 us
    all_to_all x2, waiting for transfers between devices, exchange(): return lax.all_to_all(pieces, axes, split_axis=0, concat_axis=0, tiled=True)  9.97 us
    dot_general x6, matrix products, dot(): lax.dot_general(left_side, right_side, (((left_dim,), (right_dim,)), ((),...  3.85 us
    pallas_call x8, Pallas kernels, kernel_call(): pl.pallas_call(kernel, out_shape=results, in_specs=[IN_VMEM] * len(operan...  3.54 us
  transfers between devices with their start and end apart: 9, of which 4 were waited for; matrix products, arithmetic and copies ran while one was open for 2% of the time, Pallas kernels for 0%

profile of v7, /device:TPU:1, one launch (start us, length us, event | category | flops | bytes accessed | tf_op | source)
XLA Modules:
  0.0 168.5 jit_solution(17399598551420598635)
XLA Ops:
  0.6 0.0 copy-start
  0.6 0.0 copy-start.3
  0.6 0.8 copy-done.3
  1.4 0.7 shard_map.77
  2.1 10.7 %all-to-all-start.6 = ((bf16[32,16,256]{2,1,0:T(8,128)(2,1)}), bf16[32,16,256]{2,1,0:T(8,128)(2,1)S(1)}, u32[]{:S(2)}, u32[]{:S(2)}) async-start(bf16[32,16,256]{2,1,0:T(8,128)(2,1)} %bitcast.7), calls=%async_computation.6 | async-start | bytes 524288 | tf_op jit(solution)/shard_map/all_to_all | solution.py:37
  12.8 2.1 %collective-permute-start = (bf16[256,1024]{1,0:T(8,128)(2,1)}, bf16[256,1024]{1,0:T(8,128)(2,1)S(1)}, u32[]{:S(2)}, u32[]{:S(2)}) collective-permute-start(bf16[256,1024]{1,0:T(8,128)(2,1)} %param.9), channel_id=1, source_target_pairs={{0,16},{16,0},{1,17},{17,1},{2,18},{18,2},{3,19},{19,3},{4,20},{20... | collective-permute-start | bytes 1572872 | tf_op jit(solution)/shard_map/ppermute | solution.py:150
  15.0 2.2 %collective-permute-start.1 = (bf16[256,1024]{1,0:T(8,128)(2,1)}, bf16[256,1024]{1,0:T(8,128)(2,1)S(1)}, u32[]{:S(2)}, u32[]{:S(2)}) collective-permute-start(bf16[256,1024]{1,0:T(8,128)(2,1)} %param.10), channel_id=1, source_target_pairs={{0,16},{16,0},{1,17},{17,1},{2,18},{18,2},{3,19},{19,3},{4,20},{20... | collective-permute-start | bytes 1572872 | tf_op jit(solution)/shard_map/ppermute | solution.py:150
  17.2 0.0 copy-done
  17.2 2.1 %collective-permute-start.2 = (bf16[1024,256]{1,0:T(8,128)(2,1)S(1)}, bf16[1024,256]{1,0:T(8,128)(2,1)S(1)}, u32[]{:S(2)}, u32[]{:S(2)}) collective-permute-start(bf16[1024,256]{1,0:T(8,128)(2,1)S(1)} %copy-done), channel_id=1, source_target_pairs={{0,16},{16,0},{1,17},{17,1},{2,18},{18,2},{3,19},{19,3},{4,20},{20... | collective-permute-start | bytes 1572872 | tf_op jit(solution)/shard_map/ppermute | solution.py:150
  19.4 2.2 %collective-permute-start.3 = (bf16[1024,256]{1,0:T(8,128)(2,1)}, bf16[1024,256]{1,0:T(8,128)(2,1)S(1)}, u32[]{:S(2)}, u32[]{:S(2)}) collective-permute-start(bf16[1024,256]{1,0:T(8,128)(2,1)} %turn_ref.1), channel_id=1, source_target_pairs={{0,16},{16,0},{1,17},{17,1},{2,18},{18,2},{3,19},{19,3},{4,20},{20... | collective-permute-start | bytes 1572872 | tf_op jit(solution)/shard_map/ppermute | solution.py:150
  21.6 0.0 copy-done.2
  21.6 2.1 %collective-permute-start.4 = (f32[32,256]{1,0:T(8,128)S(1)}, f32[32,256]{1,0:T(8,128)S(1)}, u32[]{:S(2)}, u32[]{:S(2)}) collective-permute-start(f32[32,256]{1,0:T(8,128)S(1)} %copy-done.2), channel_id=1, source_target_pairs={{0,16},{16,0},{1,17},{17,1},{2,18},{18,2},{3,19},{19,3},{4,20},{20... | collective-permute-start | bytes 98312 | tf_op jit(solution)/shard_map/ppermute | solution.py:150
  23.7 0.9 all-to-all-done.6
  24.6 1.4 fusion.11.preact_ref
  26.0 0.0 copy-done.6
  26.1 0.3 fusion.9.tangent_ref
  26.4 0.0 collective-permute-done.in_far_ref
  26.4 0.0 collective-permute-done.1.slope_far_ref
  26.4 0.4 shard_map.78
  26.9 0.0 copy-start.1
  26.9 0.0 collective-permute-done.4.curvature_far_ref
  26.9 0.0 collective-permute-done.2.out_far_ref
  26.9 0.0 collective-permute-done.3.turn_far_ref
  26.9 56.0 %conditional.1 = (bf16[256,2048]{1,0:T(8,128)(2,1)S(1)}, f32[16,1024]{1,0:T(8,128)S(1)}) conditional(s32[]{:T(128)} %convert_element_type.21, bf16[256,2048]{1,0:T(8,128)(2,1)S(1)} %shard_map.78, bf16[256,2048]{1,0:T(8,128)(2,1)S(1)} %shard_map.78), branch_computations={%region_0.1_spmd, %region_1.2_spmd} | conditional | flops 655360 | bytes 7405584 | solution.py:183
  26.9 13.7 %all_to_all.87.pieces_ref = bf16[4,64,2048]{2,1,0:T(8,128)(2,1)S(1)} all-to-all(bf16[4,64,2048]{2,1,0:T(8,128)(2,1)S(1)} %bitcast.35), channel_id=1, replica_groups=mesh['zh'=4,'x'=4,'c'=2,'y'=8,'zl'=2] {'x'}, dimensions={0} | all-to-all | bytes 2097152 | tf_op jit(solution)/shard_map/cond/branch_1_fun/all_to_all | solution.py:37
  40.6 0.1 branch_1_fun.2
  40.8 19.6 %all_to_all.88.pieces_ref = bf16[4,16,2048]{2,1,0:T(8,128)(2,1)S(1)} all-to-all(bf16[4,16,2048]{2,1,0:T(8,128)(2,1)S(1)} %bitcast.31), channel_id=1, replica_groups=mesh['zh'=4,'x'=4,'c'=2,'y'=8,'zl'=2] {'zh'}, dimensions={0} | all-to-all | bytes 524288 | tf_op jit(solution)/shard_map/cond/branch_1_fun/all_to_all | solution.py:37
  60.4 0.1 branch_1_fun.3
  60.5 22.4 %all_to_all.89 = bf16[16,16,2048]{2,1,0:T(8,128)(2,1)S(1)} all-to-all(bf16[16,16,2048]{2,1,0:T(8,128)(2,1)S(1)} %get-tuple-element.10), channel_id=1, replica_groups=mesh['zh'=4,'x'=4,'c'=2,'y'=8,'zl'=2] {'x','zh'}, dimensions={0} | all-to-all | bytes 2097152 | tf_op jit(solution)/shard_map/cond/branch_1_fun/all_to_all | solution.py:37
  82.9 0.0 copy-done.1
  82.9 0.7 shard_map.79
  83.6 0.3 copy-done.4
  83.9 21.7 %all_to_all.90.pieces_ref = bf16[16,16,512]{2,1,0:T(8,128)(2,1)S(1)} all-to-all(bf16[16,16,512]{2,1,0:T(8,128)(2,1)S(1)} %bitcast.32), channel_id=1, replica_groups=mesh['zh'=4,'x'=4,'c'=2,'y'=8,'zl'=2] {'y','zl'}, dimensions={0} | all-to-all | bytes 524288 | tf_op jit(solution)/shard_map/all_to_all | solution.py:37
  105.6 12.9 %all_to_all.91 = bf16[16,16,512]{2,1,0:T(8,128)(2,1)S(1)} all-to-all(bf16[16,16,512]{2,1,0:T(8,128)(2,1)S(1)} %shard_map.80), channel_id=1, replica_groups=mesh['zh'=4,'x'=4,'c'=2,'y'=8,'zl'=2] {'y','zl'}, dimensions={0} | all-to-all | bytes 524288 | tf_op jit(solution)/shard_map/all_to_all | solution.py:37
  118.5 0.5 shard_map.81
  119.0 21.4 %all_to_all.92.pieces_ref = bf16[16,16,1024]{2,1,0:T(8,128)(2,1)S(1)} all-to-all(bf16[16,16,1024]{2,1,0:T(8,128)(2,1)S(1)} %bitcast.27), channel_id=1, replica_groups=mesh['zh'=4,'x'=4,'c'=2,'y'=8,'zl'=2] {'x','zh'}, dimensions={0} | all-to-all | bytes 1048576 | tf_op jit(solution)/shard_map/all_to_all | solution.py:37
  140.4 0.9 shard_map.82
  141.3 4.8 %all-to-all-start.10 = ((bf16[16,16,1024]{2,1,0:T(8,128)(2,1)}), bf16[16,16,1024]{2,1,0:T(8,128)(2,1)S(1)}, u32[]{:S(2)}, u32[]{:S(2)}) async-start(bf16[16,16,1024]{2,1,0:T(8,128)(2,1)} %shard_map.82), calls=%async_computation.10 | async-start | bytes 1048576 | tf_op jit(solution)/shard_map/all_to_all | solution.py:37
  146.1 0.4 convolution_convert_fusion.1
  146.5 3.1 %collective-permute-start.5 = (bf16[1024,256]{1,0:T(8,128)(2,1)S(1)}, bf16[1024,256]{1,0:T(8,128)(2,1)S(1)}, u32[]{:S(2)}, u32[]{:S(2)}) collective-permute-start(bf16[1024,256]{1,0:T(8,128)(2,1)S(1)} %convolution_convert_fusion.1), channel_id=1, source_target_pairs={{0,16},{16,0},{1,17},{17,1},{2,18},{18,2},{3,19},{19,3},{4,20},{20... | collective-permute-start | bytes 1572872 | tf_op jit(solution)/shard_map/ppermute | solution.py:150
  149.6 1.5 collective-permute-done.5
  151.1 1.1 add_convert_fusion.1
  152.3 9.1 %all-to-all-done.10 = bf16[16,16,1024]{2,1,0:T(8,128)(2,1)S(1)} async-done(((bf16[16,16,1024]{2,1,0:T(8,128)(2,1)}), bf16[16,16,1024]{2,1,0:T(8,128)(2,1)S(1)}, u32[]{:S(2)}, u32[]{:S(2)}) %all-to-all-start.10) | async-done | bytes 524320 | tf_op jit(solution)/shard_map/all_to_all | solution.py:37
  161.3 0.3 convolution_convert_fusion
  161.7 4.4 %collective-permute-start.6 = (bf16[256,1024]{1,0:T(8,128)(2,1)S(1)}, bf16[256,1024]{1,0:T(8,128)(2,1)S(1)}, u32[]{:S(2)}, u32[]{:S(2)}) collective-permute-start(bf16[256,1024]{1,0:T(8,128)(2,1)S(1)} %convolution_convert_fusion), channel_id=1, source_target_pairs={{0,16},{16,0},{1,17},{17,1},{2,18},{18,2},{3,19},{19,3},{4,20},{20... | collective-permute-start | bytes 1572872 | tf_op jit(solution)/shard_map/ppermute | solution.py:150
  166.0 0.3 fusion.7
  166.4 1.2 collective-permute-done.6
  167.6 0.9 add_convert_fusion
  (7 shorter events, 0.1 us)
Async XLA Ops:
  0.6 16.6 %copy-start = (bf16[1024,256]{1,0:T(8,128)(2,1)S(1)}, bf16[1024,256]{1,0:T(8,128)(2,1)}, u32[]{:S(2)}) copy-start(bf16[1024,256]{1,0:T(8,128)(2,1)} %out_ref.3) | copy-start | bytes 1572868
  0.6 0.8 copy-start.3
  2.1 19.4 %copy-start.2 = (f32[32,256]{1,0:T(8,128)S(1)}, f32[32,256]{1,0:T(8,128)}, u32[]{:S(2)}) copy-start(f32[32,256]{1,0:T(8,128)} %curvature_ref.1) | copy-start | bytes 98308
  2.1 22.5 %all-to-all-start.6 = ((bf16[32,16,256]{2,1,0:T(8,128)(2,1)}), bf16[32,16,256]{2,1,0:T(8,128)(2,1)S(1)}, u32[]{:S(2)}, u32[]{:S(2)}) async-start(bf16[32,16,256]{2,1,0:T(8,128)(2,1)} %bitcast.7), calls=%async_computation.6 | async-start | bytes 524288 | tf_op jit(solution)/shard_map/all_to_all | solution.py:37
  12.8 13.5 %collective-permute-start = (bf16[256,1024]{1,0:T(8,128)(2,1)}, bf16[256,1024]{1,0:T(8,128)(2,1)S(1)}, u32[]{:S(2)}, u32[]{:S(2)}) collective-permute-start(bf16[256,1024]{1,0:T(8,128)(2,1)} %param.9), channel_id=1, source_target_pairs={{0,16},{16,0},{1,17},{17,1},{2,18},{18,2},{3,19},{19,3},{4,20},{20... | collective-permute-start | bytes 1572872 | tf_op jit(solution)/shard_map/ppermute | solution.py:150
  15.0 11.4 %collective-permute-start.1 = (bf16[256,1024]{1,0:T(8,128)(2,1)}, bf16[256,1024]{1,0:T(8,128)(2,1)S(1)}, u32[]{:S(2)}, u32[]{:S(2)}) collective-permute-start(bf16[256,1024]{1,0:T(8,128)(2,1)} %param.10), channel_id=1, source_target_pairs={{0,16},{16,0},{1,17},{17,1},{2,18},{18,2},{3,19},{19,3},{4,20},{20... | collective-permute-start | bytes 1572872 | tf_op jit(solution)/shard_map/ppermute | solution.py:150
  17.2 9.7 %collective-permute-start.2 = (bf16[1024,256]{1,0:T(8,128)(2,1)S(1)}, bf16[1024,256]{1,0:T(8,128)(2,1)S(1)}, u32[]{:S(2)}, u32[]{:S(2)}) collective-permute-start(bf16[1024,256]{1,0:T(8,128)(2,1)S(1)} %copy-done), channel_id=1, source_target_pairs={{0,16},{16,0},{1,17},{17,1},{2,18},{18,2},{3,19},{19,3},{4,20},{20... | collective-permute-start | bytes 1572872 | tf_op jit(solution)/shard_map/ppermute | solution.py:150
  19.4 7.5 %collective-permute-start.3 = (bf16[1024,256]{1,0:T(8,128)(2,1)}, bf16[1024,256]{1,0:T(8,128)(2,1)S(1)}, u32[]{:S(2)}, u32[]{:S(2)}) collective-permute-start(bf16[1024,256]{1,0:T(8,128)(2,1)} %turn_ref.1), channel_id=1, source_target_pairs={{0,16},{16,0},{1,17},{17,1},{2,18},{18,2},{3,19},{19,3},{4,20},{20... | collective-permute-start | bytes 1572872 | tf_op jit(solution)/shard_map/ppermute | solution.py:150
  21.6 5.3 %collective-permute-start.4 = (f32[32,256]{1,0:T(8,128)S(1)}, f32[32,256]{1,0:T(8,128)S(1)}, u32[]{:S(2)}, u32[]{:S(2)}) collective-permute-start(f32[32,256]{1,0:T(8,128)S(1)} %copy-done.2), channel_id=1, source_target_pairs={{0,16},{16,0},{1,17},{17,1},{2,18},{18,2},{3,19},{19,3},{4,20},{20... | collective-permute-start | bytes 98312 | tf_op jit(solution)/shard_map/ppermute | solution.py:150
  24.6 1.4 copy-start.6
  26.9 56.0 %copy-start.1 = (bf16[1024,256]{1,0:T(8,128)(2,1)S(1)}, bf16[1024,256]{1,0:T(8,128)(2,1)}, u32[]{:S(2)}) copy-start(bf16[1024,256]{1,0:T(8,128)(2,1)} %turn_ref.1) | copy-start | bytes 1572868
  82.9 1.0 copy-start.4
  140.4 5.7 %copy-start.5 = (bf16[256,2048]{1,0:T(8,128)(2,1)S(1)}, bf16[256,2048]{1,0:T(8,128)(2,1)}, u32[]{:S(2)}) copy-start(bf16[256,2048]{1,0:T(8,128)(2,1)} %copy-done.4) | copy-start | bytes 3145732
  141.3 20.0 %all-to-all-start.10 = ((bf16[16,16,1024]{2,1,0:T(8,128)(2,1)}), bf16[16,16,1024]{2,1,0:T(8,128)(2,1)S(1)}, u32[]{:S(2)}, u32[]{:S(2)}) async-start(bf16[16,16,1024]{2,1,0:T(8,128)(2,1)} %shard_map.82), calls=%async_computation.10 | async-start | bytes 1048576 | tf_op jit(solution)/shard_map/all_to_all | solution.py:37
  146.5 4.6 %collective-permute-start.5 = (bf16[1024,256]{1,0:T(8,128)(2,1)S(1)}, bf16[1024,256]{1,0:T(8,128)(2,1)S(1)}, u32[]{:S(2)}, u32[]{:S(2)}) collective-permute-start(bf16[1024,256]{1,0:T(8,128)(2,1)S(1)} %convolution_convert_fusion.1), channel_id=1, source_target_pairs={{0,16},{16,0},{1,17},{17,1},{2,18},{18,2},{3,19},{19,3},{4,20},{20... | collective-permute-start | bytes 1572872 | tf_op jit(solution)/shard_map/ppermute | solution.py:150
  161.7 5.9 %collective-permute-start.6 = (bf16[256,1024]{1,0:T(8,128)(2,1)S(1)}, bf16[256,1024]{1,0:T(8,128)(2,1)S(1)}, u32[]{:S(2)}, u32[]{:S(2)}) collective-permute-start(bf16[256,1024]{1,0:T(8,128)(2,1)S(1)} %convolution_convert_fusion), channel_id=1, source_target_pairs={{0,16},{16,0},{1,17},{17,1},{2,18},{18,2},{3,19},{19,3},{4,20},{20... | collective-permute-start | bytes 1572872 | tf_op jit(solution)/shard_map/ppermute | solution.py:150

commit v8 on v6

--- a/solution.py
+++ b/solution.py
@@ -214,10 +214,14 @@
     )
     hidden_grad = exchange(copies.reshape(rows, hidden), ROWS)
     product_out = product_out.astype(jnp.bfloat16)
-    hidden_grad, product_out = lax.optimization_barrier((hidden_grad, product_out))
-    far_in = swap_cores(dot(tokens_far, hidden_grad, 0, 0).astype(jnp.bfloat16))
+    sent, far_out = lax.optimization_barrier((tokens_far, far_out))
+    tokens_cross = swap_cores(sent)
+    hidden_grad, product_out, tokens_cross = lax.optimization_barrier(
+        (hidden_grad, product_out, tokens_cross)
+    )
+    far_grad = swap_cores(hidden_grad)
     own_in = lax.optimization_barrier(dot(tokens_own, hidden_grad, 0, 0))
-    product_in = (own_in + far_in.astype(jnp.float32)).astype(jnp.bfloat16)
+    product_in = (own_in + dot(tokens_cross, far_grad, 0, 0)).astype(jnp.bfloat16)
     return (product_in, product_out)
 
 

time: 162 us -> 162 us (level)
  waiting for transfers between devices: 6.51 us -> 4.23 us
  starting transfers between devices: 40.7 us -> 42.9 us
    all_to_all x2, waiting for transfers between devices: 3.8 us -> 1.51 us  [exchange(): return lax.all_to_all(pieces, axes, split_axis=0, concat_axis=0, tiled=True)]
    ppermute x7 -> x8, starting transfers between devices: 26.2 us -> 28.5 us  [swap_cores(): return lax.ppermute(block, 'c', SWAP)]
  transfers between devices with their start and end apart: 9 -> 10, of which waited for: 4 -> 4; matrix products, arithmetic and copies ran while one was open for 2% -> 2% of each run, Pallas kernels for 0% -> 0%
where the time goes in v8:
time: 162 us; the launch traced here: 161 us
  blocking collectives  104 us (64%)
  starting transfers between devices  42.9 us (26%)
  waiting for transfers between devices  4.23 us (3%)
  matrix products  3.85 us (2%)
  Pallas kernels  2.82 us (2%)
  local copies, waits for them, and re-layouts  1.81 us (1%)
    all_to_all x6, blocking collectives, exchange(): return lax.all_to_all(pieces, axes, split_axis=0, concat_axis=0, tiled=True)  104 us
    ppermute x8, starting transfers between devices, swap_cores(): return lax.ppermute(block, 'c', SWAP)  28.5 us
    all_to_all x2, starting transfers between devices, exchange(): return lax.all_to_all(pieces, axes, split_axis=0, concat_axis=0, tiled=True)  14.4 us
    dot_general x6, matrix products, dot(): lax.dot_general(left_side, right_side, (((left_dim,), (right_dim,)), ((),...  3.85 us
  transfers between devices with their start and end apart: 10, of which 4 were waited for; matrix products, arithmetic and copies ran while one was open for 2% of the time, Pallas kernels for 0%

profile of v8, /device:TPU:1, one launch (start us, length us, event | category | flops | bytes accessed | tf_op | source)
XLA Modules:
  0.0 161.0 jit_solution(5804995585240472797)
XLA Ops:
  0.6 0.0 copy-start
  0.6 1.5 broadcast_in_dim.16
  2.1 10.7 %all-to-all-start.6 = ((bf16[32,16,256]{2,1,0:T(8,128)(2,1)}), bf16[32,16,256]{2,1,0:T(8,128)(2,1)S(1)}, u32[]{:S(2)}, u32[]{:S(2)}) async-start(bf16[32,16,256]{2,1,0:T(8,128)(2,1)} %bitcast.7), calls=%async_computation.6 | async-start | bytes 524288 | tf_op jit(solution)/shard_map/all_to_all | solution.py:37
  12.8 2.1 %collective-permute-start = (bf16[256,1024]{1,0:T(8,128)(2,1)}, bf16[256,1024]{1,0:T(8,128)(2,1)S(1)}, u32[]{:S(2)}, u32[]{:S(2)}) collective-permute-start(bf16[256,1024]{1,0:T(8,128)(2,1)} %param.9), channel_id=1, source_target_pairs={{0,16},{16,0},{1,17},{17,1},{2,18},{18,2},{3,19},{19,3},{4,20},{20... | collective-permute-start | bytes 1572872 | tf_op jit(solution)/shard_map/ppermute | solution.py:145
  15.0 2.2 %collective-permute-start.1 = (bf16[256,1024]{1,0:T(8,128)(2,1)}, bf16[256,1024]{1,0:T(8,128)(2,1)S(1)}, u32[]{:S(2)}, u32[]{:S(2)}) collective-permute-start(bf16[256,1024]{1,0:T(8,128)(2,1)} %param.10), channel_id=1, source_target_pairs={{0,16},{16,0},{1,17},{17,1},{2,18},{18,2},{3,19},{19,3},{4,20},{20... | collective-permute-start | bytes 1572872 | tf_op jit(solution)/shard_map/ppermute | solution.py:145
  17.2 0.0 copy-done
  17.2 2.1 %collective-permute-start.2 = (bf16[1024,256]{1,0:T(8,128)(2,1)S(1)}, bf16[1024,256]{1,0:T(8,128)(2,1)S(1)}, u32[]{:S(2)}, u32[]{:S(2)}) collective-permute-start(bf16[1024,256]{1,0:T(8,128)(2,1)S(1)} %copy-done), channel_id=1, source_target_pairs={{0,16},{16,0},{1,17},{17,1},{2,18},{18,2},{3,19},{19,3},{4,20},{20... | collective-permute-start | bytes 1572872 | tf_op jit(solution)/shard_map/ppermute | solution.py:145
  19.4 2.2 %collective-permute-start.3 = (bf16[1024,256]{1,0:T(8,128)(2,1)}, bf16[1024,256]{1,0:T(8,128)(2,1)S(1)}, u32[]{:S(2)}, u32[]{:S(2)}) collective-permute-start(bf16[1024,256]{1,0:T(8,128)(2,1)} %turn_ref.1), channel_id=1, source_target_pairs={{0,16},{16,0},{1,17},{17,1},{2,18},{18,2},{3,19},{19,3},{4,20},{20... | collective-permute-start | bytes 1572872 | tf_op jit(solution)/shard_map/ppermute | solution.py:145
  21.6 0.0 copy-done.2
  21.6 2.1 %collective-permute-start.4 = (f32[32,256]{1,0:T(8,128)S(1)}, f32[32,256]{1,0:T(8,128)S(1)}, u32[]{:S(2)}, u32[]{:S(2)}) collective-permute-start(f32[32,256]{1,0:T(8,128)S(1)} %copy-done.2), channel_id=1, source_target_pairs={{0,16},{16,0},{1,17},{17,1},{2,18},{18,2},{3,19},{19,3},{4,20},{20... | collective-permute-start | bytes 98312 | tf_op jit(solution)/shard_map/ppermute | solution.py:145
  23.7 0.9 all-to-all-done.6
  24.6 1.4 fusion.11.preact_ref
  26.0 0.0 copy-done.5
  26.0 0.3 fusion.9.tangent_ref
  26.4 0.0 collective-permute-done.in_far_ref
  26.4 0.0 collective-permute-done.1.slope_far_ref
  26.4 0.4 shard_map.77
  26.9 0.0 copy-start.1
  26.9 0.0 collective-permute-done.4.curvature_far_ref
  26.9 0.0 collective-permute-done.2.out_far_ref
  26.9 0.0 collective-permute-done.3.turn_far_ref
  26.9 56.0 %conditional.1 = (bf16[256,2048]{1,0:T(8,128)(2,1)S(1)}, f32[16,1024]{1,0:T(8,128)S(1)}) conditional(s32[]{:T(128)} %convert_element_type.15, bf16[256,2048]{1,0:T(8,128)(2,1)S(1)} %shard_map.77, bf16[256,2048]{1,0:T(8,128)(2,1)S(1)} %shard_map.77), branch_computations={%region_0.1_spmd, %region_1.2_spmd} | conditional | flops 655360 | bytes 7405584 | solution.py:175
  26.9 13.7 %all_to_all.87.pieces_ref = bf16[4,64,2048]{2,1,0:T(8,128)(2,1)S(1)} all-to-all(bf16[4,64,2048]{2,1,0:T(8,128)(2,1)S(1)} %bitcast.34), channel_id=1, replica_groups=mesh['zh'=4,'x'=4,'c'=2,'y'=8,'zl'=2] {'x'}, dimensions={0} | all-to-all | bytes 2097152 | tf_op jit(solution)/shard_map/cond/branch_1_fun/all_to_all | solution.py:37
  40.6 0.1 branch_1_fun.2
  40.8 19.6 %all_to_all.88.pieces_ref = bf16[4,16,2048]{2,1,0:T(8,128)(2,1)S(1)} all-to-all(bf16[4,16,2048]{2,1,0:T(8,128)(2,1)S(1)} %bitcast.31), channel_id=1, replica_groups=mesh['zh'=4,'x'=4,'c'=2,'y'=8,'zl'=2] {'zh'}, dimensions={0} | all-to-all | bytes 524288 | tf_op jit(solution)/shard_map/cond/branch_1_fun/all_to_all | solution.py:37
  60.4 0.1 branch_1_fun.3
  60.5 22.4 %all_to_all.89 = bf16[16,16,2048]{2,1,0:T(8,128)(2,1)S(1)} all-to-all(bf16[16,16,2048]{2,1,0:T(8,128)(2,1)S(1)} %get-tuple-element.10), channel_id=1, replica_groups=mesh['zh'=4,'x'=4,'c'=2,'y'=8,'zl'=2] {'x','zh'}, dimensions={0} | all-to-all | bytes 2097152 | tf_op jit(solution)/shard_map/cond/branch_1_fun/all_to_all | solution.py:37
  82.9 0.0 copy-done.1
  82.9 0.7 shard_map.78
  83.6 0.3 copy-done.3
  83.9 18.9 %all_to_all.90.pieces_ref = bf16[16,16,512]{2,1,0:T(8,128)(2,1)S(1)} all-to-all(bf16[16,16,512]{2,1,0:T(8,128)(2,1)S(1)} %bitcast.32), channel_id=1, replica_groups=mesh['zh'=4,'x'=4,'c'=2,'y'=8,'zl'=2] {'y','zl'}, dimensions={0} | all-to-all | bytes 524288 | tf_op jit(solution)/shard_map/all_to_all | solution.py:37
  102.8 12.3 %all_to_all.91 = bf16[16,16,512]{2,1,0:T(8,128)(2,1)S(1)} all-to-all(bf16[16,16,512]{2,1,0:T(8,128)(2,1)S(1)} %shard_map.79), channel_id=1, replica_groups=mesh['zh'=4,'x'=4,'c'=2,'y'=8,'zl'=2] {'y','zl'}, dimensions={0} | all-to-all | bytes 524288 | tf_op jit(solution)/shard_map/all_to_all | solution.py:37
  115.1 0.5 shard_map.80
  115.6 16.7 %all_to_all.92.pieces_ref = bf16[16,16,1024]{2,1,0:T(8,128)(2,1)S(1)} all-to-all(bf16[16,16,1024]{2,1,0:T(8,128)(2,1)S(1)} %bitcast.27), channel_id=1, replica_groups=mesh['zh'=4,'x'=4,'c'=2,'y'=8,'zl'=2] {'x','zh'}, dimensions={0} | all-to-all | bytes 1048576 | tf_op jit(solution)/shard_map/all_to_all | solution.py:37
  132.3 0.9 shard_map.81
  133.2 3.7 %all-to-all-start.10 = ((bf16[16,16,1024]{2,1,0:T(8,128)(2,1)}), bf16[16,16,1024]{2,1,0:T(8,128)(2,1)S(1)}, u32[]{:S(2)}, u32[]{:S(2)}) async-start(bf16[16,16,1024]{2,1,0:T(8,128)(2,1)} %shard_map.81), calls=%async_computation.10 | async-start | bytes 1048576 | tf_op jit(solution)/shard_map/all_to_all | solution.py:37
  136.9 0.4 convolution_convert_fusion
  137.3 7.1 %collective-permute-start.5 = (bf16[1024,256]{1,0:T(8,128)(2,1)S(1)}, bf16[1024,256]{1,0:T(8,128)(2,1)S(1)}, u32[]{:S(2)}, u32[]{:S(2)}) collective-permute-start(bf16[1024,256]{1,0:T(8,128)(2,1)S(1)} %convolution_convert_fusion), channel_id=1, source_target_pairs={{0,16},{16,0},{1,17},{17,1},{2,18},{18,2},{3,19},{19,3},{4,20},{20... | collective-permute-start | bytes 1572872 | tf_op jit(solution)/shard_map/ppermute | solution.py:145
  144.4 1.5 collective-permute-done.5
  145.9 2.3 %collective-permute-start.6 = (bf16[256,256]{1,0:T(8,128)(2,1)S(1)}, bf16[256,256]{1,0:T(8,128)(2,1)S(1)}, u32[]{:S(2)}, u32[]{:S(2)}) collective-permute-start(bf16[256,256]{1,0:T(8,128)(2,1)S(1)} %dynamic-slice_bitcast_fusion.far_ref), channel_id=1, source_target_pairs={{0,16},{16,0},{1,17},{17,1},{2,18},{18,2},{3,19},{19,3},{4,20},{20... | collective-permute-start | bytes 393224 | tf_op jit(solution)/shard_map/ppermute | solution.py:145
  148.2 1.2 add_convert_fusion.1
  149.3 0.0 collective-permute-done.6
  149.3 0.6 all-to-all-done.10
  149.9 8.3 %collective-permute-start.7 = (bf16[256,1024]{1,0:T(8,128)(2,1)S(1)}, bf16[256,1024]{1,0:T(8,128)(2,1)S(1)}, u32[]{:S(2)}, u32[]{:S(2)}) collective-permute-start(bf16[256,1024]{1,0:T(8,128)(2,1)S(1)} %bitcast.41), channel_id=1, source_target_pairs={{0,16},{16,0},{1,17},{17,1},{2,18},{18,2},{3,19},{19,3},{4,20},{20... | collective-permute-start | bytes 1572872 | tf_op jit(solution)/shard_map/ppermute | solution.py:145
  158.3 0.3 fusion.7
  158.6 1.2 collective-permute-done.7
  159.8 0.3 fusion.19
  160.1 0.9 add_convert_fusion
  (7 shorter events, 0.1 us)
Async XLA Ops:
  0.6 16.6 %copy-start = (bf16[1024,256]{1,0:T(8,128)(2,1)S(1)}, bf16[1024,256]{1,0:T(8,128)(2,1)}, u32[]{:S(2)}) copy-start(bf16[1024,256]{1,0:T(8,128)(2,1)} %out_ref.3) | copy-start | bytes 1572868
  2.1 19.4 %copy-start.2 = (f32[32,256]{1,0:T(8,128)S(1)}, f32[32,256]{1,0:T(8,128)}, u32[]{:S(2)}) copy-start(f32[32,256]{1,0:T(8,128)} %curvature_ref.1) | copy-start | bytes 98308
  2.1 22.5 %all-to-all-start.6 = ((bf16[32,16,256]{2,1,0:T(8,128)(2,1)}), bf16[32,16,256]{2,1,0:T(8,128)(2,1)S(1)}, u32[]{:S(2)}, u32[]{:S(2)}) async-start(bf16[32,16,256]{2,1,0:T(8,128)(2,1)} %bitcast.7), calls=%async_computation.6 | async-start | bytes 524288 | tf_op jit(solution)/shard_map/all_to_all | solution.py:37
  12.8 13.5 %collective-permute-start = (bf16[256,1024]{1,0:T(8,128)(2,1)}, bf16[256,1024]{1,0:T(8,128)(2,1)S(1)}, u32[]{:S(2)}, u32[]{:S(2)}) collective-permute-start(bf16[256,1024]{1,0:T(8,128)(2,1)} %param.9), channel_id=1, source_target_pairs={{0,16},{16,0},{1,17},{17,1},{2,18},{18,2},{3,19},{19,3},{4,20},{20... | collective-permute-start | bytes 1572872 | tf_op jit(solution)/shard_map/ppermute | solution.py:145
  15.0 11.4 %collective-permute-start.1 = (bf16[256,1024]{1,0:T(8,128)(2,1)}, bf16[256,1024]{1,0:T(8,128)(2,1)S(1)}, u32[]{:S(2)}, u32[]{:S(2)}) collective-permute-start(bf16[256,1024]{1,0:T(8,128)(2,1)} %param.10), channel_id=1, source_target_pairs={{0,16},{16,0},{1,17},{17,1},{2,18},{18,2},{3,19},{19,3},{4,20},{20... | collective-permute-start | bytes 1572872 | tf_op jit(solution)/shard_map/ppermute | solution.py:145
  17.2 9.7 %collective-permute-start.2 = (bf16[1024,256]{1,0:T(8,128)(2,1)S(1)}, bf16[1024,256]{1,0:T(8,128)(2,1)S(1)}, u32[]{:S(2)}, u32[]{:S(2)}) collective-permute-start(bf16[1024,256]{1,0:T(8,128)(2,1)S(1)} %copy-done), channel_id=1, source_target_pairs={{0,16},{16,0},{1,17},{17,1},{2,18},{18,2},{3,19},{19,3},{4,20},{20... | collective-permute-start | bytes 1572872 | tf_op jit(solution)/shard_map/ppermute | solution.py:145
  19.4 7.5 %collective-permute-start.3 = (bf16[1024,256]{1,0:T(8,128)(2,1)}, bf16[1024,256]{1,0:T(8,128)(2,1)S(1)}, u32[]{:S(2)}, u32[]{:S(2)}) collective-permute-start(bf16[1024,256]{1,0:T(8,128)(2,1)} %turn_ref.1), channel_id=1, source_target_pairs={{0,16},{16,0},{1,17},{17,1},{2,18},{18,2},{3,19},{19,3},{4,20},{20... | collective-permute-start | bytes 1572872 | tf_op jit(solution)/shard_map/ppermute | solution.py:145
  21.6 5.3 %collective-permute-start.4 = (f32[32,256]{1,0:T(8,128)S(1)}, f32[32,256]{1,0:T(8,128)S(1)}, u32[]{:S(2)}, u32[]{:S(2)}) collective-permute-start(f32[32,256]{1,0:T(8,128)S(1)} %copy-done.2), channel_id=1, source_target_pairs={{0,16},{16,0},{1,17},{17,1},{2,18},{18,2},{3,19},{19,3},{4,20},{20... | collective-permute-start | bytes 98312 | tf_op jit(solution)/shard_map/ppermute | solution.py:145
  24.6 1.4 copy-start.5
  26.9 56.0 %copy-start.1 = (bf16[1024,256]{1,0:T(8,128)(2,1)S(1)}, bf16[1024,256]{1,0:T(8,128)(2,1)}, u32[]{:S(2)}) copy-start(bf16[1024,256]{1,0:T(8,128)(2,1)} %turn_ref.1) | copy-start | bytes 1572868
  82.9 1.0 copy-start.3
  132.3 4.6 %copy-start.4 = (bf16[256,2048]{1,0:T(8,128)(2,1)S(1)}, bf16[256,2048]{1,0:T(8,128)(2,1)}, u32[]{:S(2)}) copy-start(bf16[256,2048]{1,0:T(8,128)(2,1)} %copy-done.3) | copy-start | bytes 3145732
  133.2 16.7 %all-to-all-start.10 = ((bf16[16,16,1024]{2,1,0:T(8,128)(2,1)}), bf16[16,16,1024]{2,1,0:T(8,128)(2,1)S(1)}, u32[]{:S(2)}, u32[]{:S(2)}) async-start(bf16[16,16,1024]{2,1,0:T(8,128)(2,1)} %shard_map.81), calls=%async_computation.10 | async-start | bytes 1048576 | tf_op jit(solution)/shard_map/all_to_all | solution.py:37
  137.3 8.6 %collective-permute-start.5 = (bf16[1024,256]{1,0:T(8,128)(2,1)S(1)}, bf16[1024,256]{1,0:T(8,128)(2,1)S(1)}, u32[]{:S(2)}, u32[]{:S(2)}) collective-permute-start(bf16[1024,256]{1,0:T(8,128)(2,1)S(1)} %convolution_convert_fusion), channel_id=1, source_target_pairs={{0,16},{16,0},{1,17},{17,1},{2,18},{18,2},{3,19},{19,3},{4,20},{20... | collective-permute-start | bytes 1572872 | tf_op jit(solution)/shard_map/ppermute | solution.py:145
  145.9 3.4 %collective-permute-start.6 = (bf16[256,256]{1,0:T(8,128)(2,1)S(1)}, bf16[256,256]{1,0:T(8,128)(2,1)S(1)}, u32[]{:S(2)}, u32[]{:S(2)}) collective-permute-start(bf16[256,256]{1,0:T(8,128)(2,1)S(1)} %dynamic-slice_bitcast_fusion.far_ref), channel_id=1, source_target_pairs={{0,16},{16,0},{1,17},{17,1},{2,18},{18,2},{3,19},{19,3},{4,20},{20... | collective-permute-start | bytes 393224 | tf_op jit(solution)/shard_map/ppermute | solution.py:145
  149.9 9.8 %collective-permute-start.7 = (bf16[256,1024]{1,0:T(8,128)(2,1)S(1)}, bf16[256,1024]{1,0:T(8,128)(2,1)S(1)}, u32[]{:S(2)}, u32[]{:S(2)}) collective-permute-start(bf16[256,1024]{1,0:T(8,128)(2,1)S(1)} %bitcast.41), channel_id=1, source_target_pairs={{0,16},{16,0},{1,17},{17,1},{2,18},{18,2},{3,19},{19,3},{4,20},{20... | collective-permute-start | bytes 1572872 | tf_op jit(solution)/shard_map/ppermute | solution.py:145

commit v9 on v8

--- a/solution.py
+++ b/solution.py
@@ -173,7 +173,7 @@
         (joined, out_far, turn_far, curvature_far)
     )
     both, derivative = lax.cond(
-        core != lax.axis_index("zl"),
+        core == 1,
         lambda j: staged_then_direct(j, share),
         lambda j: direct_then_staged(j, share),
         joined,

time: 162 us -> 163 us (level)
  starting transfers between devices: 42.9 us -> 46 us
  blocking collectives: 104 us -> 102 us
    ppermute x8, starting transfers between devices: 28.5 us -> 31.7 us  [swap_cores(): return lax.ppermute(block, 'c', SWAP)]
    all_to_all x6, blocking collectives: 104 us -> 102 us  [exchange(): return lax.all_to_all(pieces, axes, split_axis=0, concat_axis=0, tiled=True)]
  transfers between devices with their start and end apart: 10 -> 10, of which waited for: 4 -> 3; matrix products, arithmetic and copies ran while one was open for 2% -> 2% of each run, Pallas kernels for 0% -> 0%
where the time goes in v9:
time: 163 us; the launch traced here: 162 us
  blocking collectives  102 us (63%)
  starting transfers between devices  46 us (28%)
  matrix products  3.85 us (2%)
  waiting for transfers between devices  3.64 us (2%)
  Pallas kernels  2.82 us (2%)
  local copies, waits for them, and re-layouts  1.81 us (1%)
    all_to_all x6, blocking collectives, exchange(): return lax.all_to_all(pieces, axes, split_axis=0, concat_axis=0, tiled=True)  102 us
    ppermute x8, starting transfers between devices, swap_cores(): return lax.ppermute(block, 'c', SWAP)  31.7 us
    all_to_all x2, starting transfers between devices, exchange(): return lax.all_to_all(pieces, axes, split_axis=0, concat_axis=0, tiled=True)  14.3 us
    dot_general x6, matrix products, dot(): lax.dot_general(left_side, right_side, (((left_dim,), (right_dim,)), ((),...  3.85 us
  transfers between devices with their start and end apart: 10, of which 3 were waited for; matrix products, arithmetic and copies ran while one was open for 2% of the time, Pallas kernels for 0%

profile of v9, /device:TPU:1, one launch (start us, length us, event | category | flops | bytes accessed | tf_op | source)
XLA Modules:
  0.0 161.8 jit_solution(8618128065901463617)
XLA Ops:
  0.6 0.0 copy-start
  0.6 1.5 broadcast_in_dim.16
  2.1 10.7 %all-to-all-start.6 = ((bf16[32,16,256]{2,1,0:T(8,128)(2,1)}), bf16[32,16,256]{2,1,0:T(8,128)(2,1)S(1)}, u32[]{:S(2)}, u32[]{:S(2)}) async-start(bf16[32,16,256]{2,1,0:T(8,128)(2,1)} %bitcast.7), calls=%async_computation.6 | async-start | bytes 524288 | tf_op jit(solution)/shard_map/all_to_all | solution.py:37
  12.8 2.1 %collective-permute-start = (bf16[256,1024]{1,0:T(8,128)(2,1)}, bf16[256,1024]{1,0:T(8,128)(2,1)S(1)}, u32[]{:S(2)}, u32[]{:S(2)}) collective-permute-start(bf16[256,1024]{1,0:T(8,128)(2,1)} %param.9), channel_id=1, source_target_pairs={{0,16},{16,0},{1,17},{17,1},{2,18},{18,2},{3,19},{19,3},{4,20},{20... | collective-permute-start | bytes 1572872 | tf_op jit(solution)/shard_map/ppermute | solution.py:145
  15.0 2.2 %collective-permute-start.1 = (bf16[256,1024]{1,0:T(8,128)(2,1)}, bf16[256,1024]{1,0:T(8,128)(2,1)S(1)}, u32[]{:S(2)}, u32[]{:S(2)}) collective-permute-start(bf16[256,1024]{1,0:T(8,128)(2,1)} %param.10), channel_id=1, source_target_pairs={{0,16},{16,0},{1,17},{17,1},{2,18},{18,2},{3,19},{19,3},{4,20},{20... | collective-permute-start | bytes 1572872 | tf_op jit(solution)/shard_map/ppermute | solution.py:145
  17.2 0.0 copy-done
  17.2 2.1 %collective-permute-start.2 = (bf16[1024,256]{1,0:T(8,128)(2,1)S(1)}, bf16[1024,256]{1,0:T(8,128)(2,1)S(1)}, u32[]{:S(2)}, u32[]{:S(2)}) collective-permute-start(bf16[1024,256]{1,0:T(8,128)(2,1)S(1)} %copy-done), channel_id=1, source_target_pairs={{0,16},{16,0},{1,17},{17,1},{2,18},{18,2},{3,19},{19,3},{4,20},{20... | collective-permute-start | bytes 1572872 | tf_op jit(solution)/shard_map/ppermute | solution.py:145
  19.4 2.2 %collective-permute-start.3 = (bf16[1024,256]{1,0:T(8,128)(2,1)}, bf16[1024,256]{1,0:T(8,128)(2,1)S(1)}, u32[]{:S(2)}, u32[]{:S(2)}) collective-permute-start(bf16[1024,256]{1,0:T(8,128)(2,1)} %turn_ref.1), channel_id=1, source_target_pairs={{0,16},{16,0},{1,17},{17,1},{2,18},{18,2},{3,19},{19,3},{4,20},{20... | collective-permute-start | bytes 1572872 | tf_op jit(solution)/shard_map/ppermute | solution.py:145
  21.6 0.0 copy-done.2
  21.6 2.1 %collective-permute-start.4 = (f32[32,256]{1,0:T(8,128)S(1)}, f32[32,256]{1,0:T(8,128)S(1)}, u32[]{:S(2)}, u32[]{:S(2)}) collective-permute-start(f32[32,256]{1,0:T(8,128)S(1)} %copy-done.2), channel_id=1, source_target_pairs={{0,16},{16,0},{1,17},{17,1},{2,18},{18,2},{3,19},{19,3},{4,20},{20... | collective-permute-start | bytes 98312 | tf_op jit(solution)/shard_map/ppermute | solution.py:145
  23.7 0.9 all-to-all-done.6
  24.6 1.4 fusion.11.preact_ref
  26.0 0.0 copy-done.5
  26.0 0.3 fusion.9.tangent_ref
  26.4 0.0 collective-permute-done.in_far_ref
  26.4 0.0 collective-permute-done.1.slope_far_ref
  26.4 0.4 shard_map.77
  26.9 0.0 copy-start.1
  26.9 0.0 collective-permute-done.4.curvature_far_ref
  26.9 0.0 collective-permute-done.2.out_far_ref
  26.9 0.0 collective-permute-done.3.turn_far_ref
  26.9 55.7 %conditional.1 = (bf16[256,2048]{1,0:T(8,128)(2,1)S(1)}, f32[16,1024]{1,0:T(8,128)S(1)}) conditional(s32[]{:T(128)} %convert_element_type.15, bf16[256,2048]{1,0:T(8,128)(2,1)S(1)} %shard_map.77, bf16[256,2048]{1,0:T(8,128)(2,1)S(1)} %shard_map.77), branch_computations={%region_0.1_spmd, %region_1.2_spmd} | conditional | flops 655360 | bytes 7405584 | solution.py:175
  26.9 13.7 %all_to_all.87.pieces_ref = bf16[4,64,2048]{2,1,0:T(8,128)(2,1)S(1)} all-to-all(bf16[4,64,2048]{2,1,0:T(8,128)(2,1)S(1)} %bitcast.34), channel_id=1, replica_groups=mesh['zh'=4,'x'=4,'c'=2,'y'=8,'zl'=2] {'x'}, dimensions={0} | all-to-all | bytes 2097152 | tf_op jit(solution)/shard_map/cond/branch_1_fun/all_to_all | solution.py:37
  40.6 0.1 branch_1_fun.2
  40.8 21.0 %all_to_all.88.pieces_ref = bf16[4,16,2048]{2,1,0:T(8,128)(2,1)S(1)} all-to-all(bf16[4,16,2048]{2,1,0:T(8,128)(2,1)S(1)} %bitcast.31), channel_id=1, replica_groups=mesh['zh'=4,'x'=4,'c'=2,'y'=8,'zl'=2] {'zh'}, dimensions={0} | all-to-all | bytes 524288 | tf_op jit(solution)/shard_map/cond/branch_1_fun/all_to_all | solution.py:37
  61.7 0.1 branch_1_fun.3
  61.9 20.7 %all_to_all.89 = bf16[16,16,2048]{2,1,0:T(8,128)(2,1)S(1)} all-to-all(bf16[16,16,2048]{2,1,0:T(8,128)(2,1)S(1)} %get-tuple-element.10), channel_id=1, replica_groups=mesh['zh'=4,'x'=4,'c'=2,'y'=8,'zl'=2] {'x','zh'}, dimensions={0} | all-to-all | bytes 2097152 | tf_op jit(solution)/shard_map/cond/branch_1_fun/all_to_all | solution.py:37
  82.6 0.0 copy-done.1
  82.6 0.7 shard_map.78
  83.3 0.3 copy-done.3
  83.6 18.1 %all_to_all.90.pieces_ref = bf16[16,16,512]{2,1,0:T(8,128)(2,1)S(1)} all-to-all(bf16[16,16,512]{2,1,0:T(8,128)(2,1)S(1)} %bitcast.32), channel_id=1, replica_groups=mesh['zh'=4,'x'=4,'c'=2,'y'=8,'zl'=2] {'y','zl'}, dimensions={0} | all-to-all | bytes 524288 | tf_op jit(solution)/shard_map/all_to_all | solution.py:37
  101.7 12.2 %all_to_all.91 = bf16[16,16,512]{2,1,0:T(8,128)(2,1)S(1)} all-to-all(bf16[16,16,512]{2,1,0:T(8,128)(2,1)S(1)} %shard_map.79), channel_id=1, replica_groups=mesh['zh'=4,'x'=4,'c'=2,'y'=8,'zl'=2] {'y','zl'}, dimensions={0} | all-to-all | bytes 524288 | tf_op jit(solution)/shard_map/all_to_all | solution.py:37
  113.9 0.5 shard_map.80
  114.4 16.2 %all_to_all.92.pieces_ref = bf16[16,16,1024]{2,1,0:T(8,128)(2,1)S(1)} all-to-all(bf16[16,16,1024]{2,1,0:T(8,128)(2,1)S(1)} %bitcast.27), channel_id=1, replica_groups=mesh['zh'=4,'x'=4,'c'=2,'y'=8,'zl'=2] {'x','zh'}, dimensions={0} | all-to-all | bytes 1048576 | tf_op jit(solution)/shard_map/all_to_all | solution.py:37
  130.6 0.9 shard_map.81
  131.5 3.6 %all-to-all-start.10 = ((bf16[16,16,1024]{2,1,0:T(8,128)(2,1)}), bf16[16,16,1024]{2,1,0:T(8,128)(2,1)S(1)}, u32[]{:S(2)}, u32[]{:S(2)}) async-start(bf16[16,16,1024]{2,1,0:T(8,128)(2,1)} %shard_map.81), calls=%async_computation.10 | async-start | bytes 1048576 | tf_op jit(solution)/shard_map/all_to_all | solution.py:37
  135.1 0.4 convolution_convert_fusion
  135.4 8.8 %collective-permute-start.5 = (bf16[1024,256]{1,0:T(8,128)(2,1)S(1)}, bf16[1024,256]{1,0:T(8,128)(2,1)S(1)}, u32[]{:S(2)}, u32[]{:S(2)}) collective-permute-start(bf16[1024,256]{1,0:T(8,128)(2,1)S(1)} %convolution_convert_fusion), channel_id=1, source_target_pairs={{0,16},{16,0},{1,17},{17,1},{2,18},{18,2},{3,19},{19,3},{4,20},{20... | collective-permute-start | bytes 1572872 | tf_op jit(solution)/shard_map/ppermute | solution.py:145
  144.2 1.5 collective-permute-done.5
  145.8 2.3 %collective-permute-start.6 = (bf16[256,256]{1,0:T(8,128)(2,1)S(1)}, bf16[256,256]{1,0:T(8,128)(2,1)S(1)}, u32[]{:S(2)}, u32[]{:S(2)}) collective-permute-start(bf16[256,256]{1,0:T(8,128)(2,1)S(1)} %dynamic-slice_bitcast_fusion.far_ref), channel_id=1, source_target_pairs={{0,16},{16,0},{1,17},{17,1},{2,18},{18,2},{3,19},{19,3},{4,20},{20... | collective-permute-start | bytes 393224 | tf_op jit(solution)/shard_map/ppermute | solution.py:145
  148.0 1.2 add_convert_fusion.1
  149.2 0.0 collective-permute-done.6
  149.2 0.0 all-to-all-done.10
  149.2 9.9 %collective-permute-start.7 = (bf16[256,1024]{1,0:T(8,128)(2,1)S(1)}, bf16[256,1024]{1,0:T(8,128)(2,1)S(1)}, u32[]{:S(2)}, u32[]{:S(2)}) collective-permute-start(bf16[256,1024]{1,0:T(8,128)(2,1)S(1)} %bitcast.41), channel_id=1, source_target_pairs={{0,16},{16,0},{1,17},{17,1},{2,18},{18,2},{3,19},{19,3},{4,20},{20... | collective-permute-start | bytes 1572872 | tf_op jit(solution)/shard_map/ppermute | solution.py:145
  159.1 0.3 fusion.7
  159.4 1.2 collective-permute-done.7
  160.6 0.3 fusion.19
  160.9 0.9 add_convert_fusion
  (7 shorter events, 0.1 us)
Async XLA Ops:
  0.6 16.6 %copy-start = (bf16[1024,256]{1,0:T(8,128)(2,1)S(1)}, bf16[1024,256]{1,0:T(8,128)(2,1)}, u32[]{:S(2)}) copy-start(bf16[1024,256]{1,0:T(8,128)(2,1)} %out_ref.3) | copy-start | bytes 1572868
  2.1 19.4 %copy-start.2 = (f32[32,256]{1,0:T(8,128)S(1)}, f32[32,256]{1,0:T(8,128)}, u32[]{:S(2)}) copy-start(f32[32,256]{1,0:T(8,128)} %curvature_ref.1) | copy-start | bytes 98308
  2.1 22.5 %all-to-all-start.6 = ((bf16[32,16,256]{2,1,0:T(8,128)(2,1)}), bf16[32,16,256]{2,1,0:T(8,128)(2,1)S(1)}, u32[]{:S(2)}, u32[]{:S(2)}) async-start(bf16[32,16,256]{2,1,0:T(8,128)(2,1)} %bitcast.7), calls=%async_computation.6 | async-start | bytes 524288 | tf_op jit(solution)/shard_map/all_to_all | solution.py:37
  12.8 13.5 %collective-permute-start = (bf16[256,1024]{1,0:T(8,128)(2,1)}, bf16[256,1024]{1,0:T(8,128)(2,1)S(1)}, u32[]{:S(2)}, u32[]{:S(2)}) collective-permute-start(bf16[256,1024]{1,0:T(8,128)(2,1)} %param.9), channel_id=1, source_target_pairs={{0,16},{16,0},{1,17},{17,1},{2,18},{18,2},{3,19},{19,3},{4,20},{20... | collective-permute-start | bytes 1572872 | tf_op jit(solution)/shard_map/ppermute | solution.py:145
  15.0 11.4 %collective-permute-start.1 = (bf16[256,1024]{1,0:T(8,128)(2,1)}, bf16[256,1024]{1,0:T(8,128)(2,1)S(1)}, u32[]{:S(2)}, u32[]{:S(2)}) collective-permute-start(bf16[256,1024]{1,0:T(8,128)(2,1)} %param.10), channel_id=1, source_target_pairs={{0,16},{16,0},{1,17},{17,1},{2,18},{18,2},{3,19},{19,3},{4,20},{20... | collective-permute-start | bytes 1572872 | tf_op jit(solution)/shard_map/ppermute | solution.py:145
  17.2 9.7 %collective-permute-start.2 = (bf16[1024,256]{1,0:T(8,128)(2,1)S(1)}, bf16[1024,256]{1,0:T(8,128)(2,1)S(1)}, u32[]{:S(2)}, u32[]{:S(2)}) collective-permute-start(bf16[1024,256]{1,0:T(8,128)(2,1)S(1)} %copy-done), channel_id=1, source_target_pairs={{0,16},{16,0},{1,17},{17,1},{2,18},{18,2},{3,19},{19,3},{4,20},{20... | collective-permute-start | bytes 1572872 | tf_op jit(solution)/shard_map/ppermute | solution.py:145
  19.4 7.5 %collective-permute-start.3 = (bf16[1024,256]{1,0:T(8,128)(2,1)}, bf16[1024,256]{1,0:T(8,128)(2,1)S(1)}, u32[]{:S(2)}, u32[]{:S(2)}) collective-permute-start(bf16[1024,256]{1,0:T(8,128)(2,1)} %turn_ref.1), channel_id=1, source_target_pairs={{0,16},{16,0},{1,17},{17,1},{2,18},{18,2},{3,19},{19,3},{4,20},{20... | collective-permute-start | bytes 1572872 | tf_op jit(solution)/shard_map/ppermute | solution.py:145
  21.6 5.3 %collective-permute-start.4 = (f32[32,256]{1,0:T(8,128)S(1)}, f32[32,256]{1,0:T(8,128)S(1)}, u32[]{:S(2)}, u32[]{:S(2)}) collective-permute-start(f32[32,256]{1,0:T(8,128)S(1)} %copy-done.2), channel_id=1, source_target_pairs={{0,16},{16,0},{1,17},{17,1},{2,18},{18,2},{3,19},{19,3},{4,20},{20... | collective-permute-start | bytes 98312 | tf_op jit(solution)/shard_map/ppermute | solution.py:145
  24.6 1.4 copy-start.5
  26.9 55.7 %copy-start.1 = (bf16[1024,256]{1,0:T(8,128)(2,1)S(1)}, bf16[1024,256]{1,0:T(8,128)(2,1)}, u32[]{:S(2)}) copy-start(bf16[1024,256]{1,0:T(8,128)(2,1)} %turn_ref.1) | copy-start | bytes 1572868
  82.6 1.0 copy-start.3
  130.6 4.5 %copy-start.4 = (bf16[256,2048]{1,0:T(8,128)(2,1)S(1)}, bf16[256,2048]{1,0:T(8,128)(2,1)}, u32[]{:S(2)}) copy-start(bf16[256,2048]{1,0:T(8,128)(2,1)} %copy-done.3) | copy-start | bytes 3145732
  131.5 17.7 %all-to-all-start.10 = ((bf16[16,16,1024]{2,1,0:T(8,128)(2,1)}), bf16[16,16,1024]{2,1,0:T(8,128)(2,1)S(1)}, u32[]{:S(2)}, u32[]{:S(2)}) async-start(bf16[16,16,1024]{2,1,0:T(8,128)(2,1)} %shard_map.81), calls=%async_computation.10 | async-start | bytes 1048576 | tf_op jit(solution)/shard_map/all_to_all | solution.py:37
  135.4 10.3 %collective-permute-start.5 = (bf16[1024,256]{1,0:T(8,128)(2,1)S(1)}, bf16[1024,256]{1,0:T(8,128)(2,1)S(1)}, u32[]{:S(2)}, u32[]{:S(2)}) collective-permute-start(bf16[1024,256]{1,0:T(8,128)(2,1)S(1)} %convolution_convert_fusion), channel_id=1, source_target_pairs={{0,16},{16,0},{1,17},{17,1},{2,18},{18,2},{3,19},{19,3},{4,20},{20... | collective-permute-start | bytes 1572872 | tf_op jit(solution)/shard_map/ppermute | solution.py:145
  145.8 3.4 %collective-permute-start.6 = (bf16[256,256]{1,0:T(8,128)(2,1)S(1)}, bf16[256,256]{1,0:T(8,128)(2,1)S(1)}, u32[]{:S(2)}, u32[]{:S(2)}) collective-permute-start(bf16[256,256]{1,0:T(8,128)(2,1)S(1)} %dynamic-slice_bitcast_fusion.far_ref), channel_id=1, source_target_pairs={{0,16},{16,0},{1,17},{17,1},{2,18},{18,2},{3,19},{19,3},{4,20},{20... | collective-permute-start | bytes 393224 | tf_op jit(solution)/shard_map/ppermute | solution.py:145
  149.2 11.4 %collective-permute-start.7 = (bf16[256,1024]{1,0:T(8,128)(2,1)S(1)}, bf16[256,1024]{1,0:T(8,128)(2,1)S(1)}, u32[]{:S(2)}, u32[]{:S(2)}) collective-permute-start(bf16[256,1024]{1,0:T(8,128)(2,1)S(1)} %bitcast.41), channel_id=1, source_target_pairs={{0,16},{16,0},{1,17},{17,1},{2,18},{18,2},{3,19},{19,3},{4,20},{20... | collective-permute-start | bytes 1572872 | tf_op jit(solution)/shard_map/ppermute | solution.py:145
